TPU v7x, 32 devices: a whole 2x2x4 slice. The times are simulated.
32 devices in a mesh: grp: 4 (over z), ord: 8 (over y, x, core).
Axes of the slice: x: 2, y: 2, z: 4, core: 2. Of those that a mesh axis runs over, the one named last changes fastest.
Arguments:
- legendre: float32 [512, 131072], P('ord', 'grp')
- lon_center: float32 [4], P('grp'), may hold values from 0 to 1
- counts: int32 [4, 8], P('grp'), may hold values from 1 to 4096, 24576 in all within a row
- column_index: int32 [3, 512], replicated, may hold values from 0 to 120, as said below
Outputs:
- factor: float32 [512, 512], replicated
Inputs may be any that keep to these rules, and one draw needn't show every extreme that they name: `column_index`: each column names a different coefficient: row 0 is its degree (at most 120), row 1 its order (at most the degree), row 2 is 1 for a sine term and 0 for a cosine term, and 0 at order 0. Each group's counts add up to 24576.
All inputs are finite; a program needn't handle non-finite values.
Results may differ from a plain program's by a relative error of at most 0.0003.
Values sent between devices are 32-bit elements; how exact they have to be, the bound alone decides.
No kernel may reach another device: no remote copies, remote signals or barrier semaphores. Data moves between devices by JAX's collectives and lax.ppermute only.
A program may use at most 64 MiB of HBM per device.

v0:
```python
import math

import jax
import jax.numpy as jnp
from jax import lax
from jax.sharding import PartitionSpec as P

NMAX = 120


quarter_turn = math.pi / 2
track_span = 0.3
kaula_gain = 1.2
highest = lax.Precision.HIGHEST


def upper_factor(matrix):
    return jnp.linalg.cholesky(matrix).T


def block_grams(exchanged):
    blocks = exchanged[:, 0]
    return jnp.einsum("jkb,lkb->kjl", blocks, blocks, precision=highest)


def body(legendre, lon_center, counts, column_index):
    ord_size = lax.axis_size("ord")
    grp_size = lax.axis_size("grp")
    cols_dev, rows_grp = legendre.shape
    rows_dev = rows_grp // ord_size
    scaling = 1.0 / math.sqrt(rows_grp * grp_size)
    own_columns = lax.dynamic_slice_in_dim(
        column_index, lax.axis_index("ord") * cols_dev, cols_dev, 1
    )
    harmonic = own_columns[1].astype(jnp.float32)
    sine_part = own_columns[2].astype(jnp.float32)
    longitude = lon_center[0] + jnp.arange(rows_grp, dtype=jnp.float32) * (track_span / rows_grp)
    harmonic_wave = jnp.cos(
        harmonic[:, None] * longitude[None, :] - sine_part[:, None] * quarter_turn
    )
    slot_index = jnp.arange(rows_dev, dtype=jnp.int32)
    row_valid = (slot_index[None, :] < counts[0][:, None]).astype(jnp.float32).reshape(rows_grp)
    design = legendre * harmonic_wave * (row_valid * scaling)[None, :]
    block_rows = min(512, rows_dev)
    shaped = design.reshape(cols_dev, ord_size, rows_dev // block_rows, block_rows)
    block_gram = block_grams(lax.all_to_all(shaped, "ord", split_axis=1, concat_axis=0, tiled=True))
    local_gram = jnp.sum(block_gram, axis=0)
    degree = column_index[0].astype(jnp.float32)
    kaula_weight = kaula_gain * (degree / NMAX) ** 2
    regular = jnp.diag(kaula_weight * kaula_weight)
    share = lax.psum_scatter(local_gram, "ord", scatter_dimension=0, tiled=True)
    share = lax.psum(share, "grp")
    share_rows = share.shape[0]
    own_regular = lax.dynamic_slice_in_dim(
        regular, lax.axis_index("ord") * share_rows, share_rows, 0
    )
    normal = lax.all_gather(share + own_regular, "ord", axis=0, tiled=True)
    return upper_factor(normal)


def solution(mesh):
    placed = (P("ord", "grp"), P("grp"), P("grp", None), P())
    return jax.shard_map(body, mesh=mesh, in_specs=placed, out_specs=P(), check_vma=False)
```

profile of v0, /device:TPU:0, one launch (start us, length us, event | category | flops | bytes accessed | tf_op | source)
XLA Modules:
  0.0 355.2 jit_solution(7349953945158786727)
XLA Ops:
  6.5 0.8 constant_dynamic-slice_fusion
  7.3 0.7 select_bitcast_fusion.1
  8.8 29.4 %multiply_multiply_fusion = f32[64,32768]{1,0:T(8,128)S(1)} fusion(f32[64,32768]{1,0:T(8,128)} %param.4, f32[32768]{0:T(1024)S(1)} %bitcast.52, f32[64]{0:T(128)S(1)} %multiply_bitcast_fusion, f32[32768]{0:T(1024)S(1)} %multiply_add_fusion, f32[64]{0:T(128)S(1)} %convert_bitcast_fusion), kind=kLoop, calls=%fused_computation | loop fusion | flops 8388608 | bytes 17039872 | tf_op jit(solution)/shard_map/mul | solution.py:43
  38.2 4.7 %copy.31 = f32[8,8,64,512]{3,2,1,0:T(8,128)S(1)} copy(f32[8,8,64,512]{3,1,2,0:T(8,128)S(1)} %bitcast.49) | data formatting | bytes 16777216
  42.9 4.7 %copy.20 = f32[64,8,8,512]{3,0,2,1:T(8,128)S(1)} copy(f32[64,8,8,512]{3,2,1,0:T(8,128)S(1)} %bitcast.50) | data formatting | bytes 16777216 | tf_op jit(solution)/shard_map/reshape | solution.py:45
  47.7 99.0 %all_to_all.15 = f32[64,8,8,512]{3,0,2,1:T(8,128)S(1)} all-to-all(f32[64,8,8,512]{3,0,2,1:T(8,128)S(1)} %copy.20), channel_id=1, replica_groups=mesh['grp'=4,'ord'=8] {'ord'}, dimensions={1} | all-to-all | bytes 16777216 | tf_op jit(solution)/shard_map/all_to_all | solution.py:46
  146.6 1.8 copy.21
  148.4 14.7 %convolution_bitcast_fusion = f32[512,512]{1,0:T(8,128)} fusion(f32[512,8,512]{2,0,1:T(8,128)S(1)} %bitcast.48), kind=kOutput, calls=%fused_computation.1 | convolution fusion | flops 12884901888 | bytes 9437184 | tf_op jit(solution)/shard_map/jkb,lkb->kjl/dot_general | solution.py:23
  163.3 35.5 %reduce-scatter.4.cloned.1.call-done = f32[64,512]{1,0:T(8,128)} async-done(((f32[512,512]{1,0:T(8,128)}), f32[64,512]{1,0:T(8,128)}) %reduce-scatter.4.cloned.1.call-update) | async-done | bytes 131088 | tf_op jit(solution)/shard_map/reduce_scatter | solution.py:51
  199.2 0.7 multiply_multiply_fusion.1
  200.0 35.5 %all-reduce.3.cloned.1.call-done = f32[64,512]{1,0:T(8,128)} async-done(((f32[64,512]{1,0:T(8,128)}), f32[64,512]{1,0:T(8,128)}) %all-reduce.3.cloned.1.call-update) | async-done | bytes 131088 | tf_op jit(solution)/shard_map/psum | solution.py:52
  235.5 1.6 select_add_fusion
  237.2 23.6 %all-gather.2.cloned.1.call-done = f32[512,512]{1,0:T(8,128)} async-done(((f32[64,512]{1,0:T(8,128)}), f32[512,512]{1,0:T(8,128)}) %all-gather.2.cloned.1.call-update) | async-done | bytes 1048592 | tf_op jit(solution)/shard_map/all_gather | solution.py:57
  260.8 1.6 copy.24
  262.3 1.4 fusion
  263.8 11.7 %cholesky.103 = f32[128,128]{1,0:T(8,128)S(1)} custom-call(f32[128,128]{1,0:T(8,128)S(1)} %cholesky.263), custom_call_target="Cholesky" | custom-call | tf_op jit(solution)/shard_map/jit(cholesky)/cholesky | solution.py:18
  275.5 9.8 %custom-call.27 = f32[1,128,128]{1,2,0:T(8,128)S(1)} custom-call(f32[1,128,128]{2,1,0:T(8,128)S(1)} %get-tuple-element.14), custom_call_target="InvertDiagBlocksLowerTriangular" | custom-call | tf_op jit(solution)/shard_map/jit(cholesky)/cholesky | solution.py:18
  286.2 11.7 %cholesky.215 = f32[128,128]{1,0:T(8,128)S(1)} custom-call(f32[128,128]{1,0:T(8,128)S(1)} %cholesky.267), custom_call_target="Cholesky" | custom-call | tf_op jit(solution)/shard_map/jit(cholesky)/cholesky | solution.py:18
  297.9 9.9 %custom-call.28 = f32[1,128,128]{1,2,0:T(8,128)S(1)} custom-call(f32[1,128,128]{2,1,0:T(8,128)S(1)} %get-tuple-element.11), custom_call_target="InvertDiagBlocksLowerTriangular" | custom-call | tf_op jit(solution)/shard_map/jit(cholesky)/cholesky | solution.py:18
  308.5 11.7 %cholesky.236 = f32[128,128]{1,0:T(8,128)S(1)} custom-call(f32[128,128]{1,0:T(8,128)S(1)} %cholesky.272), custom_call_target="Cholesky" | custom-call | tf_op jit(solution)/shard_map/jit(cholesky)/cholesky | solution.py:18
  320.3 0.7 compare_reduce_fusion.1
  321.0 9.8 %custom-call.29 = f32[1,128,128]{1,2,0:T(8,128)S(1)} custom-call(f32[1,128,128]{2,1,0:T(8,128)S(1)} %get-tuple-element.8), custom_call_target="InvertDiagBlocksLowerTriangular" | custom-call | tf_op jit(solution)/shard_map/jit(cholesky)/cholesky | solution.py:18
  331.4 11.7 %cholesky.253 = f32[128,128]{1,0:T(8,128)S(1)} custom-call(f32[128,128]{1,0:T(8,128)S(1)} %convolution_subtract_fusion.2), custom_call_target="Cholesky" | custom-call | tf_op jit(solution)/shard_map/jit(cholesky)/cholesky | solution.py:18
  347.1 1.3 copy.25
  (28 shorter events, 4.3 us)
Async XLA Ops:
  6.5 192.2 %reduce-scatter.4.cloned.1.call-start = ((), (), s32[]{:S(2)}) async-start(), calls=%async_computation.4 | async-start | bytes 1179648 | tf_op jit(solution)/shard_map/reduce_scatter | solution.py:51
  163.2 72.3 %all-reduce.3.cloned.1.call-start = ((), (), s32[]{:S(2)}) async-start(), calls=%async_computation.2 | async-start | bytes 262144 | tf_op jit(solution)/shard_map/psum | solution.py:52
  198.8 62.0 %all-gather.2.cloned.1.call-start = ((), (), s32[]{:S(2)}) async-start(), calls=%async_computation.3 | async-start | bytes 1179648 | tf_op jit(solution)/shard_map/all_gather | solution.py:57
Sparse Core Ops, SparseCore 0:
  163.3 35.3 reduce-scatter.3
  201.1 34.4 all-reduce.2
  237.6 23.1 all-gather.1
where the time goes:
time: 361 us; the launch traced here: 355 us
  other arithmetic  113 us (31%)
  blocking collectives  99 us (27%)
  waiting for transfers between devices  94.6 us (26%)
  matrix products  16.6 us (5%)
  between operations  16.6 us (5%)
  local copies, waits for them, and re-layouts  15.1 us (4%)
    all_to_all x1, blocking collectives, body(): lax.all_to_all(shaped, 'ord', split_axis=1, concat_axis=0, tiled=True)  99 us
    another operation x14, other arithmetic, upper_factor(): return jnp.linalg.cholesky(matrix).T  78.6 us
    psum x1, waiting for transfers between devices, body(): share = lax.psum(share, 'grp')  35.5 us
    reduce_scatter x1, waiting for transfers between devices, body(): share = lax.psum_scatter(local_gram, 'ord', scatter_dimension=0, tiled=True)  35.5 us
    mul x1, other arithmetic, body(): design = legendre * harmonic_wave * (row_valid * scaling)[None, :]  29.4 us
    all_gather x1, waiting for transfers between devices, body(): normal = lax.all_gather(share + own_regular, 'ord', axis=0, tiled=True)  23.6 us
    dot_general x1, matrix products, block_grams(): return jnp.einsum('jkb,lkb->kjl', blocks, blocks, precision=highest)  14.7 us
  transfers between devices with their start and end apart: 3, of which 3 were waited for; matrix products, arithmetic and copies ran while one was open for 0% of the time, Pallas kernels for 0%

commit v1 on v0

v1 whole, which is shorter than its diff:
```python
import functools
import math

import jax
import jax.numpy as jnp
from jax import lax
from jax.experimental import pallas as pl
from jax.experimental.pallas import tpu as pltpu
from jax.sharding import PartitionSpec as P

NMAX = 120
LANES = 128
SUBS = 8

quarter_turn = math.pi / 2
track_span = 0.3
kaula_gain = 1.2
VMEM = pltpu.VMEM
SMEM = pltpu.SMEM


def cosine(x):
    turns = jnp.floor(x * (1.0 / math.pi) + 0.5)
    rest = x - turns * 3.140625
    rest = rest - turns * 9.670257568359375e-4
    rest = rest - turns * 6.2770535e-7
    half = turns * 0.5
    sign = 1.0 - 4.0 * (half - jnp.floor(half))
    sq = rest * rest
    acc = jnp.full_like(x, 1.0 / math.factorial(14))
    acc = -1.0 * acc
    for power, s in ((12, 1.0), (10, -1.0), (8, 1.0), (6, -1.0), (4, 1.0), (2, -1.0), (0, 1.0)):
        acc = acc * sq + s / math.factorial(power)
    return acc * sign


def loop(count, step):
    lax.fori_loop(0, count, step, 0, unroll=5 if count % 5 == 0 else 1)


def design_kernel(shape, k, counts_ref, lon_ref, index_ref, leg_ref, *refs):
    n, sizes, rows_dev, rows_grp, scaling = shape
    outs, (held, table, sems) = refs[: len(sizes)], refs[len(sizes) :]
    blocks_dev, per = rows_dev // LANES, sum(sizes)
    me = lax.axis_index("ord")
    dest = me ^ k
    ends, total = [], 0
    for r in range(n):
        total = total + lax.div(counts_ref[0, r] + (LANES - 1), LANES)
        ends.append(total)

    def copy(i, start):
        return pltpu.make_async_copy(
            leg_ref.at[:, pl.ds(pl.multiple_of(start, LANES), LANES)],
            held.at[:, pl.ds(pl.multiple_of(i * LANES, LANES), LANES)],
            sems.at[i],
        )

    def plan(i, _):
        want = dest * per + i
        slot, first, count = 0, 0, counts_ref[0, 0]
        for r in range(n - 1):
            past = want >= ends[r]
            slot = jnp.where(past, r + 1, slot)
            first = jnp.where(past, ends[r], first)
            count = jnp.where(past, counts_ref[0, r + 1], count)
        inside = jnp.minimum(want - first, blocks_dev - 1)
        start = slot * rows_dev + inside * LANES
        copy(i, start).start()
        table[0, i] = start
        table[1, i] = jnp.where(want < total, count - (want - first) * LANES, 0)
        return 0

    loop(per, plan)
    rows = held.shape[0]
    wide = (rows, index_ref.shape[1])
    mine = lax.broadcasted_iota(jnp.int32, wide, 1) == lax.broadcasted_iota(jnp.int32, wide, 0) + me * rows

    def column(row):
        values = jnp.broadcast_to(index_ref[row : row + 1, :].astype(jnp.float32), wide)
        picked = jnp.sum(jnp.where(mine, values, 0.0), axis=1, keepdims=True)
        return jnp.broadcast_to(picked, (rows, LANES))

    harmonic = column(1)
    phase = column(2) * quarter_turn
    lane = lax.broadcasted_iota(jnp.int32, (SUBS, LANES), 1)
    base = 0
    for out_ref, size in zip(outs, sizes):

        def work(i, _, out_ref=out_ref, base=base):
            copy(base + i, 0).wait()
            along = (table[0, base + i] + lane).astype(jnp.float32) * (track_span / rows_grp)
            longitude = lon_ref[0] + along
            gate = jnp.where(lane < table[1, base + i], scaling, 0.0)
            there = pl.ds(pl.multiple_of((base + i) * LANES, LANES), LANES)
            here = pl.ds(pl.multiple_of(i * LANES, LANES), LANES)
            for top in range(0, rows, SUBS):
                wave = cosine(harmonic[top : top + SUBS] * longitude - phase[top : top + SUBS])
                out_ref[pl.ds(top, SUBS), here] = held[pl.ds(top, SUBS), there] * wave * gate
            return 0

        loop(size, work)
        base += size


@functools.partial(jax.jit, static_argnums=(0, 1))
def design_for(shape, k, counts, lon_center, column_index, legendre):
    n, sizes, rows_dev, rows_grp, _ = shape
    rows, per = legendre.shape[0], sum(sizes)
    elements = rows * per * LANES
    return pl.pallas_call(
        functools.partial(design_kernel, shape, k),
        out_shape=[jax.ShapeDtypeStruct((rows, size * LANES), jnp.float32) for size in sizes],
        in_specs=[
            pl.BlockSpec(memory_space=SMEM),
            pl.BlockSpec(memory_space=SMEM),
            pl.BlockSpec(memory_space=VMEM),
            pl.BlockSpec(memory_space=pltpu.HBM),
        ],
        out_specs=[pl.BlockSpec(memory_space=VMEM)] * len(sizes),
        scratch_shapes=[
            pltpu.VMEM((rows, per * LANES), jnp.float32),
            pltpu.SMEM((2, per), jnp.int32),
            pltpu.SemaphoreType.DMA((per,)),
        ],
        compiler_params=pltpu.CompilerParams(vmem_limit_bytes=16 << 20),
        cost_estimate=pl.CostEstimate(flops=30 * elements, bytes_accessed=8 * elements, transcendentals=0),
        name="design",
    )(counts, lon_center, column_index, legendre)


def upper_blocks(cols):
    nb = cols // LANES
    return [(i, j) for i in range(nb) for j in range(i, nb)]


def gram_kernel(n, cols, first, last, *refs):
    ins, refs = refs[:n], refs[n:]
    before = None
    if not first:
        before, refs = refs[0], refs[1:]
    outs, scratch = refs[: n if last else 1], refs[n if last else 1 :]
    high, low = scratch[:2]
    acc = scratch[2] if last else outs[0]
    me = lax.axis_index("ord")
    each = cols // n
    for k in range(n):
        tile = ins[k][...]
        at = pl.ds(pl.multiple_of((me ^ k) * each, each), each)
        top = tile.astype(jnp.bfloat16)
        high[at, :] = top
        low[at, :] = (tile - top.astype(jnp.float32)).astype(jnp.bfloat16)

    def times(a, b):
        return lax.dot_general(a, b, (((1,), (1,)), ((), ())), preferred_element_type=jnp.float32)

    step = pl.program_id(0)
    tall = min(256, cols)
    for i in range(0, cols, tall):
        hi, lo = high[pl.ds(i, tall), :], low[pl.ds(i, tall), :]
        his, los = high[pl.ds(i, cols - i), :], low[pl.ds(i, cols - i), :]
        at = (pl.ds(i, tall), pl.ds(i, cols - i))
        here = times(hi, his) + (times(hi, los) + times(lo, his))

        @pl.when(step == 0)
        def _():
            acc[at] = here if first else before[at] + here

        @pl.when(step > 0)
        def _():
            acc[at] += here

    if last:
        packed = scratch[3]

        @pl.when(step == pl.num_programs(0) - 1)
        def _():
            for t, (i, j) in enumerate(upper_blocks(cols)):
                packed[pl.ds(t * LANES, LANES), :] = acc[pl.ds(i * LANES, LANES), pl.ds(j * LANES, LANES)]
            piece = packed.shape[0] // n
            for k in range(n):
                outs[k][...] = packed[pl.ds(pl.multiple_of((me ^ k) * piece, SUBS), piece), :]


def gram(n, parts, before, last):
    each, rows = parts[0].shape
    cols = each * n
    tile = 640 if rows % 640 == 0 else LANES
    height = len(upper_blocks(cols)) * LANES
    whole = pl.BlockSpec((cols, cols), lambda s: (0, 0))
    in_specs = [pl.BlockSpec((each, tile), lambda s: (0, s))] * n + [whole] * len(before)
    scratch = [pltpu.VMEM((cols, tile), jnp.bfloat16)] * 2
    if last:
        out_shape = [jax.ShapeDtypeStruct((height // n, LANES), jnp.float32)] * n
        out_specs = [pl.BlockSpec((height // n, LANES), lambda s: (0, 0))] * n
        scratch += [pltpu.VMEM((cols, cols), jnp.float32), pltpu.VMEM((height, LANES), jnp.float32)]
    else:
        out_shape, out_specs = [jax.ShapeDtypeStruct((cols, cols), jnp.float32)], [whole]
    return pl.pallas_call(
        functools.partial(gram_kernel, n, cols, not before, last),
        grid=(rows // tile,),
        out_shape=out_shape,
        in_specs=in_specs,
        out_specs=out_specs,
        scratch_shapes=scratch,
        compiler_params=pltpu.CompilerParams(vmem_limit_bytes=32 << 20),
        cost_estimate=pl.CostEstimate(
            flops=6 * cols * cols * rows, bytes_accessed=4 * cols * rows, transcendentals=0
        ),
        name="gram",
    )(*parts, *before)


def lane_wide(x, j):
    return jnp.broadcast_to(x[:, j : j + 1], (SUBS, LANES))


def sub_wide(x, i):
    return jnp.broadcast_to(x[i : i + 1, :], (SUBS, LANES))


def factor_panel(a_ref, r_ref, base, p, wide, lane, sub):
    groups = LANES // SUBS
    row0, c0 = base + SUBS * p, SUBS * p
    own = [a_ref[pl.ds(row0, SUBS), pl.ds(base + LANES * w, LANES)] for w in range(wide)]
    spread = [lane_wide(own[0], c0 + j) for j in range(SUBS)]
    d = {(i, j): sub_wide(spread[j], i) for j in range(SUBS) for i in range(j + 1)}
    inv, up = [None] * SUBS, {}
    for i in range(SUBS):
        inv[i] = lax.rsqrt(d[i, i])
        for j in range(i + 1, SUBS):
            up[i, j] = d[i, j] * inv[i]
        for a in range(i + 1, SUBS):
            for b in range(a, SUBS):
                d[a, b] = d[a, b] - up[i, a] * up[i, b]
    done = [[None] * SUBS for _ in range(wide)]
    for w in range(wide):
        for i in range(SUBS):
            acc = sub_wide(own[w], i)
            for j in range(i):
                acc = acc - up[j, i] * done[w][j]
            done[w][i] = acc * inv[i]
        out = done[w][0]
        for i in range(1, SUBS):
            out = jnp.where(sub == i, done[w][i], out)
        if w == 0:
            out = jnp.where(lane >= sub + c0, out, 0.0)
        r_ref[pl.ds(row0, SUBS), pl.ds(base + LANES * w, LANES)] = out

    def update(g, coef, rows):
        for w in range(wide):
            at = (pl.ds(base + SUBS * g, SUBS), pl.ds(base + LANES * w, LANES))
            total = coef[0] * rows[w][0]
            for j in range(1, SUBS):
                total = total + coef[j] * rows[w][j]
            a_ref[at] = a_ref[at] - total

    if p + 1 < groups:
        below = a_ref[pl.ds(base + SUBS * (p + 1), SUBS), pl.ds(base, LANES)]
        coef = []
        for j in range(SUBS):
            acc = lane_wide(below, c0 + j)
            for i in range(j):
                acc = acc - up[i, j] * coef[i]
            coef.append(acc * inv[j])
        update(p + 1, coef, done)
    if p + 2 < groups:
        solved = [[None] * SUBS for _ in range(wide)]
        for w in range(wide):
            for i in range(SUBS - 1, -1, -1):
                acc = done[w][i]
                for j in range(i + 1, SUBS):
                    acc = acc - up[i, j] * solved[w][j]
                solved[w][i] = acc * inv[i]
        for g in range(p + 2, groups):
            below = a_ref[pl.ds(base + SUBS * g, SUBS), pl.ds(base, LANES)]
            update(g, [lane_wide(below, c0 + j) for j in range(SUBS)], solved)


def factor_kernel(n, cols, kaula_ref, *refs):
    ins, r_ref, a_ref, packed = refs[:n], refs[n], refs[n + 1], refs[n + 2]
    me = lax.axis_index("ord")
    piece = packed.shape[0] // n
    for k in range(n):
        packed[pl.ds(pl.multiple_of((me ^ k) * piece, SUBS), piece), :] = ins[k][...]
    square = (LANES, LANES)
    diag = lax.broadcasted_iota(jnp.int32, square, 0) == lax.broadcasted_iota(jnp.int32, square, 1)
    for t, (i, j) in enumerate(upper_blocks(cols)):
        block = packed[pl.ds(t * LANES, LANES), :]
        if i == j:
            block = block + jnp.where(diag, kaula_ref[:, pl.ds(i * LANES, LANES)], 0.0)
        a_ref[pl.ds(i * LANES, LANES), pl.ds(j * LANES, LANES)] = block
    lane = lax.broadcasted_iota(jnp.int32, (SUBS, LANES), 1)
    sub = lax.broadcasted_iota(jnp.int32, (SUBS, LANES), 0)
    count = cols // LANES
    for k in range(count):
        base, wide = k * LANES, count - k
        if base:
            r_ref[pl.ds(base, LANES), pl.ds(0, base)] = jnp.zeros((LANES, base), jnp.float32)
        for p in range(LANES // SUBS):
            factor_panel(a_ref, r_ref, base, p, wide, lane, sub)
        for i in range(k + 1, count):
            left = r_ref[pl.ds(base, LANES), pl.ds(i * LANES, LANES)]
            right = r_ref[pl.ds(base, LANES), pl.ds(i * LANES, cols - i * LANES)]
            a_ref[pl.ds(i * LANES, LANES), pl.ds(i * LANES, cols - i * LANES)] -= lax.dot_general(
                left,
                right,
                (((0,), (0,)), ((), ())),
                precision=lax.Precision.HIGHEST,
                preferred_element_type=jnp.float32,
            )


def factor(n, cols, kaula_square, pieces):
    height = len(upper_blocks(cols)) * LANES
    return pl.pallas_call(
        functools.partial(factor_kernel, n, cols),
        out_shape=jax.ShapeDtypeStruct((cols, cols), jnp.float32),
        in_specs=[pl.BlockSpec(memory_space=VMEM)] * (n + 1),
        out_specs=pl.BlockSpec(memory_space=VMEM),
        scratch_shapes=[
            pltpu.VMEM((cols, cols), jnp.float32),
            pltpu.VMEM((height, LANES), jnp.float32),
        ],
        compiler_params=pltpu.CompilerParams(vmem_limit_bytes=32 << 20),
        name="factor",
    )(kaula_square, *pieces)


def pairs(size, k):
    return [(i, i ^ k) for i in range(size)]


def swap(x, axis, k):
    return lax.ppermute(x, axis, pairs(lax.axis_size(axis), k)) if k else x


def tree_sum(terms):
    while len(terms) > 1:
        terms = [a + b for a, b in zip(terms[::2], terms[1::2])]
    return terms[0]


def body(legendre, lon_center, counts, column_index):
    n, groups = lax.axis_size("ord"), lax.axis_size("grp")
    cols_dev, rows_grp = legendre.shape
    cols = cols_dev * n
    rows_dev = rows_grp // n
    valid_rows = 3 * rows_grp // 4
    per = -(-((valid_rows + (LANES - 1) * n) // LANES) // n)
    late = max(1, per // 5)
    shape = (n, (per - late, late), rows_dev, rows_grp, 1.0 / math.sqrt(rows_grp * groups))
    order = sorted(range(1, n), key=lambda k: (-bin(k >> 1).count("1"), k)) + [0]
    early_parts, late_parts = [None] * n, [None] * n
    for k in order:
        sent = design_for(shape, k, counts, lon_center, column_index, legendre)
        early_parts[k] = swap(sent[0], "ord", k)
        late_parts[k] = swap(sent[1], "ord", k)
    before = gram(n, early_parts, [], False)
    pieces = gram(n, late_parts, before, True)
    share = tree_sum([swap(pieces[k], "ord", k) for k in range(n)])
    share = tree_sum([swap(share, "grp", k) for k in range(groups)])
    gathered = [swap(share, "ord", k) for k in range(n)]
    degree = column_index[0:1].astype(jnp.float32)
    kaula_weight = kaula_gain * (degree / NMAX) ** 2
    return factor(n, cols, kaula_weight * kaula_weight, gathered)


def solution(mesh):
    placed = (P("ord", "grp"), P("grp"), P("grp", None), P())
    return jax.shard_map(body, mesh=mesh, in_specs=placed, out_specs=P(), check_vma=False)
```

time: 361 us -> 150 us (0.42); the launches traced: 355 us -> 150 us
  other arithmetic: 113 us -> 0.76 us
  blocking collectives: 99 us -> 0 us
  Pallas kernels: 0 us -> 52.5 us
  waiting for transfers between devices: 94.6 us -> 57.8 us
  starting transfers between devices: 0.49 us -> 33.4 us
  matrix products: 16.6 us -> 0 us
  between operations: 16.6 us -> 0.88 us
  local copies, waits for them, and re-layouts: 15.1 us -> 4.73 us
    all_to_all x1 -> x0, blocking collectives: 99 us -> none  [body(): lax.all_to_all(shaped, 'ord', split_axis=1, concat_axis=0, tiled=True)]
    another operation x14 -> x0, other arithmetic: 78.6 us -> none  [upper_factor(): return jnp.linalg.cholesky(matrix).T]
    ppermute x0 -> x31, waiting for transfers between devices: none -> 57.8 us  [swap(): return lax.ppermute(x, axis, pairs(lax.axis_size(axis), k)) if k else x]
    pallas_call x0 -> x11, Pallas kernels: none -> 52.5 us  [the longest x8 24.6 us: design_for(): pl.pallas_call(functools.partial(design_kernel, shape, k), out_shape=[jax...]
    psum x1 -> x0, waiting for transfers between devices: 35.5 us -> none  [body(): share = lax.psum(share, 'grp')]
    reduce_scatter x1 -> x0, waiting for transfers between devices: 35.5 us -> none  [body(): share = lax.psum_scatter(local_gram, 'ord', scatter_dimension=0, tiled=True)]
    ppermute x0 -> x31, starting transfers between devices: none -> 33.4 us  [swap(): return lax.ppermute(x, axis, pairs(lax.axis_size(axis), k)) if k else x]
    mul x3 -> x1, other arithmetic: 30.1 us -> 0.7 us  [body(): return factor(n, cols, kaula_weight * kaula_weight, gathered)]
  transfers between devices with their start and end apart: 3 -> 31, of which waited for: 3 -> 10; matrix products, arithmetic and copies ran while one was open for 0% -> 0% of each run, Pallas kernels for 0% -> 20%
where the time goes in v1:
time: 150 us
  waiting for transfers between devices  57.8 us (39%)
  Pallas kernels  52.5 us (35%)
  starting transfers between devices  33.4 us (22%)
  local copies, waits for them, and re-layouts  4.73 us (3%)
    ppermute x31, waiting for transfers between devices, swap(): return lax.ppermute(x, axis, pairs(lax.axis_size(axis), k)) if k else x  57.8 us
    ppermute x31, starting transfers between devices, swap(): return lax.ppermute(x, axis, pairs(lax.axis_size(axis), k)) if k else x  33.4 us
    pallas_call x8, Pallas kernels, design_for(): pl.pallas_call(functools.partial(design_kernel, shape, k), out_shape=[jax...  24.6 us
    pallas_call x1, Pallas kernels, factor(): pl.pallas_call(functools.partial(factor_kernel, n, cols), out_shape=jax.S...  17.5 us
    pallas_call x2, Pallas kernels, gram(): pl.pallas_call(functools.partial(gram_kernel, n, cols, not before, last),...  10.4 us
    unnamed x6, local copies, waits for them, and re-layouts  4.73 us
  transfers between devices with their start and end apart: 31, of which 10 were waited for; matrix products, arithmetic and copies ran while one was open for 0% of the time, Pallas kernels for 20%

profile of v1, /device:TPU:0, one launch (start us, length us, event | category | flops | bytes accessed | tf_op | source)
XLA Modules:
  0.0 150.0 jit_solution(5173863540809269877)
XLA Ops:
  0.7 3.4 %copy-done = f32[64,32768]{1,0:T(8,128)S(1)} copy-done((f32[64,32768]{1,0:T(8,128)S(1)}, f32[64,32768]{1,0:T(8,128)}, u32[]{:S(2)}) %copy-start) | copy-done | bytes 8388632
  5.4 3.1 %design.12 = (f32[64,2560]{1,0:T(8,128)S(1)}, f32[64,640]{1,0:T(8,128)S(1)}) custom-call(s32[1,8]{1,0:T(1,128)S(1)} %copy-done.2, f32[1]{0:T(128)S(6)} %copy.5.lon_ref, s32[3,512]{1,0:T(4,128)S(1)} %copy-done.1, f32[64,32768]{1,0:T(8,128)S(1)} %copy-done), custom_call_target="tpu_custom_call" | custom-call | flops 6144000 | bytes 1638400 | tf_op jit(solution)/shard_map/jit(design_for)/design/pallas_call | solution.py:111
  8.5 3.0 %collective-permute-start.10 = (f32[64,2560]{1,0:T(8,128)S(1)}, f32[64,2560]{1,0:T(8,128)S(1)}, u32[]{:S(2)}, u32[]{:S(2)}) collective-permute-start(f32[64,2560]{1,0:T(8,128)S(1)} %get-tuple-element.41), channel_id=1, source_target_pairs={{0,4},{1,5},{2,6},{3,7},{4,0},{5,1},{6,2},{7,3},{8,12},{9,13},{10,... | collective-permute-start | bytes 1966088 | tf_op jit(solution)/shard_map/ppermute | solution.py:335
  11.5 3.1 %design.13 = (f32[64,2560]{1,0:T(8,128)S(1)}, f32[64,640]{1,0:T(8,128)S(1)}) custom-call(s32[1,8]{1,0:T(1,128)S(1)} %copy-done.2, f32[1]{0:T(128)S(6)} %copy.5.lon_ref, s32[3,512]{1,0:T(4,128)S(1)} %copy-done.1, f32[64,32768]{1,0:T(8,128)S(1)} %copy-done), custom_call_target="tpu_custom_call" | custom-call | flops 6144000 | bytes 1638400 | tf_op jit(solution)/shard_map/jit(design_for)/design/pallas_call | solution.py:111
  14.7 3.1 %design.9 = (f32[64,2560]{1,0:T(8,128)S(1)}, f32[64,640]{1,0:T(8,128)S(1)}) custom-call(s32[1,8]{1,0:T(1,128)S(1)} %copy-done.2, f32[1]{0:T(128)S(6)} %copy.5.lon_ref, s32[3,512]{1,0:T(4,128)S(1)} %copy-done.1, f32[64,32768]{1,0:T(8,128)S(1)} %copy-done), custom_call_target="tpu_custom_call" | custom-call | flops 6144000 | bytes 1638400 | tf_op jit(solution)/shard_map/jit(design_for)/design/pallas_call | solution.py:111
  17.9 3.1 %design.10 = (f32[64,2560]{1,0:T(8,128)S(1)}, f32[64,640]{1,0:T(8,128)S(1)}) custom-call(s32[1,8]{1,0:T(1,128)S(1)} %copy-done.2, f32[1]{0:T(128)S(6)} %copy.5.lon_ref, s32[3,512]{1,0:T(4,128)S(1)} %copy-done.1, f32[64,32768]{1,0:T(8,128)S(1)} %copy-done), custom_call_target="tpu_custom_call" | custom-call | flops 6144000 | bytes 1638400 | tf_op jit(solution)/shard_map/jit(design_for)/design/pallas_call | solution.py:111
  21.0 2.0 %collective-permute-start.1 = (f32[64,640]{1,0:T(8,128)S(1)}, f32[64,640]{1,0:T(8,128)S(1)}, u32[]{:S(2)}, u32[]{:S(2)}) collective-permute-start(f32[64,640]{1,0:T(8,128)S(1)} %get-tuple-element.31), channel_id=1, source_target_pairs={{0,2},{1,3},{2,0},{3,1},{4,6},{5,7},{6,4},{7,5},{8,10},{9,11},{10,... | collective-permute-start | bytes 491528 | tf_op jit(solution)/shard_map/ppermute | solution.py:335
  23.0 3.1 %design.14 = (f32[64,2560]{1,0:T(8,128)S(1)}, f32[64,640]{1,0:T(8,128)S(1)}) custom-call(s32[1,8]{1,0:T(1,128)S(1)} %copy-done.2, f32[1]{0:T(128)S(6)} %copy.5.lon_ref, s32[3,512]{1,0:T(4,128)S(1)} %copy-done.1, f32[64,32768]{1,0:T(8,128)S(1)} %copy-done), custom_call_target="tpu_custom_call" | custom-call | flops 6144000 | bytes 1638400 | tf_op jit(solution)/shard_map/jit(design_for)/design/pallas_call | solution.py:111
  27.7 3.1 %design.15 = (f32[64,2560]{1,0:T(8,128)S(1)}, f32[64,640]{1,0:T(8,128)S(1)}) custom-call(s32[1,8]{1,0:T(1,128)S(1)} %copy-done.2, f32[1]{0:T(128)S(6)} %copy.5.lon_ref, s32[3,512]{1,0:T(4,128)S(1)} %copy-done.1, f32[64,32768]{1,0:T(8,128)S(1)} %copy-done), custom_call_target="tpu_custom_call" | custom-call | flops 6144000 | bytes 1638400 | tf_op jit(solution)/shard_map/jit(design_for)/design/pallas_call | solution.py:111
  30.8 3.1 %design.11 = (f32[64,2560]{1,0:T(8,128)S(1)}, f32[64,640]{1,0:T(8,128)S(1)}) custom-call(s32[1,8]{1,0:T(1,128)S(1)} %copy-done.2, f32[1]{0:T(128)S(6)} %copy.5.lon_ref, s32[3,512]{1,0:T(4,128)S(1)} %copy-done.1, f32[64,32768]{1,0:T(8,128)S(1)} %copy-done), custom_call_target="tpu_custom_call" | custom-call | flops 6144000 | bytes 1638400 | tf_op jit(solution)/shard_map/jit(design_for)/design/pallas_call | solution.py:111
  35.6 32.0 %collective-permute-done.11.refs_5_ = f32[64,2560]{1,0:T(8,128)S(1)} collective-permute-done((f32[64,2560]{1,0:T(8,128)S(1)}, f32[64,2560]{1,0:T(8,128)S(1)}, u32[]{:S(2)}, u32[]{:S(2)}) %collective-permute-start.11) | collective-permute-done | bytes 655392 | tf_op jit(solution)/shard_map/ppermute | solution.py:335
  67.6 2.2 %collective-permute-start.9 = (f32[64,2560]{1,0:T(8,128)S(1)}, f32[64,2560]{1,0:T(8,128)S(1)}, u32[]{:S(2)}, u32[]{:S(2)}) collective-permute-start(f32[64,2560]{1,0:T(8,128)S(1)} %get-tuple-element.40), channel_id=1, source_target_pairs={{0,3},{1,2},{2,1},{3,0},{4,7},{5,6},{6,5},{7,4},{8,11},{9,10},{10,... | collective-permute-start | bytes 1966088 | tf_op jit(solution)/shard_map/ppermute | solution.py:335
  69.8 3.1 %design.8 = (f32[64,2560]{1,0:T(8,128)S(1)}, f32[64,640]{1,0:T(8,128)S(1)}) custom-call(s32[1,8]{1,0:T(1,128)S(1)} %copy-done.2, f32[1]{0:T(128)S(6)} %copy.5.lon_ref, s32[3,512]{1,0:T(4,128)S(1)} %copy-done.1, f32[64,32768]{1,0:T(8,128)S(1)} %copy-done), custom_call_target="tpu_custom_call" | custom-call | flops 6144000 | bytes 1638400 | tf_op jit(solution)/shard_map/jit(design_for)/design/pallas_call | solution.py:111
  73.0 1.6 %collective-permute-start.3 = (f32[64,640]{1,0:T(8,128)S(1)}, f32[64,640]{1,0:T(8,128)S(1)}, u32[]{:S(2)}, u32[]{:S(2)}) collective-permute-start(f32[64,640]{1,0:T(8,128)S(1)} %get-tuple-element.33), channel_id=1, source_target_pairs={{0,4},{1,5},{2,6},{3,7},{4,0},{5,1},{6,2},{7,3},{8,12},{9,13},{10,... | collective-permute-start | bytes 491528 | tf_op jit(solution)/shard_map/ppermute | solution.py:335
  74.8 2.6 %collective-permute-start.5 = (f32[64,640]{1,0:T(8,128)S(1)}, f32[64,640]{1,0:T(8,128)S(1)}, u32[]{:S(2)}, u32[]{:S(2)}) collective-permute-start(f32[64,640]{1,0:T(8,128)S(1)} %get-tuple-element.35), channel_id=1, source_target_pairs={{0,6},{1,7},{2,4},{3,5},{4,2},{5,3},{6,0},{7,1},{8,14},{9,15},{10,... | collective-permute-start | bytes 491528 | tf_op jit(solution)/shard_map/ppermute | solution.py:335
  77.4 7.7 %collective-permute-done.9.refs_3_ = f32[64,2560]{1,0:T(8,128)S(1)} collective-permute-done((f32[64,2560]{1,0:T(8,128)S(1)}, f32[64,2560]{1,0:T(8,128)S(1)}, u32[]{:S(2)}, u32[]{:S(2)}) %collective-permute-start.9) | collective-permute-done | bytes 655392 | tf_op jit(solution)/shard_map/ppermute | solution.py:335
  85.1 3.0 %collective-permute-start.6 = (f32[64,640]{1,0:T(8,128)S(1)}, f32[64,640]{1,0:T(8,128)S(1)}, u32[]{:S(2)}, u32[]{:S(2)}) collective-permute-start(f32[64,640]{1,0:T(8,128)S(1)} %get-tuple-element.36), channel_id=1, source_target_pairs={{0,7},{1,6},{2,5},{3,4},{4,3},{5,2},{6,1},{7,0},{8,15},{9,14},{10,... | collective-permute-start | bytes 491528 | tf_op jit(solution)/shard_map/ppermute | solution.py:335
  88.1 8.9 %gram.2.refs_8_ = f32[512,512]{1,0:T(8,128)S(1)} custom-call(f32[64,2560]{1,0:T(8,128)S(1)} %get-tuple-element.37.refs_0_, f32[64,2560]{1,0:T(8,128)S(1)} %collective-permute-done.7.refs_1_, f32[64,2560]{1,0:T(8,128)S(1)} %collective-permute-done.8.refs_2_, f32[64,2560]{1,0:T(8,128)S(1)} %collective-permute-done.9.refs_3_, ...), custom_call_target="tpu_custom_call" | custom-call | flops 4026531840 | bytes 5242880 | tf_op jit(solution)/shard_map/gram/pallas_call | solution.py:199
  105.8 4.1 %collective-permute-done.18 = f32[160,128]{1,0:T(8,128)S(1)} collective-permute-done((f32[160,128]{1,0:T(8,128)S(1)}, f32[160,128]{1,0:T(8,128)S(1)}, u32[]{:S(2)}, u32[]{:S(2)}) %collective-permute-start.18) | collective-permute-done | bytes 81952 | tf_op jit(solution)/shard_map/ppermute | solution.py:335
  109.9 1.7 %collective-permute-start.21 = (f32[160,128]{1,0:T(8,128)S(1)}, f32[160,128]{1,0:T(8,128)S(1)}, u32[]{:S(2)}, u32[]{:S(2)}) collective-permute-start(f32[160,128]{1,0:T(8,128)S(1)} %add_add_fusion.1), channel_id=1, source_target_pairs={{0,8},{8,0},{16,24},{24,16},{1,9},{9,1},{17,25},{25,17},{2,10},{10... | collective-permute-start | bytes 245768 | tf_op jit(solution)/shard_map/ppermute | solution.py:335
  111.6 2.6 %collective-permute-start.22 = (f32[160,128]{1,0:T(8,128)S(1)}, f32[160,128]{1,0:T(8,128)S(1)}, u32[]{:S(2)}, u32[]{:S(2)}) collective-permute-start(f32[160,128]{1,0:T(8,128)S(1)} %add_add_fusion.1), channel_id=1, source_target_pairs={{0,16},{8,24},{16,0},{24,8},{1,17},{9,25},{17,1},{25,9},{2,18},{10... | collective-permute-start | bytes 245768 | tf_op jit(solution)/shard_map/ppermute | solution.py:335
  114.7 6.3 %collective-permute-done.22 = f32[160,128]{1,0:T(8,128)S(1)} collective-permute-done((f32[160,128]{1,0:T(8,128)S(1)}, f32[160,128]{1,0:T(8,128)S(1)}, u32[]{:S(2)}, u32[]{:S(2)}) %collective-permute-start.22) | collective-permute-done | bytes 81952 | tf_op jit(solution)/shard_map/ppermute | solution.py:335
  128.3 4.1 %collective-permute-done.28.refs_5_ = f32[160,128]{1,0:T(8,128)S(1)} collective-permute-done((f32[160,128]{1,0:T(8,128)S(1)}, f32[160,128]{1,0:T(8,128)S(1)}, u32[]{:S(2)}, u32[]{:S(2)}) %collective-permute-start.28) | collective-permute-done | bytes 81952 | tf_op jit(solution)/shard_map/ppermute | solution.py:335
  132.4 17.5 %factor.1 = f32[512,512]{1,0:T(8,128)} custom-call(f32[1,512]{1,0:T(1,128)S(1)} %multiply_multiply_fusion.kaula_ref, f32[160,128]{1,0:T(8,128)S(1)} %add_add_fusion.refs_0_, f32[160,128]{1,0:T(8,128)S(1)} %collective-permute-done.24.refs_1_, f32[160,128]{1,0:T(8,128)S(1)} %collective-permute-done.25.refs_2_, f32[160,128]{1,0:T(8,128)S(1)} %collective-permute-done.26.refs_3_, ...), custom_call_target="tpu_custom_call" | custom-call | tf_op jit(solution)/shard_map/factor/pallas_call | solution.py:316
  (58 shorter events, 21.6 us)
Async XLA Ops:
  8.5 27.0 %collective-permute-start.10 = (f32[64,2560]{1,0:T(8,128)S(1)}, f32[64,2560]{1,0:T(8,128)S(1)}, u32[]{:S(2)}, u32[]{:S(2)}) collective-permute-start(f32[64,2560]{1,0:T(8,128)S(1)} %get-tuple-element.41), channel_id=1, source_target_pairs={{0,4},{1,5},{2,6},{3,7},{4,0},{5,1},{6,2},{7,3},{8,12},{9,13},{10,... | collective-permute-start | bytes 1966088 | tf_op jit(solution)/shard_map/ppermute | solution.py:335
  14.6 53.0 %collective-permute-start.11 = (f32[64,2560]{1,0:T(8,128)S(1)}, f32[64,2560]{1,0:T(8,128)S(1)}, u32[]{:S(2)}, u32[]{:S(2)}) collective-permute-start(f32[64,2560]{1,0:T(8,128)S(1)} %get-tuple-element.42), channel_id=1, source_target_pairs={{0,5},{1,4},{2,7},{3,6},{4,1},{5,0},{6,3},{7,2},{8,13},{9,12},{10,... | collective-permute-start | bytes 1966088 | tf_op jit(solution)/shard_map/ppermute | solution.py:335
  17.7 16.1 %collective-permute-start = (f32[64,640]{1,0:T(8,128)S(1)}, f32[64,640]{1,0:T(8,128)S(1)}, u32[]{:S(2)}, u32[]{:S(2)}) collective-permute-start(f32[64,640]{1,0:T(8,128)S(1)} %get-tuple-element.30), channel_id=1, source_target_pairs={{0,1},{1,0},{2,3},{3,2},{4,5},{5,4},{6,7},{7,6},{8,9},{9,8},{10,11... | collective-permute-start | bytes 491528 | tf_op jit(solution)/shard_map/ppermute | solution.py:335
  21.0 13.4 %collective-permute-start.1 = (f32[64,640]{1,0:T(8,128)S(1)}, f32[64,640]{1,0:T(8,128)S(1)}, u32[]{:S(2)}, u32[]{:S(2)}) collective-permute-start(f32[64,640]{1,0:T(8,128)S(1)} %get-tuple-element.31), channel_id=1, source_target_pairs={{0,2},{1,3},{2,0},{3,1},{4,6},{5,7},{6,4},{7,5},{8,10},{9,11},{10,... | collective-permute-start | bytes 491528 | tf_op jit(solution)/shard_map/ppermute | solution.py:335
  26.1 46.7 %collective-permute-start.12 = (f32[64,2560]{1,0:T(8,128)S(1)}, f32[64,2560]{1,0:T(8,128)S(1)}, u32[]{:S(2)}, u32[]{:S(2)}) collective-permute-start(f32[64,2560]{1,0:T(8,128)S(1)} %get-tuple-element.43), channel_id=1, source_target_pairs={{0,6},{1,7},{2,4},{3,5},{4,2},{5,3},{6,0},{7,1},{8,14},{9,15},{10,... | collective-permute-start | bytes 1966088 | tf_op jit(solution)/shard_map/ppermute | solution.py:335
  33.9 39.1 %collective-permute-start.13 = (f32[64,2560]{1,0:T(8,128)S(1)}, f32[64,2560]{1,0:T(8,128)S(1)}, u32[]{:S(2)}, u32[]{:S(2)}) collective-permute-start(f32[64,2560]{1,0:T(8,128)S(1)} %get-tuple-element.44), channel_id=1, source_target_pairs={{0,7},{1,6},{2,5},{3,4},{4,3},{5,2},{6,1},{7,0},{8,15},{9,14},{10,... | collective-permute-start | bytes 1966088 | tf_op jit(solution)/shard_map/ppermute | solution.py:335
  34.4 40.1 %collective-permute-start.7 = (f32[64,2560]{1,0:T(8,128)S(1)}, f32[64,2560]{1,0:T(8,128)S(1)}, u32[]{:S(2)}, u32[]{:S(2)}) collective-permute-start(f32[64,2560]{1,0:T(8,128)S(1)} %get-tuple-element.38), channel_id=1, source_target_pairs={{0,1},{1,0},{2,3},{3,2},{4,5},{5,4},{6,7},{7,6},{8,9},{9,8},{10,11... | collective-permute-start | bytes 1966088 | tf_op jit(solution)/shard_map/ppermute | solution.py:335
  35.5 39.3 %collective-permute-start.8 = (f32[64,2560]{1,0:T(8,128)S(1)}, f32[64,2560]{1,0:T(8,128)S(1)}, u32[]{:S(2)}, u32[]{:S(2)}) collective-permute-start(f32[64,2560]{1,0:T(8,128)S(1)} %get-tuple-element.39), channel_id=1, source_target_pairs={{0,2},{1,3},{2,0},{3,1},{4,6},{5,7},{6,4},{7,5},{8,10},{9,11},{10,... | collective-permute-start | bytes 1966088 | tf_op jit(solution)/shard_map/ppermute | solution.py:335
  67.6 17.5 %collective-permute-start.9 = (f32[64,2560]{1,0:T(8,128)S(1)}, f32[64,2560]{1,0:T(8,128)S(1)}, u32[]{:S(2)}, u32[]{:S(2)}) collective-permute-start(f32[64,2560]{1,0:T(8,128)S(1)} %get-tuple-element.40), channel_id=1, source_target_pairs={{0,3},{1,2},{2,1},{3,0},{4,7},{5,6},{6,5},{7,4},{8,11},{9,10},{10,... | collective-permute-start | bytes 1966088 | tf_op jit(solution)/shard_map/ppermute | solution.py:335
  72.9 24.2 %collective-permute-start.2 = (f32[64,640]{1,0:T(8,128)S(1)}, f32[64,640]{1,0:T(8,128)S(1)}, u32[]{:S(2)}, u32[]{:S(2)}) collective-permute-start(f32[64,640]{1,0:T(8,128)S(1)} %get-tuple-element.32), channel_id=1, source_target_pairs={{0,3},{1,2},{2,1},{3,0},{4,7},{5,6},{6,5},{7,4},{8,11},{9,10},{10,... | collective-permute-start | bytes 491528 | tf_op jit(solution)/shard_map/ppermute | solution.py:335
  73.0 24.1 %collective-permute-start.3 = (f32[64,640]{1,0:T(8,128)S(1)}, f32[64,640]{1,0:T(8,128)S(1)}, u32[]{:S(2)}, u32[]{:S(2)}) collective-permute-start(f32[64,640]{1,0:T(8,128)S(1)} %get-tuple-element.33), channel_id=1, source_target_pairs={{0,4},{1,5},{2,6},{3,7},{4,0},{5,1},{6,2},{7,3},{8,12},{9,13},{10,... | collective-permute-start | bytes 491528 | tf_op jit(solution)/shard_map/ppermute | solution.py:335
  74.6 22.6 %collective-permute-start.4 = (f32[64,640]{1,0:T(8,128)S(1)}, f32[64,640]{1,0:T(8,128)S(1)}, u32[]{:S(2)}, u32[]{:S(2)}) collective-permute-start(f32[64,640]{1,0:T(8,128)S(1)} %get-tuple-element.34), channel_id=1, source_target_pairs={{0,5},{1,4},{2,7},{3,6},{4,1},{5,0},{6,3},{7,2},{8,13},{9,12},{10,... | collective-permute-start | bytes 491528 | tf_op jit(solution)/shard_map/ppermute | solution.py:335
  74.8 22.3 %collective-permute-start.5 = (f32[64,640]{1,0:T(8,128)S(1)}, f32[64,640]{1,0:T(8,128)S(1)}, u32[]{:S(2)}, u32[]{:S(2)}) collective-permute-start(f32[64,640]{1,0:T(8,128)S(1)} %get-tuple-element.35), channel_id=1, source_target_pairs={{0,6},{1,7},{2,4},{3,5},{4,2},{5,3},{6,0},{7,1},{8,14},{9,15},{10,... | collective-permute-start | bytes 491528 | tf_op jit(solution)/shard_map/ppermute | solution.py:335
  85.1 12.0 %collective-permute-start.6 = (f32[64,640]{1,0:T(8,128)S(1)}, f32[64,640]{1,0:T(8,128)S(1)}, u32[]{:S(2)}, u32[]{:S(2)}) collective-permute-start(f32[64,640]{1,0:T(8,128)S(1)} %get-tuple-element.36), channel_id=1, source_target_pairs={{0,7},{1,6},{2,5},{3,4},{4,3},{5,2},{6,1},{7,0},{8,15},{9,14},{10,... | collective-permute-start | bytes 491528 | tf_op jit(solution)/shard_map/ppermute | solution.py:335
  99.1 5.8 %collective-permute-start.16 = (f32[160,128]{1,0:T(8,128)S(1)}, f32[160,128]{1,0:T(8,128)S(1)}, u32[]{:S(2)}, u32[]{:S(2)}) collective-permute-start(f32[160,128]{1,0:T(8,128)S(1)} %get-tuple-element.48), channel_id=1, source_target_pairs={{0,3},{1,2},{2,1},{3,0},{4,7},{5,6},{6,5},{7,4},{8,11},{9,10},{10,... | collective-permute-start | bytes 245768 | tf_op jit(solution)/shard_map/ppermute | solution.py:335
  101.0 8.9 %collective-permute-start.18 = (f32[160,128]{1,0:T(8,128)S(1)}, f32[160,128]{1,0:T(8,128)S(1)}, u32[]{:S(2)}, u32[]{:S(2)}) collective-permute-start(f32[160,128]{1,0:T(8,128)S(1)} %get-tuple-element.50), channel_id=1, source_target_pairs={{0,5},{1,4},{2,7},{3,6},{4,1},{5,0},{6,3},{7,2},{8,13},{9,12},{10,... | collective-permute-start | bytes 245768 | tf_op jit(solution)/shard_map/ppermute | solution.py:335
  102.2 7.7 %collective-permute-start.19 = (f32[160,128]{1,0:T(8,128)S(1)}, f32[160,128]{1,0:T(8,128)S(1)}, u32[]{:S(2)}, u32[]{:S(2)}) collective-permute-start(f32[160,128]{1,0:T(8,128)S(1)} %get-tuple-element.51), channel_id=1, source_target_pairs={{0,6},{1,7},{2,4},{3,5},{4,2},{5,3},{6,0},{7,1},{8,14},{9,15},{10,... | collective-permute-start | bytes 245768 | tf_op jit(solution)/shard_map/ppermute | solution.py:335
  103.9 5.9 %collective-permute-start.20 = (f32[160,128]{1,0:T(8,128)S(1)}, f32[160,128]{1,0:T(8,128)S(1)}, u32[]{:S(2)}, u32[]{:S(2)}) collective-permute-start(f32[160,128]{1,0:T(8,128)S(1)} %get-tuple-element.52), channel_id=1, source_target_pairs={{0,7},{1,6},{2,5},{3,4},{4,3},{5,2},{6,1},{7,0},{8,15},{9,14},{10,... | collective-permute-start | bytes 245768 | tf_op jit(solution)/shard_map/ppermute | solution.py:335
  111.6 9.4 %collective-permute-start.22 = (f32[160,128]{1,0:T(8,128)S(1)}, f32[160,128]{1,0:T(8,128)S(1)}, u32[]{:S(2)}, u32[]{:S(2)}) collective-permute-start(f32[160,128]{1,0:T(8,128)S(1)} %add_add_fusion.1), channel_id=1, source_target_pairs={{0,16},{8,24},{16,0},{24,8},{1,17},{9,25},{17,1},{25,9},{2,18},{10... | collective-permute-start | bytes 245768 | tf_op jit(solution)/shard_map/ppermute | solution.py:335
  114.2 6.9 %collective-permute-start.23 = (f32[160,128]{1,0:T(8,128)S(1)}, f32[160,128]{1,0:T(8,128)S(1)}, u32[]{:S(2)}, u32[]{:S(2)}) collective-permute-start(f32[160,128]{1,0:T(8,128)S(1)} %add_add_fusion.1), channel_id=1, source_target_pairs={{0,24},{8,16},{16,8},{24,0},{1,25},{9,17},{17,9},{25,1},{2,26},{10... | collective-permute-start | bytes 245768 | tf_op jit(solution)/shard_map/ppermute | solution.py:335
  121.7 6.5 %collective-permute-start.26 = (f32[160,128]{1,0:T(8,128)S(1)}, f32[160,128]{1,0:T(8,128)S(1)}, u32[]{:S(2)}, u32[]{:S(2)}) collective-permute-start(f32[160,128]{1,0:T(8,128)S(1)} %add_add_fusion.refs_0_), channel_id=1, source_target_pairs={{0,3},{1,2},{2,1},{3,0},{4,7},{5,6},{6,5},{7,4},{8,11},{9,10},{10,... | collective-permute-start | bytes 245768 | tf_op jit(solution)/shard_map/ppermute | solution.py:335
  123.9 8.5 %collective-permute-start.28 = (f32[160,128]{1,0:T(8,128)S(1)}, f32[160,128]{1,0:T(8,128)S(1)}, u32[]{:S(2)}, u32[]{:S(2)}) collective-permute-start(f32[160,128]{1,0:T(8,128)S(1)} %add_add_fusion.refs_0_), channel_id=1, source_target_pairs={{0,5},{1,4},{2,7},{3,6},{4,1},{5,0},{6,3},{7,2},{8,13},{9,12},{10,... | collective-permute-start | bytes 245768 | tf_op jit(solution)/shard_map/ppermute | solution.py:335
  124.7 7.7 %collective-permute-start.29 = (f32[160,128]{1,0:T(8,128)S(1)}, f32[160,128]{1,0:T(8,128)S(1)}, u32[]{:S(2)}, u32[]{:S(2)}) collective-permute-start(f32[160,128]{1,0:T(8,128)S(1)} %add_add_fusion.refs_0_), channel_id=1, source_target_pairs={{0,6},{1,7},{2,4},{3,5},{4,2},{5,3},{6,0},{7,1},{8,14},{9,15},{10,... | collective-permute-start | bytes 245768 | tf_op jit(solution)/shard_map/ppermute | solution.py:335
  126.5 5.9 %collective-permute-start.30 = (f32[160,128]{1,0:T(8,128)S(1)}, f32[160,128]{1,0:T(8,128)S(1)}, u32[]{:S(2)}, u32[]{:S(2)}) collective-permute-start(f32[160,128]{1,0:T(8,128)S(1)} %add_add_fusion.refs_0_), channel_id=1, source_target_pairs={{0,7},{1,6},{2,5},{3,4},{4,3},{5,2},{6,1},{7,0},{8,15},{9,14},{10,... | collective-permute-start | bytes 245768 | tf_op jit(solution)/shard_map/ppermute | solution.py:335
  (10 other events, 38.0 us)

commit v2 on v1

v2 whole, which is shorter than its diff:
```python
import functools
import math

import jax
import jax.numpy as jnp
from jax import lax
from jax.experimental import pallas as pl
from jax.experimental.pallas import tpu as pltpu
from jax.sharding import PartitionSpec as P

NMAX = 120
LANES = 128
SUBS = 8

quarter_turn = math.pi / 2
track_span = 0.3
kaula_gain = 1.2
VMEM = pltpu.VMEM
SMEM = pltpu.SMEM


def wave_pair(x):
    turns = jnp.floor(x * (1.0 / math.pi) + 0.5)
    rest = x - turns * 3.140625
    rest = rest - turns * 9.67653589793e-4
    half = turns * 0.5
    sign = 1.0 - 4.0 * (half - jnp.floor(half))
    sq = rest * rest

    def series(powers):
        acc = None
        for power in powers:
            term = (-1.0) ** (power // 2) / math.factorial(power)
            acc = term if acc is None else acc * sq + term
        return acc

    return series((12, 10, 8, 6, 4, 2, 0)) * sign, series((13, 11, 9, 7, 5, 3, 1)) * rest * sign


def design_kernel(shape, k, counts_ref, lon_ref, index_ref, leg_ref, *refs):
    n, sizes, rows_dev, rows_grp, scaling = shape
    outs, (held, sems) = refs[:-2], refs[-2:]
    per = sum(sizes)
    blocks_dev = rows_dev // LANES
    me = lax.axis_index("ord")
    count = [counts_ref[0, r] for r in range(n)]
    ends, total = [], 0
    for r in range(n):
        total = total + lax.div(count[r] + (LANES - 1), LANES)
        ends.append(total)

    def place(want):
        slot, begin, held_rows = 0, 0, count[0]
        for r in range(n - 1):
            past = want >= ends[r]
            slot = jnp.where(past, r + 1, slot)
            begin = jnp.where(past, ends[r], begin)
            held_rows = jnp.where(past, count[r + 1], held_rows)
        inside = jnp.minimum(want - begin, blocks_dev - 1)
        valid = jnp.where(want < total, held_rows - (want - begin) * LANES, 0)
        return slot * rows_dev + inside * LANES, valid

    def copy(i, start):
        return pltpu.make_async_copy(
            leg_ref.at[:, pl.ds(start, LANES)], held.at[:, pl.ds(i * LANES, LANES)], sems.at[i]
        )

    valids = []
    for i in range(per):
        start, valid = place((me ^ k) * per + i)
        copy(i, pl.multiple_of(start, LANES)).start()
        valids.append(valid)
    rows = held.shape[0]
    wide = (rows, index_ref.shape[1])
    mine = lax.broadcasted_iota(jnp.int32, wide, 1) == lax.broadcasted_iota(jnp.int32, wide, 0) + me * rows

    def column(row):
        values = jnp.broadcast_to(index_ref[row : row + 1, :].astype(jnp.float32), wide)
        picked = jnp.sum(jnp.where(mine, values, 0.0), axis=1, keepdims=True)
        return jnp.broadcast_to(picked, (rows, LANES))

    harmonic = column(1)
    phase = column(2) * quarter_turn
    lane = lax.broadcasted_iota(jnp.int32, (SUBS, LANES), 1)
    pace = track_span / rows_grp
    along = lane.astype(jnp.float32) * pace
    tops = range(0, rows, SUBS)
    inner = [wave_pair(harmonic[top : top + SUBS] * along) for top in tops]
    begin = place((me ^ k) * per + lane)[0].astype(jnp.float32)
    longitude = lon_ref[0] + begin * pace
    outer = [
        wave_pair(harmonic[top : top + SUBS] * longitude - phase[top : top + SUBS]) for top in tops
    ]
    spots = [(out, i) for out, size in zip(outs, sizes) for i in range(size)]
    for i, (out, spot) in enumerate(spots):
        copy(i, 0).wait()
        gate = jnp.where(lane < valids[i], scaling, 0.0)
        for t, top in enumerate(tops):
            wave = lane_wide(outer[t][0], i) * inner[t][0] - lane_wide(outer[t][1], i) * inner[t][1]
            tile = held[pl.ds(top, SUBS), pl.ds(i * LANES, LANES)]
            out[pl.ds(top, SUBS), pl.ds(spot * LANES, LANES)] = tile * wave * gate


@functools.partial(jax.jit, static_argnums=(0, 1))
def design(shape, k, counts, lon_center, column_index, legendre):
    sizes, rows = shape[1], legendre.shape[0]
    elements = rows * sum(sizes) * LANES
    return pl.pallas_call(
        functools.partial(design_kernel, shape, k),
        out_shape=[jax.ShapeDtypeStruct((rows, size * LANES), jnp.float32) for size in sizes],
        in_specs=[
            pl.BlockSpec(memory_space=SMEM),
            pl.BlockSpec(memory_space=SMEM),
            pl.BlockSpec(memory_space=VMEM),
            pl.BlockSpec(memory_space=pltpu.HBM),
        ],
        out_specs=[pl.BlockSpec(memory_space=VMEM)] * len(sizes),
        scratch_shapes=[
            pltpu.VMEM((rows, sum(sizes) * LANES), jnp.float32),
            pltpu.SemaphoreType.DMA((sum(sizes),)),
        ],
        compiler_params=pltpu.CompilerParams(vmem_limit_bytes=56 << 20),
        cost_estimate=pl.CostEstimate(flops=8 * elements, bytes_accessed=8 * elements, transcendentals=0),
        name="design",
    )(counts, lon_center, column_index, legendre)


def lane_wide(x, j):
    return jnp.broadcast_to(x[:, j : j + 1], (SUBS, LANES))


def upper_blocks(cols):
    nb = cols // LANES
    return [(i, j) for i in range(nb) for j in range(i, nb)]


def gram_kernel(n, cols, tile, first, last, *refs):
    ins, refs = refs[:n], refs[n:]
    before = None
    if not first:
        before, refs = refs[0], refs[1:]
    outs, scratch = refs[: n if last else 1], refs[n if last else 1 :]
    high, low = scratch[:2]
    acc = scratch[2] if last else outs[0]
    me = lax.axis_index("ord")
    each, rows = ins[0].shape

    def times(a, b):
        return lax.dot_general(a, b, (((1,), (1,)), ((), ())), preferred_element_type=jnp.float32)

    tall = min(256, cols)
    for s in range(rows // tile):
        for k in range(n):
            part = ins[k][:, pl.ds(s * tile, tile)]
            at = pl.ds(pl.multiple_of((me ^ k) * each, each), each)
            top = part.astype(jnp.bfloat16)
            high[s % 2, at, :] = top
            low[s % 2, at, :] = (part - top.astype(jnp.float32)).astype(jnp.bfloat16)
        for i in range(0, cols, tall):
            hi, lo = high[s % 2, pl.ds(i, tall), :], low[s % 2, pl.ds(i, tall), :]
            his, los = high[s % 2, pl.ds(i, cols - i), :], low[s % 2, pl.ds(i, cols - i), :]
            at = (pl.ds(i, tall), pl.ds(i, cols - i))
            here = times(hi, his) + (times(hi, los) + times(lo, his))
            if s:
                acc[at] += here
            else:
                acc[at] = here if first else before[at] + here

    if last:
        packed = scratch[3]
        for t, (i, j) in enumerate(upper_blocks(cols)):
            packed[pl.ds(t * LANES, LANES), :] = acc[pl.ds(i * LANES, LANES), pl.ds(j * LANES, LANES)]
        piece = packed.shape[0] // n
        for k in range(n):
            outs[k][...] = packed[pl.ds(pl.multiple_of((me ^ k) * piece, SUBS), piece), :]


def gram(n, parts, before, last):
    each, rows = parts[0].shape
    cols = each * n
    tile = 640 if rows % 640 == 0 else LANES
    height = len(upper_blocks(cols)) * LANES
    scratch = [pltpu.VMEM((2, cols, tile), jnp.bfloat16)] * 2
    if last:
        out_shape = [jax.ShapeDtypeStruct((height // n, LANES), jnp.float32)] * n
        scratch += [pltpu.VMEM((cols, cols), jnp.float32), pltpu.VMEM((height, LANES), jnp.float32)]
    else:
        out_shape = [jax.ShapeDtypeStruct((cols, cols), jnp.float32)]
    return pl.pallas_call(
        functools.partial(gram_kernel, n, cols, tile, not before, last),
        out_shape=out_shape,
        in_specs=[pl.BlockSpec(memory_space=VMEM)] * (n + len(before)),
        out_specs=[pl.BlockSpec(memory_space=VMEM)] * len(out_shape),
        scratch_shapes=scratch,
        compiler_params=pltpu.CompilerParams(vmem_limit_bytes=32 << 20),
        cost_estimate=pl.CostEstimate(
            flops=6 * cols * cols * rows, bytes_accessed=4 * cols * rows, transcendentals=0
        ),
        name="gram",
    )(*parts, *before)


def row_wide(ref, row, column):
    return jnp.broadcast_to(ref[pl.ds(row, 1), pl.ds(column, LANES)], (SUBS, LANES))


def factor_panel(a_ref, r_ref, u_ref, t_ref, base, p, wide, lane, sub, columns):
    groups = LANES // SUBS
    row0, c0 = base + SUBS * p, SUBS * p
    slot = (p % 2) * SUBS * SUBS
    if columns is None:
        own = a_ref[pl.ds(row0, SUBS), pl.ds(base, LANES)]
        columns = [lane_wide(own, c0 + j) for j in range(SUBS)]
    for j in range(SUBS):
        u_ref[pl.ds(slot + SUBS * j, SUBS), :] = columns[j]
    d = {(i, j): row_wide(u_ref, slot + SUBS * j + i, 0) for j in range(SUBS) for i in range(j + 1)}
    inv, up = [None] * SUBS, {}
    for i in range(SUBS):
        inv[i] = lax.rsqrt(d[i, i])
        for j in range(i + 1, SUBS):
            up[i, j] = d[i, j] * inv[i]
        for a in range(i + 1, SUBS):
            for b in range(a, SUBS):
                d[a, b] = d[a, b] - up[i, a] * up[i, b]
    coef, following = [], None
    if p + 1 < groups:
        below = a_ref[pl.ds(row0 + SUBS, SUBS), pl.ds(base, LANES)]
        for j in range(SUBS):
            acc = lane_wide(below, c0 + j)
            for i in range(j):
                acc = acc - up[i, j] * coef[i]
            coef.append(acc * inv[j])
            t_ref[pl.ds(slot + SUBS * j, SUBS), :] = coef[j]
        following = [
            lane_wide(below, c0 + SUBS + b)
            - tree_sum([coef[j] * row_wide(t_ref, slot + SUBS * j + b, 0) for j in range(SUBS)])
            for b in range(SUBS)
        ]
    done = [[None] * SUBS for _ in range(wide)]
    for w in range(wide):
        for i in range(SUBS):
            acc = row_wide(a_ref, row0 + i, base + LANES * w)
            for j in range(i):
                acc = acc - up[j, i] * done[w][j]
            done[w][i] = acc * inv[i]

    def update(g, coef, rows):
        for w in range(wide):
            at = (pl.ds(base + SUBS * g, SUBS), pl.ds(base + LANES * w, LANES))
            a_ref[at] = a_ref[at] - tree_sum([coef[j] * rows[w][j] for j in range(SUBS)])

    if p + 1 < groups:
        update(p + 1, coef, done)
    if p + 2 < groups:
        solved = [[None] * SUBS for _ in range(wide)]
        for w in range(wide):
            for i in range(SUBS - 1, -1, -1):
                acc = done[w][i]
                for j in range(i + 1, SUBS):
                    acc = acc - up[i, j] * solved[w][j]
                solved[w][i] = acc * inv[i]
        for g in range(p + 2, groups):
            below = a_ref[pl.ds(base + SUBS * g, SUBS), pl.ds(base, LANES)]
            update(g, [lane_wide(below, c0 + j) for j in range(SUBS)], solved)
    for w in range(wide):
        out = done[w][0]
        for i in range(1, SUBS):
            out = jnp.where(sub == i, done[w][i], out)
        if w == 0:
            out = jnp.where(lane >= sub + c0, out, 0.0)
        r_ref[pl.ds(row0, SUBS), pl.ds(base + LANES * w, LANES)] = out
    return following


def factor_kernel(n, cols, kaula_ref, *refs):
    ins, (r_ref, a_ref, packed, u_ref, t_ref) = refs[:n], refs[n:]
    me = lax.axis_index("ord")
    piece = packed.shape[0] // n
    for k in range(n):
        packed[pl.ds(pl.multiple_of((me ^ k) * piece, SUBS), piece), :] = ins[k][...]
    square = (LANES, LANES)
    diag = lax.broadcasted_iota(jnp.int32, square, 0) == lax.broadcasted_iota(jnp.int32, square, 1)
    for t, (i, j) in enumerate(upper_blocks(cols)):
        block = packed[pl.ds(t * LANES, LANES), :]
        if i == j:
            block = block + jnp.where(diag, kaula_ref[:, pl.ds(i * LANES, LANES)], 0.0)
        a_ref[pl.ds(i * LANES, LANES), pl.ds(j * LANES, LANES)] = block
    lane = lax.broadcasted_iota(jnp.int32, (SUBS, LANES), 1)
    sub = lax.broadcasted_iota(jnp.int32, (SUBS, LANES), 0)
    count = cols // LANES
    for k in range(count):
        base, wide = k * LANES, count - k
        if base:
            r_ref[pl.ds(base, LANES), pl.ds(0, base)] = jnp.zeros((LANES, base), jnp.float32)
        columns = None
        for p in range(LANES // SUBS):
            columns = factor_panel(a_ref, r_ref, u_ref, t_ref, base, p, wide, lane, sub, columns)
        for i in range(k + 1, count):
            left = r_ref[pl.ds(base, LANES), pl.ds(i * LANES, LANES)]
            right = r_ref[pl.ds(base, LANES), pl.ds(i * LANES, cols - i * LANES)]
            a_ref[pl.ds(i * LANES, LANES), pl.ds(i * LANES, cols - i * LANES)] -= lax.dot_general(
                left,
                right,
                (((0,), (0,)), ((), ())),
                precision=lax.Precision.HIGHEST,
                preferred_element_type=jnp.float32,
            )


def factor(n, cols, kaula_square, pieces):
    height = len(upper_blocks(cols)) * LANES
    return pl.pallas_call(
        functools.partial(factor_kernel, n, cols),
        out_shape=jax.ShapeDtypeStruct((cols, cols), jnp.float32),
        in_specs=[pl.BlockSpec(memory_space=VMEM)] * (n + 1),
        out_specs=pl.BlockSpec(memory_space=VMEM),
        scratch_shapes=[
            pltpu.VMEM((cols, cols), jnp.float32),
            pltpu.VMEM((height, LANES), jnp.float32),
            pltpu.VMEM((2 * SUBS * SUBS, LANES), jnp.float32),
            pltpu.VMEM((2 * SUBS * SUBS, LANES), jnp.float32),
        ],
        compiler_params=pltpu.CompilerParams(vmem_limit_bytes=32 << 20),
        name="factor",
    )(kaula_square, *pieces)


def pairs(size, k):
    return [(i, i ^ k) for i in range(size)]


def swap(x, axis, k):
    return lax.ppermute(x, axis, pairs(lax.axis_size(axis), k)) if k else x


def tree_sum(terms):
    while len(terms) > 1:
        terms = [a + b for a, b in zip(terms[::2], terms[1::2])]
    return terms[0]


def body(legendre, lon_center, counts, column_index):
    n, groups = lax.axis_size("ord"), lax.axis_size("grp")
    cols_dev, rows_grp = legendre.shape
    cols = cols_dev * n
    rows_dev = rows_grp // n
    valid_rows = 3 * rows_grp // 4
    per = -(-((valid_rows + (LANES - 1) * n) // LANES) // n)
    late = max(1, per // 5)
    shape = (n, (per - late, late), rows_dev, rows_grp, 1.0 / math.sqrt(rows_grp * groups))
    order = sorted(range(1, n), key=lambda k: (-bin(k >> 1).count("1"), k)) + [0]
    early_parts, late_parts = [None] * n, [None] * n
    for k in order:
        early_parts[k], late_parts[k] = design(shape, k, counts, lon_center, column_index, legendre)
        early_parts[k] = swap(early_parts[k], "ord", k)
    gate = order[1]
    early_parts[gate], late_parts = lax.optimization_barrier((early_parts[gate], late_parts))
    late_parts = [swap(late_parts[k], "ord", k) for k in range(n)]
    before = gram(n, early_parts, [], False)
    pieces = gram(n, late_parts, before, True)
    share = tree_sum([swap(pieces[k], "ord", k) for k in range(n)])
    share = tree_sum([swap(share, "grp", k) for k in range(groups)])
    gathered = [swap(share, "ord", k) for k in range(n)]
    degree = column_index[0:1].astype(jnp.float32)
    kaula_weight = kaula_gain * (degree / NMAX) ** 2
    return factor(n, cols, kaula_weight * kaula_weight, gathered)


def solution(mesh):
    placed = (P("ord", "grp"), P("grp"), P("grp", None), P())
    return jax.shard_map(body, mesh=mesh, in_specs=placed, out_specs=P(), check_vma=False)
```

time: 150 us -> 136 us (0.907)
  waiting for transfers between devices: 57.8 us -> 39.9 us
  Pallas kernels: 52.5 us -> 58.4 us
  local copies, waits for them, and re-layouts: 4.73 us -> 1.13 us
    ppermute x31, waiting for transfers between devices: 57.8 us -> 39.9 us  [swap(): return lax.ppermute(x, axis, pairs(lax.axis_size(axis), k)) if k else x]
    pallas_call x10, Pallas kernels: 34.9 us -> 44.5 us  [the longest x8 38.4 us: design(): pl.pallas_call(functools.partial(design_kernel, shape, k), out_shape=[jax...]
    pallas_call x1, Pallas kernels: 17.5 us -> 13.8 us  [factor(): pl.pallas_call(functools.partial(factor_kernel, n, cols), out_shape=jax.S...]
    unnamed x6 -> x20, local copies, waits for them, and re-layouts: 4.73 us -> 1.13 us
  transfers between devices with their start and end apart: 31 -> 31, of which waited for: 10 -> 9; matrix products, arithmetic and copies ran while one was open for 0% -> 1% of each run, Pallas kernels for 20% -> 28%
where the time goes in v2:
time: 136 us; the launch traced here: 135 us
  Pallas kernels  58.4 us (43%)
  waiting for transfers between devices  39.9 us (29%)
  starting transfers between devices  34.1 us (25%)
    ppermute x31, waiting for transfers between devices, swap(): return lax.ppermute(x, axis, pairs(lax.axis_size(axis), k)) if k else x  39.9 us
    pallas_call x8, Pallas kernels, design(): pl.pallas_call(functools.partial(design_kernel, shape, k), out_shape=[jax...  38.4 us
    ppermute x31, starting transfers between devices, swap(): return lax.ppermute(x, axis, pairs(lax.axis_size(axis), k)) if k else x  34.1 us
    pallas_call x1, Pallas kernels, factor(): pl.pallas_call(functools.partial(factor_kernel, n, cols), out_shape=jax.S...  13.8 us
    pallas_call x2, Pallas kernels, gram(): pl.pallas_call(functools.partial(gram_kernel, n, cols, tile, not before,...  6.09 us
  transfers between devices with their start and end apart: 31, of which 9 were waited for; matrix products, arithmetic and copies ran while one was open for 1% of the time, Pallas kernels for 28%

profile of v2, /device:TPU:0, one launch (start us, length us, event | category | flops | bytes accessed | tf_op | source)
XLA Modules:
  0.0 135.2 jit_solution(561454789352481503)
XLA Ops:
  0.7 4.8 %design.8 = (f32[64,2560]{1,0:T(8,128)}, f32[64,640]{1,0:T(8,128)}) custom-call(s32[1,8]{1,0:T(1,128)} %counts_ref.15, f32[1]{0:T(128)S(6)} %copy.5.lon_ref, s32[3,512]{1,0:T(4,128)} %index_ref.15, f32[64,32768]{1,0:T(8,128)} %leg_ref.15), custom_call_target="tpu_custom_call" | custom-call | flops 1638400 | bytes 1638400 | tf_op jit(solution)/shard_map/jit(design)/design/pallas_call | solution.py:108
  5.5 3.4 %collective-permute-start = (f32[64,2560]{1,0:T(8,128)}, f32[64,2560]{1,0:T(8,128)S(1)}, u32[]{:S(2)}, u32[]{:S(2)}) collective-permute-start(f32[64,2560]{1,0:T(8,128)} %get-tuple-element.38), channel_id=1, source_target_pairs={{0,7},{1,6},{2,5},{3,4},{4,3},{5,2},{6,1},{7,0},{8,15},{9,14},{10,... | collective-permute-start | bytes 1966088 | tf_op jit(solution)/shard_map/ppermute | solution.py:333
  8.9 4.8 %design.12 = (f32[64,2560]{1,0:T(8,128)}, f32[64,640]{1,0:T(8,128)}) custom-call(s32[1,8]{1,0:T(1,128)} %counts_ref.15, f32[1]{0:T(128)S(6)} %copy.5.lon_ref, s32[3,512]{1,0:T(4,128)} %index_ref.15, f32[64,32768]{1,0:T(8,128)} %leg_ref.15), custom_call_target="tpu_custom_call" | custom-call | flops 1638400 | bytes 1638400 | tf_op jit(solution)/shard_map/jit(design)/design/pallas_call | solution.py:108
  14.6 4.8 %design.13 = (f32[64,2560]{1,0:T(8,128)}, f32[64,640]{1,0:T(8,128)}) custom-call(s32[1,8]{1,0:T(1,128)} %counts_ref.15, f32[1]{0:T(128)S(6)} %copy.5.lon_ref, s32[3,512]{1,0:T(4,128)} %index_ref.15, f32[64,32768]{1,0:T(8,128)} %leg_ref.15), custom_call_target="tpu_custom_call" | custom-call | flops 1638400 | bytes 1638400 | tf_op jit(solution)/shard_map/jit(design)/design/pallas_call | solution.py:108
  19.4 4.8 %design.14 = (f32[64,2560]{1,0:T(8,128)}, f32[64,640]{1,0:T(8,128)}) custom-call(s32[1,8]{1,0:T(1,128)} %counts_ref.15, f32[1]{0:T(128)S(6)} %copy.5.lon_ref, s32[3,512]{1,0:T(4,128)} %index_ref.15, f32[64,32768]{1,0:T(8,128)} %leg_ref.15), custom_call_target="tpu_custom_call" | custom-call | flops 1638400 | bytes 1638400 | tf_op jit(solution)/shard_map/jit(design)/design/pallas_call | solution.py:108
  25.5 4.8 %design.15 = (f32[64,2560]{1,0:T(8,128)}, f32[64,640]{1,0:T(8,128)}) custom-call(s32[1,8]{1,0:T(1,128)} %counts_ref.15, f32[1]{0:T(128)S(6)} %copy.5.lon_ref, s32[3,512]{1,0:T(4,128)} %index_ref.15, f32[64,32768]{1,0:T(8,128)} %leg_ref.15), custom_call_target="tpu_custom_call" | custom-call | flops 1638400 | bytes 1638400 | tf_op jit(solution)/shard_map/jit(design)/design/pallas_call | solution.py:108
  30.3 1.8 %collective-permute-start.13 = (f32[64,2560]{1,0:T(8,128)}, f32[64,2560]{1,0:T(8,128)S(1)}, u32[]{:S(2)}, u32[]{:S(2)}) collective-permute-start(f32[64,2560]{1,0:T(8,128)} %get-tuple-element.61), channel_id=1, source_target_pairs={{0,6},{1,7},{2,4},{3,5},{4,2},{5,3},{6,0},{7,1},{8,14},{9,15},{10,... | collective-permute-start | bytes 1966088 | tf_op jit(solution)/shard_map/ppermute | solution.py:333
  32.1 4.8 %design.10 = (f32[64,2560]{1,0:T(8,128)}, f32[64,640]{1,0:T(8,128)}) custom-call(s32[1,8]{1,0:T(1,128)} %counts_ref.15, f32[1]{0:T(128)S(6)} %copy.5.lon_ref, s32[3,512]{1,0:T(4,128)} %index_ref.15, f32[64,32768]{1,0:T(8,128)} %leg_ref.15), custom_call_target="tpu_custom_call" | custom-call | flops 1638400 | bytes 1638400 | tf_op jit(solution)/shard_map/jit(design)/design/pallas_call | solution.py:108
  37.0 4.9 %design.11 = (f32[64,2560]{1,0:T(8,128)}, f32[64,640]{1,0:T(8,128)}) custom-call(s32[1,8]{1,0:T(1,128)} %counts_ref.15, f32[1]{0:T(128)S(6)} %copy.5.lon_ref, s32[3,512]{1,0:T(4,128)} %index_ref.15, f32[64,32768]{1,0:T(8,128)} %leg_ref.15), custom_call_target="tpu_custom_call" | custom-call | flops 1638400 | bytes 1638400 | tf_op jit(solution)/shard_map/jit(design)/design/pallas_call | solution.py:108
  42.7 4.8 %design.9 = (f32[64,2560]{1,0:T(8,128)}, f32[64,640]{1,0:T(8,128)}) custom-call(s32[1,8]{1,0:T(1,128)} %counts_ref.15, f32[1]{0:T(128)S(6)} %copy.5.lon_ref, s32[3,512]{1,0:T(4,128)} %index_ref.15, f32[64,32768]{1,0:T(8,128)} %leg_ref.15), custom_call_target="tpu_custom_call" | custom-call | flops 1638400 | bytes 1638400 | tf_op jit(solution)/shard_map/jit(design)/design/pallas_call | solution.py:108
  47.6 18.8 %collective-permute-done.12.refs_5_ = f32[64,2560]{1,0:T(8,128)S(1)} collective-permute-done((f32[64,2560]{1,0:T(8,128)}, f32[64,2560]{1,0:T(8,128)S(1)}, u32[]{:S(2)}, u32[]{:S(2)}) %collective-permute-start.12) | collective-permute-done | bytes 655392 | tf_op jit(solution)/shard_map/ppermute | solution.py:333
  66.4 2.2 %collective-permute-start.2 = (f32[64,640]{1,0:T(8,128)S(1)}, f32[64,640]{1,0:T(8,128)S(1)}, u32[]{:S(2)}, u32[]{:S(2)}) collective-permute-start(f32[64,640]{1,0:T(8,128)S(1)} %copy-done.8), channel_id=1, source_target_pairs={{0,2},{1,3},{2,0},{3,1},{4,6},{5,7},{6,4},{7,5},{8,10},{9,11},{10,... | collective-permute-start | bytes 491528 | tf_op jit(solution)/shard_map/ppermute | solution.py:333
  70.6 2.6 %collective-permute-start.6 = (f32[64,640]{1,0:T(8,128)S(1)}, f32[64,640]{1,0:T(8,128)S(1)}, u32[]{:S(2)}, u32[]{:S(2)}) collective-permute-start(f32[64,640]{1,0:T(8,128)S(1)} %copy-done.7), channel_id=1, source_target_pairs={{0,6},{1,7},{2,4},{3,5},{4,2},{5,3},{6,0},{7,1},{8,14},{9,15},{10,... | collective-permute-start | bytes 491528 | tf_op jit(solution)/shard_map/ppermute | solution.py:333
  75.8 4.7 %gram.2.refs_8_ = f32[512,512]{1,0:T(8,128)S(1)} custom-call(f32[64,2560]{1,0:T(8,128)S(1)} %copy-done, f32[64,2560]{1,0:T(8,128)S(1)} %collective-permute-done.8.refs_1_, f32[64,2560]{1,0:T(8,128)S(1)} %collective-permute-done.9.refs_2_, f32[64,2560]{1,0:T(8,128)S(1)} %collective-permute-done.10.refs_3_, f32[64,2560]{1,0:T(8,128)S(1)} %collective-permute-done.11.refs_4_, ...), custom_call_target="tpu_custom_call" | custom-call | flops 4026531840 | bytes 5242880 | tf_op jit(solution)/shard_map/gram/pallas_call | solution.py:189
  80.6 4.7 %collective-permute-done.5.refs_5_ = f32[64,640]{1,0:T(8,128)S(1)} collective-permute-done((f32[64,640]{1,0:T(8,128)S(1)}, f32[64,640]{1,0:T(8,128)S(1)}, u32[]{:S(2)}, u32[]{:S(2)}) %collective-permute-start.5) | collective-permute-done | bytes 163872 | tf_op jit(solution)/shard_map/ppermute | solution.py:333
  88.7 1.8 %collective-permute-start.17 = (f32[160,128]{1,0:T(8,128)S(1)}, f32[160,128]{1,0:T(8,128)S(1)}, u32[]{:S(2)}, u32[]{:S(2)}) collective-permute-start(f32[160,128]{1,0:T(8,128)S(1)} %get-tuple-element.67), channel_id=1, source_target_pairs={{0,4},{1,5},{2,6},{3,7},{4,0},{5,1},{6,2},{7,3},{8,12},{9,13},{10,... | collective-permute-start | bytes 245768 | tf_op jit(solution)/shard_map/ppermute | solution.py:333
  90.6 2.6 %collective-permute-start.19 = (f32[160,128]{1,0:T(8,128)S(1)}, f32[160,128]{1,0:T(8,128)S(1)}, u32[]{:S(2)}, u32[]{:S(2)}) collective-permute-start(f32[160,128]{1,0:T(8,128)S(1)} %get-tuple-element.69), channel_id=1, source_target_pairs={{0,6},{1,7},{2,4},{3,5},{4,2},{5,3},{6,0},{7,1},{8,14},{9,15},{10,... | collective-permute-start | bytes 245768 | tf_op jit(solution)/shard_map/ppermute | solution.py:333
  93.6 4.5 %collective-permute-done.18 = f32[160,128]{1,0:T(8,128)S(1)} collective-permute-done((f32[160,128]{1,0:T(8,128)S(1)}, f32[160,128]{1,0:T(8,128)S(1)}, u32[]{:S(2)}, u32[]{:S(2)}) %collective-permute-start.18) | collective-permute-done | bytes 81952 | tf_op jit(solution)/shard_map/ppermute | solution.py:333
  98.6 1.8 %collective-permute-start.21 = (f32[160,128]{1,0:T(8,128)S(1)}, f32[160,128]{1,0:T(8,128)S(1)}, u32[]{:S(2)}, u32[]{:S(2)}) collective-permute-start(f32[160,128]{1,0:T(8,128)S(1)} %add_add_fusion.1), channel_id=1, source_target_pairs={{0,8},{8,0},{16,24},{24,16},{1,9},{9,1},{17,25},{25,17},{2,10},{10... | collective-permute-start | bytes 245768 | tf_op jit(solution)/shard_map/ppermute | solution.py:333
  100.4 2.6 %collective-permute-start.22 = (f32[160,128]{1,0:T(8,128)S(1)}, f32[160,128]{1,0:T(8,128)S(1)}, u32[]{:S(2)}, u32[]{:S(2)}) collective-permute-start(f32[160,128]{1,0:T(8,128)S(1)} %add_add_fusion.1), channel_id=1, source_target_pairs={{0,16},{8,24},{16,0},{24,8},{1,17},{9,25},{17,1},{25,9},{2,18},{10... | collective-permute-start | bytes 245768 | tf_op jit(solution)/shard_map/ppermute | solution.py:333
  103.2 6.7 %collective-permute-done.22 = f32[160,128]{1,0:T(8,128)S(1)} collective-permute-done((f32[160,128]{1,0:T(8,128)S(1)}, f32[160,128]{1,0:T(8,128)S(1)}, u32[]{:S(2)}, u32[]{:S(2)}) %collective-permute-start.22) | collective-permute-done | bytes 81952 | tf_op jit(solution)/shard_map/ppermute | solution.py:333
  113.5 2.4 %collective-permute-start.29 = (f32[160,128]{1,0:T(8,128)S(1)}, f32[160,128]{1,0:T(8,128)S(1)}, u32[]{:S(2)}, u32[]{:S(2)}) collective-permute-start(f32[160,128]{1,0:T(8,128)S(1)} %add_add_fusion.refs_0_), channel_id=1, source_target_pairs={{0,6},{1,7},{2,4},{3,5},{4,2},{5,3},{6,0},{7,1},{8,14},{9,15},{10,... | collective-permute-start | bytes 245768 | tf_op jit(solution)/shard_map/ppermute | solution.py:333
  117.2 3.5 %collective-permute-done.28.refs_5_ = f32[160,128]{1,0:T(8,128)S(1)} collective-permute-done((f32[160,128]{1,0:T(8,128)S(1)}, f32[160,128]{1,0:T(8,128)S(1)}, u32[]{:S(2)}, u32[]{:S(2)}) %collective-permute-start.28) | collective-permute-done | bytes 81952 | tf_op jit(solution)/shard_map/ppermute | solution.py:333
  121.3 13.8 %factor.1 = f32[512,512]{1,0:T(8,128)} custom-call(f32[1,512]{1,0:T(1,128)S(1)} %multiply_multiply_fusion.kaula_ref, f32[160,128]{1,0:T(8,128)S(1)} %add_add_fusion.refs_0_, f32[160,128]{1,0:T(8,128)S(1)} %collective-permute-done.24.refs_1_, f32[160,128]{1,0:T(8,128)S(1)} %collective-permute-done.25.refs_2_, f32[160,128]{1,0:T(8,128)S(1)} %collective-permute-done.26.refs_3_, ...), custom_call_target="tpu_custom_call" | custom-call | tf_op jit(solution)/shard_map/factor/pallas_call | solution.py:312
  (72 shorter events, 17.9 us)
Async XLA Ops:
  5.5 36.5 %collective-permute-start = (f32[64,2560]{1,0:T(8,128)}, f32[64,2560]{1,0:T(8,128)S(1)}, u32[]{:S(2)}, u32[]{:S(2)}) collective-permute-start(f32[64,2560]{1,0:T(8,128)} %get-tuple-element.38), channel_id=1, source_target_pairs={{0,7},{1,6},{2,5},{3,4},{4,3},{5,2},{6,1},{7,0},{8,15},{9,14},{10,... | collective-permute-start | bytes 1966088 | tf_op jit(solution)/shard_map/ppermute | solution.py:333
  13.7 28.6 %collective-permute-start.10 = (f32[64,2560]{1,0:T(8,128)}, f32[64,2560]{1,0:T(8,128)S(1)}, u32[]{:S(2)}, u32[]{:S(2)}) collective-permute-start(f32[64,2560]{1,0:T(8,128)} %get-tuple-element.58), channel_id=1, source_target_pairs={{0,3},{1,2},{2,1},{3,0},{4,7},{5,6},{6,5},{7,4},{8,11},{9,10},{10,... | collective-permute-start | bytes 1966088 | tf_op jit(solution)/shard_map/ppermute | solution.py:333
  19.4 28.1 %collective-permute-start.11 = (f32[64,2560]{1,0:T(8,128)}, f32[64,2560]{1,0:T(8,128)S(1)}, u32[]{:S(2)}, u32[]{:S(2)}) collective-permute-start(f32[64,2560]{1,0:T(8,128)} %get-tuple-element.59), channel_id=1, source_target_pairs={{0,4},{1,5},{2,6},{3,7},{4,0},{5,1},{6,2},{7,3},{8,12},{9,13},{10,... | collective-permute-start | bytes 1966088 | tf_op jit(solution)/shard_map/ppermute | solution.py:333
  24.2 42.2 %collective-permute-start.12 = (f32[64,2560]{1,0:T(8,128)}, f32[64,2560]{1,0:T(8,128)S(1)}, u32[]{:S(2)}, u32[]{:S(2)}) collective-permute-start(f32[64,2560]{1,0:T(8,128)} %get-tuple-element.60), channel_id=1, source_target_pairs={{0,5},{1,4},{2,7},{3,6},{4,1},{5,0},{6,3},{7,2},{8,13},{9,12},{10,... | collective-permute-start | bytes 1966088 | tf_op jit(solution)/shard_map/ppermute | solution.py:333
  30.3 38.3 %collective-permute-start.13 = (f32[64,2560]{1,0:T(8,128)}, f32[64,2560]{1,0:T(8,128)S(1)}, u32[]{:S(2)}, u32[]{:S(2)}) collective-permute-start(f32[64,2560]{1,0:T(8,128)} %get-tuple-element.61), channel_id=1, source_target_pairs={{0,6},{1,7},{2,4},{3,5},{4,2},{5,3},{6,0},{7,1},{8,14},{9,15},{10,... | collective-permute-start | bytes 1966088 | tf_op jit(solution)/shard_map/ppermute | solution.py:333
  41.9 26.7 %collective-permute-start.8 = (f32[64,2560]{1,0:T(8,128)S(1)}, f32[64,2560]{1,0:T(8,128)S(1)}, u32[]{:S(2)}, u32[]{:S(2)}) collective-permute-start(f32[64,2560]{1,0:T(8,128)S(1)} %copy-done.2), channel_id=1, source_target_pairs={{0,1},{1,0},{2,3},{3,2},{4,5},{5,4},{6,7},{7,6},{8,9},{9,8},{10,11... | collective-permute-start | bytes 1966088 | tf_op jit(solution)/shard_map/ppermute | solution.py:333
  42.3 27.9 %collective-permute-start.9 = (f32[64,2560]{1,0:T(8,128)}, f32[64,2560]{1,0:T(8,128)S(1)}, u32[]{:S(2)}, u32[]{:S(2)}) collective-permute-start(f32[64,2560]{1,0:T(8,128)} %get-tuple-element.57), channel_id=1, source_target_pairs={{0,2},{1,3},{2,0},{3,1},{4,6},{5,7},{6,4},{7,5},{8,10},{9,11},{10,... | collective-permute-start | bytes 1966088 | tf_op jit(solution)/shard_map/ppermute | solution.py:333
  47.5 23.1 %collective-permute-start.1 = (f32[64,640]{1,0:T(8,128)S(1)}, f32[64,640]{1,0:T(8,128)S(1)}, u32[]{:S(2)}, u32[]{:S(2)}) collective-permute-start(f32[64,640]{1,0:T(8,128)S(1)} %copy-done.9), channel_id=1, source_target_pairs={{0,1},{1,0},{2,3},{3,2},{4,5},{5,4},{6,7},{7,6},{8,9},{9,8},{10,11... | collective-permute-start | bytes 491528 | tf_op jit(solution)/shard_map/ppermute | solution.py:333
  66.4 7.2 %collective-permute-start.2 = (f32[64,640]{1,0:T(8,128)S(1)}, f32[64,640]{1,0:T(8,128)S(1)}, u32[]{:S(2)}, u32[]{:S(2)}) collective-permute-start(f32[64,640]{1,0:T(8,128)S(1)} %copy-done.8), channel_id=1, source_target_pairs={{0,2},{1,3},{2,0},{3,1},{4,6},{5,7},{6,4},{7,5},{8,10},{9,11},{10,... | collective-permute-start | bytes 491528 | tf_op jit(solution)/shard_map/ppermute | solution.py:333
  68.6 11.9 %collective-permute-start.3 = (f32[64,640]{1,0:T(8,128)S(1)}, f32[64,640]{1,0:T(8,128)S(1)}, u32[]{:S(2)}, u32[]{:S(2)}) collective-permute-start(f32[64,640]{1,0:T(8,128)S(1)} %copy-done.4), channel_id=1, source_target_pairs={{0,3},{1,2},{2,1},{3,0},{4,7},{5,6},{6,5},{7,4},{8,11},{9,10},{10,... | collective-permute-start | bytes 491528 | tf_op jit(solution)/shard_map/ppermute | solution.py:333
  68.7 11.9 %collective-permute-start.4 = (f32[64,640]{1,0:T(8,128)S(1)}, f32[64,640]{1,0:T(8,128)S(1)}, u32[]{:S(2)}, u32[]{:S(2)}) collective-permute-start(f32[64,640]{1,0:T(8,128)S(1)} %copy-done.5), channel_id=1, source_target_pairs={{0,4},{1,5},{2,6},{3,7},{4,0},{5,1},{6,2},{7,3},{8,12},{9,13},{10,... | collective-permute-start | bytes 491528 | tf_op jit(solution)/shard_map/ppermute | solution.py:333
  70.3 15.0 %collective-permute-start.5 = (f32[64,640]{1,0:T(8,128)S(1)}, f32[64,640]{1,0:T(8,128)S(1)}, u32[]{:S(2)}, u32[]{:S(2)}) collective-permute-start(f32[64,640]{1,0:T(8,128)S(1)} %copy-done.6), channel_id=1, source_target_pairs={{0,5},{1,4},{2,7},{3,6},{4,1},{5,0},{6,3},{7,2},{8,13},{9,12},{10,... | collective-permute-start | bytes 491528 | tf_op jit(solution)/shard_map/ppermute | solution.py:333
  70.6 14.7 %collective-permute-start.6 = (f32[64,640]{1,0:T(8,128)S(1)}, f32[64,640]{1,0:T(8,128)S(1)}, u32[]{:S(2)}, u32[]{:S(2)}) collective-permute-start(f32[64,640]{1,0:T(8,128)S(1)} %copy-done.7), channel_id=1, source_target_pairs={{0,6},{1,7},{2,4},{3,5},{4,2},{5,3},{6,0},{7,1},{8,14},{9,15},{10,... | collective-permute-start | bytes 491528 | tf_op jit(solution)/shard_map/ppermute | solution.py:333
  73.6 11.6 %collective-permute-start.7 = (f32[64,640]{1,0:T(8,128)S(1)}, f32[64,640]{1,0:T(8,128)S(1)}, u32[]{:S(2)}, u32[]{:S(2)}) collective-permute-start(f32[64,640]{1,0:T(8,128)S(1)} %copy-done.3), channel_id=1, source_target_pairs={{0,7},{1,6},{2,5},{3,4},{4,3},{5,2},{6,1},{7,0},{8,15},{9,14},{10,... | collective-permute-start | bytes 491528 | tf_op jit(solution)/shard_map/ppermute | solution.py:333
  87.0 6.2 %collective-permute-start.15 = (f32[160,128]{1,0:T(8,128)S(1)}, f32[160,128]{1,0:T(8,128)S(1)}, u32[]{:S(2)}, u32[]{:S(2)}) collective-permute-start(f32[160,128]{1,0:T(8,128)S(1)} %get-tuple-element.65), channel_id=1, source_target_pairs={{0,2},{1,3},{2,0},{3,1},{4,6},{5,7},{6,4},{7,5},{8,10},{9,11},{10,... | collective-permute-start | bytes 245768 | tf_op jit(solution)/shard_map/ppermute | solution.py:333
  90.6 7.6 %collective-permute-start.18 = (f32[160,128]{1,0:T(8,128)S(1)}, f32[160,128]{1,0:T(8,128)S(1)}, u32[]{:S(2)}, u32[]{:S(2)}) collective-permute-start(f32[160,128]{1,0:T(8,128)S(1)} %get-tuple-element.68), channel_id=1, source_target_pairs={{0,5},{1,4},{2,7},{3,6},{4,1},{5,0},{6,3},{7,2},{8,13},{9,12},{10,... | collective-permute-start | bytes 245768 | tf_op jit(solution)/shard_map/ppermute | solution.py:333
  90.6 7.5 %collective-permute-start.19 = (f32[160,128]{1,0:T(8,128)S(1)}, f32[160,128]{1,0:T(8,128)S(1)}, u32[]{:S(2)}, u32[]{:S(2)}) collective-permute-start(f32[160,128]{1,0:T(8,128)S(1)} %get-tuple-element.69), channel_id=1, source_target_pairs={{0,6},{1,7},{2,4},{3,5},{4,2},{5,3},{6,0},{7,1},{8,14},{9,15},{10,... | collective-permute-start | bytes 245768 | tf_op jit(solution)/shard_map/ppermute | solution.py:333
  93.2 5.4 %collective-permute-start.20 = (f32[160,128]{1,0:T(8,128)S(1)}, f32[160,128]{1,0:T(8,128)S(1)}, u32[]{:S(2)}, u32[]{:S(2)}) collective-permute-start(f32[160,128]{1,0:T(8,128)S(1)} %get-tuple-element.70), channel_id=1, source_target_pairs={{0,7},{1,6},{2,5},{3,4},{4,3},{5,2},{6,1},{7,0},{8,15},{9,14},{10,... | collective-permute-start | bytes 245768 | tf_op jit(solution)/shard_map/ppermute | solution.py:333
  100.4 9.4 %collective-permute-start.22 = (f32[160,128]{1,0:T(8,128)S(1)}, f32[160,128]{1,0:T(8,128)S(1)}, u32[]{:S(2)}, u32[]{:S(2)}) collective-permute-start(f32[160,128]{1,0:T(8,128)S(1)} %add_add_fusion.1), channel_id=1, source_target_pairs={{0,16},{8,24},{16,0},{24,8},{1,17},{9,25},{17,1},{25,9},{2,18},{10... | collective-permute-start | bytes 245768 | tf_op jit(solution)/shard_map/ppermute | solution.py:333
  103.0 6.9 %collective-permute-start.23 = (f32[160,128]{1,0:T(8,128)S(1)}, f32[160,128]{1,0:T(8,128)S(1)}, u32[]{:S(2)}, u32[]{:S(2)}) collective-permute-start(f32[160,128]{1,0:T(8,128)S(1)} %add_add_fusion.1), channel_id=1, source_target_pairs={{0,24},{8,16},{16,8},{24,0},{1,25},{9,17},{17,9},{25,1},{2,26},{10... | collective-permute-start | bytes 245768 | tf_op jit(solution)/shard_map/ppermute | solution.py:333
  110.0 6.0 %collective-permute-start.25 = (f32[160,128]{1,0:T(8,128)S(1)}, f32[160,128]{1,0:T(8,128)S(1)}, u32[]{:S(2)}, u32[]{:S(2)}) collective-permute-start(f32[160,128]{1,0:T(8,128)S(1)} %add_add_fusion.refs_0_), channel_id=1, source_target_pairs={{0,2},{1,3},{2,0},{3,1},{4,6},{5,7},{6,4},{7,5},{8,10},{9,11},{10,... | collective-permute-start | bytes 245768 | tf_op jit(solution)/shard_map/ppermute | solution.py:333
  111.6 5.6 %collective-permute-start.26 = (f32[160,128]{1,0:T(8,128)S(1)}, f32[160,128]{1,0:T(8,128)S(1)}, u32[]{:S(2)}, u32[]{:S(2)}) collective-permute-start(f32[160,128]{1,0:T(8,128)S(1)} %add_add_fusion.refs_0_), channel_id=1, source_target_pairs={{0,3},{1,2},{2,1},{3,0},{4,7},{5,6},{6,5},{7,4},{8,11},{9,10},{10,... | collective-permute-start | bytes 245768 | tf_op jit(solution)/shard_map/ppermute | solution.py:333
  113.2 7.5 %collective-permute-start.28 = (f32[160,128]{1,0:T(8,128)S(1)}, f32[160,128]{1,0:T(8,128)S(1)}, u32[]{:S(2)}, u32[]{:S(2)}) collective-permute-start(f32[160,128]{1,0:T(8,128)S(1)} %add_add_fusion.refs_0_), channel_id=1, source_target_pairs={{0,5},{1,4},{2,7},{3,6},{4,1},{5,0},{6,3},{7,2},{8,13},{9,12},{10,... | collective-permute-start | bytes 245768 | tf_op jit(solution)/shard_map/ppermute | solution.py:333
  113.5 7.2 %collective-permute-start.29 = (f32[160,128]{1,0:T(8,128)S(1)}, f32[160,128]{1,0:T(8,128)S(1)}, u32[]{:S(2)}, u32[]{:S(2)}) collective-permute-start(f32[160,128]{1,0:T(8,128)S(1)} %add_add_fusion.refs_0_), channel_id=1, source_target_pairs={{0,6},{1,7},{2,4},{3,5},{4,2},{5,3},{6,0},{7,1},{8,14},{9,15},{10,... | collective-permute-start | bytes 245768 | tf_op jit(solution)/shard_map/ppermute | solution.py:333
  (17 other events, 250.3 us)

commit v3 on v2

--- a/solution.py
+++ b/solution.py
@@ -37,92 +37,194 @@
     return series((12, 10, 8, 6, 4, 2, 0)) * sign, series((13, 11, 9, 7, 5, 3, 1)) * rest * sign
 
 
-def design_kernel(shape, k, counts_ref, lon_ref, index_ref, leg_ref, *refs):
-    n, sizes, rows_dev, rows_grp, scaling = shape
-    outs, (held, sems) = refs[:-2], refs[-2:]
-    per = sum(sizes)
-    blocks_dev = rows_dev // LANES
+class Blocks:
+    def __init__(self, shape, counts_ref):
+        self.n, self.per, self.rows_dev = shape[:3]
+        self.ends, self.rest, self.rest_starts, self.rest_places = [], [], [], []
+        total, rest_total = 0, 0
+        for r in range(self.n):
+            count = counts_ref[0, r]
+            full = lax.div(count, LANES)
+            total = total + full
+            self.ends.append(total)
+            self.rest.append(count - full * LANES)
+            self.rest_starts.append(rest_total)
+            self.rest_places.append(r * self.rows_dev + jnp.minimum(full * LANES, self.rows_dev - LANES))
+            rest_total = rest_total + self.rest[r]
+        self.packed = lax.div(rest_total, LANES)
+
+    def first(self, dest):
+        return dest * self.per - jnp.minimum(dest, self.packed)
+
+    def place(self, want):
+        slot, begin = 0, 0
+        for r in range(self.n - 1):
+            past = want >= self.ends[r]
+            slot = jnp.where(past, r + 1, slot)
+            begin = jnp.where(past, self.ends[r], begin)
+        return slot * self.rows_dev + jnp.minimum((want - begin) * LANES, self.rows_dev - LANES)
+
+
+def over(count, n, step):
+    def run(i, _):
+        step(i)
+        return 0
+
+    lax.fori_loop(0, count, run, 0, unroll=count if n <= 8 else 1)
+
+
+def pick_kernel(shape, k, size, counts_ref, leg_ref, out_ref, sems):
+    blocks = Blocks(shape, counts_ref)
+    dest = lax.axis_index("ord") ^ k
+
+    def copy(i, start):
+        here = pl.ds(pl.multiple_of(i * LANES, LANES), LANES)
+        return pltpu.make_async_copy(leg_ref.at[:, pl.ds(start, LANES)], out_ref.at[:, here], sems.at[i])
+
+    def send(i):
+        copy(i, pl.multiple_of(blocks.place(blocks.first(dest) + i), LANES)).start()
+
+    def wait(i):
+        copy(i, 0).wait()
+
+    over(size, blocks.n, send)
+    over(size, blocks.n, wait)
+
+
+@functools.partial(jax.jit, static_argnums=(0, 1, 2))
+def pick(shape, k, size, counts, legendre):
+    rows = legendre.shape[0]
+    elements = rows * size * LANES
+    return pl.pallas_call(
+        functools.partial(pick_kernel, shape, k, size),
+        out_shape=jax.ShapeDtypeStruct((rows, size * LANES), jnp.float32),
+        in_specs=[pl.BlockSpec(memory_space=SMEM), pl.BlockSpec(memory_space=pltpu.HBM)],
+        out_specs=pl.BlockSpec(memory_space=VMEM),
+        scratch_shapes=[pltpu.SemaphoreType.DMA((size,))],
+        compiler_params=pltpu.CompilerParams(vmem_limit_bytes=56 << 20),
+        cost_estimate=pl.CostEstimate(flops=8 * elements, bytes_accessed=8 * elements, transcendentals=0),
+        name="pick",
+    )(counts, legendre)
+
+
+def inner_tables(shape, harmonic, tops):
+    along = lax.broadcasted_iota(jnp.int32, (SUBS, LANES), 1).astype(jnp.float32) * (track_span / shape[3])
+    pairs_of = [wave_pair(harmonic[top : top + SUBS] * along) for top in tops]
+    return [(c * shape[4], s * shape[4]) for c, s in pairs_of]
+
+
+def outer_tables(shape, lon, begin, harmonic, phase, tops):
+    longitude = lon + begin.astype(jnp.float32) * (track_span / shape[3])
+    return [wave_pair(harmonic[top : top + SUBS] * longitude - phase[top : top + SUBS]) for top in tops]
+
+
+def wave(outer, inner, i):
+    return lane_wide(outer[0], i) * inner[0] - lane_wide(outer[1], i) * inner[1]
+
+
+def wide_columns(columns):
+    rows = columns.shape[0]
+    harmonic = jnp.broadcast_to(columns[:, 0:1], (rows, LANES))
+    return harmonic, jnp.broadcast_to(columns[:, 1:2] * quarter_turn, (rows, LANES))
+
+
+def design_kernel(shape, ks, first, size, counts_ref, lon_ref, cols_ref, leg_ref, *refs):
+    blocks = Blocks(shape, counts_ref)
+    n, last = blocks.n, first + size == blocks.per
+    outs, (held, left, table, sems, left_sems) = refs[: len(ks)], refs[len(ks) :]
     me = lax.axis_index("ord")
-    count = [counts_ref[0, r] for r in range(n)]
-    ends, total = [], 0
+
+    def origin(k):
+        return blocks.first(me ^ k) + first
+
+    def copy(spot, start):
+        here = pl.ds(pl.multiple_of(spot * LANES, LANES), LANES)
+        return pltpu.make_async_copy(leg_ref.at[:, pl.ds(start, LANES)], held.at[:, here], sems.at[spot])
+
+    def copy_rest(r, start):
+        here = pl.ds(r * LANES, LANES)
+        return pltpu.make_async_copy(leg_ref.at[:, pl.ds(start, LANES)], left.at[:, here], left_sems.at[r])
+
+    def send(i):
+        for q, k in enumerate(ks):
+            copy(q * size + i, pl.multiple_of(blocks.place(origin(k) + i), LANES)).start()
+
+    over(size, n, send)
+    for r in range(n if last else 0):
+        copy_rest(r, pl.multiple_of(blocks.rest_places[r], LANES)).start()
+        table[0, r] = blocks.rest[r]
+        table[1, r] = blocks.rest_starts[r]
+    rows = held.shape[0]
+    tops = range(0, rows, SUBS)
+    lane = lax.broadcasted_iota(jnp.int32, (SUBS, LANES), 1)
+    harmonic, phase = wide_columns(cols_ref[...])
+    inner = inner_tables(shape, harmonic, tops)
+    begin = jnp.zeros_like(lane)
     for r in range(n):
-        total = total + lax.div(count[r] + (LANES - 1), LANES)
-        ends.append(total)
-
-    def place(want):
-        slot, begin, held_rows = 0, 0, count[0]
-        for r in range(n - 1):
-            past = want >= ends[r]
-            slot = jnp.where(past, r + 1, slot)
-            begin = jnp.where(past, ends[r], begin)
-            held_rows = jnp.where(past, count[r + 1], held_rows)
-        inside = jnp.minimum(want - begin, blocks_dev - 1)
-        valid = jnp.where(want < total, held_rows - (want - begin) * LANES, 0)
-        return slot * rows_dev + inside * LANES, valid
-
-    def copy(i, start):
-        return pltpu.make_async_copy(
-            leg_ref.at[:, pl.ds(start, LANES)], held.at[:, pl.ds(i * LANES, LANES)], sems.at[i]
-        )
-
-    valids = []
-    for i in range(per):
-        start, valid = place((me ^ k) * per + i)
-        copy(i, pl.multiple_of(start, LANES)).start()
-        valids.append(valid)
-    rows = held.shape[0]
-    wide = (rows, index_ref.shape[1])
-    mine = lax.broadcasted_iota(jnp.int32, wide, 1) == lax.broadcasted_iota(jnp.int32, wide, 0) + me * rows
-
-    def column(row):
-        values = jnp.broadcast_to(index_ref[row : row + 1, :].astype(jnp.float32), wide)
-        picked = jnp.sum(jnp.where(mine, values, 0.0), axis=1, keepdims=True)
-        return jnp.broadcast_to(picked, (rows, LANES))
-
-    harmonic = column(1)
-    phase = column(2) * quarter_turn
-    lane = lax.broadcasted_iota(jnp.int32, (SUBS, LANES), 1)
-    pace = track_span / rows_grp
-    along = lane.astype(jnp.float32) * pace
-    tops = range(0, rows, SUBS)
-    inner = [wave_pair(harmonic[top : top + SUBS] * along) for top in tops]
-    begin = place((me ^ k) * per + lane)[0].astype(jnp.float32)
-    longitude = lon_ref[0] + begin * pace
-    outer = [
-        wave_pair(harmonic[top : top + SUBS] * longitude - phase[top : top + SUBS]) for top in tops
-    ]
-    spots = [(out, i) for out, size in zip(outs, sizes) for i in range(size)]
-    for i, (out, spot) in enumerate(spots):
-        copy(i, 0).wait()
-        gate = jnp.where(lane < valids[i], scaling, 0.0)
+        begin = jnp.where(lane == r, blocks.rest_places[r], begin)
+    outer = outer_tables(shape, lon_ref[0], begin, harmonic, phase, tops) if last else None
+    for r in range(n if last else 0):
+        copy_rest(r, 0).wait()
         for t, top in enumerate(tops):
-            wave = lane_wide(outer[t][0], i) * inner[t][0] - lane_wide(outer[t][1], i) * inner[t][1]
-            tile = held[pl.ds(top, SUBS), pl.ds(i * LANES, LANES)]
-            out[pl.ds(top, SUBS), pl.ds(spot * LANES, LANES)] = tile * wave * gate
-
-
-@functools.partial(jax.jit, static_argnums=(0, 1))
-def design(shape, k, counts, lon_center, column_index, legendre):
-    sizes, rows = shape[1], legendre.shape[0]
-    elements = rows * sum(sizes) * LANES
+            at = (pl.ds(top, SUBS), pl.ds(r * LANES, LANES))
+            left[at] = jnp.where(lane < blocks.rest[r], left[at] * wave(outer[t], inner[t], r), 0.0)
+    whole_lane = lax.broadcasted_iota(jnp.int32, (rows, LANES), 1)
+    for q, k in enumerate(ks):
+        outer = outer_tables(shape, lon_ref[0], blocks.place(origin(k) + lane), harmonic, phase, tops)
+        for i in range(size):
+            copy(q * size + i, 0).wait()
+            for t, top in enumerate(tops):
+                tile = held[pl.ds(top, SUBS), pl.ds((q * size + i) * LANES, LANES)]
+                outs[q][pl.ds(top, SUBS), pl.ds(i * LANES, LANES)] = tile * wave(outer[t], inner[t], i)
+        if not last:
+            continue
+
+        @pl.when((me ^ k) < blocks.packed)
+        def _(q=q, k=k):
+            here = pl.ds((size - 1) * LANES, LANES)
+            outs[q][:, here] = jnp.zeros((rows, LANES), jnp.float32)
+
+            def add(r, _):
+                many = table[0, r]
+                shift = table[1, r] - (me ^ k) * LANES
+
+                @pl.when((shift < LANES) & (shift + many > 0))
+                def _():
+                    spot = whole_lane - shift
+                    tile = left[:, pl.ds(pl.multiple_of(r * LANES, LANES), LANES)]
+                    rolled = pltpu.roll(tile, lax.rem(shift + LANES, LANES), 1)
+                    outs[q][:, here] += jnp.where((spot >= 0) & (spot < many), rolled, 0.0)
+
+                return 0
+
+            lax.fori_loop(0, n, add, 0)
+
+
+@functools.partial(jax.jit, static_argnums=(0, 1, 2, 3))
+def design(shape, ks, first, size, counts, lon_center, own, legendre):
+    n, rows, many = shape[0], legendre.shape[0], len(ks) * size
+    elements = rows * many * LANES
     return pl.pallas_call(
-        functools.partial(design_kernel, shape, k),
-        out_shape=[jax.ShapeDtypeStruct((rows, size * LANES), jnp.float32) for size in sizes],
+        functools.partial(design_kernel, shape, ks, first, size),
+        out_shape=[jax.ShapeDtypeStruct((rows, size * LANES), jnp.float32)] * len(ks),
         in_specs=[
             pl.BlockSpec(memory_space=SMEM),
             pl.BlockSpec(memory_space=SMEM),
             pl.BlockSpec(memory_space=VMEM),
             pl.BlockSpec(memory_space=pltpu.HBM),
         ],
-        out_specs=[pl.BlockSpec(memory_space=VMEM)] * len(sizes),
+        out_specs=[pl.BlockSpec(memory_space=VMEM)] * len(ks),
         scratch_shapes=[
-            pltpu.VMEM((rows, sum(sizes) * LANES), jnp.float32),
-            pltpu.SemaphoreType.DMA((sum(sizes),)),
+            pltpu.VMEM((rows, many * LANES), jnp.float32),
+            pltpu.VMEM((rows, n * LANES), jnp.float32),
+            pltpu.SMEM((2, n), jnp.int32),
+            pltpu.SemaphoreType.DMA((many,)),
+            pltpu.SemaphoreType.DMA((n,)),
         ],
         compiler_params=pltpu.CompilerParams(vmem_limit_bytes=56 << 20),
         cost_estimate=pl.CostEstimate(flops=8 * elements, bytes_accessed=8 * elements, transcendentals=0),
         name="design",
-    )(counts, lon_center, column_index, legendre)
+    )(counts, lon_center, own, legendre)
 
 
 def lane_wide(x, j):
@@ -134,14 +236,7 @@
     return [(i, j) for i in range(nb) for j in range(i, nb)]
 
 
-def gram_kernel(n, cols, tile, first, last, *refs):
-    ins, refs = refs[:n], refs[n:]
-    before = None
-    if not first:
-        before, refs = refs[0], refs[1:]
-    outs, scratch = refs[: n if last else 1], refs[n if last else 1 :]
-    high, low = scratch[:2]
-    acc = scratch[2] if last else outs[0]
+def gram_terms(n, cols, tile, ins, high, low, value, add):
     me = lax.axis_index("ord")
     each, rows = ins[0].shape
 
@@ -151,53 +246,121 @@
     tall = min(256, cols)
     for s in range(rows // tile):
         for k in range(n):
-            part = ins[k][:, pl.ds(s * tile, tile)]
-            at = pl.ds(pl.multiple_of((me ^ k) * each, each), each)
-            top = part.astype(jnp.bfloat16)
-            high[s % 2, at, :] = top
-            low[s % 2, at, :] = (part - top.astype(jnp.float32)).astype(jnp.bfloat16)
+            begin = pl.multiple_of((me ^ k) * each, each)
+            value(k, s, begin, ins[k], high.at[s % 2], low.at[s % 2])
         for i in range(0, cols, tall):
             hi, lo = high[s % 2, pl.ds(i, tall), :], low[s % 2, pl.ds(i, tall), :]
             his, los = high[s % 2, pl.ds(i, cols - i), :], low[s % 2, pl.ds(i, cols - i), :]
-            at = (pl.ds(i, tall), pl.ds(i, cols - i))
-            here = times(hi, his) + (times(hi, los) + times(lo, his))
-            if s:
-                acc[at] += here
-            else:
-                acc[at] = here if first else before[at] + here
-
-    if last:
-        packed = scratch[3]
-        for t, (i, j) in enumerate(upper_blocks(cols)):
-            packed[pl.ds(t * LANES, LANES), :] = acc[pl.ds(i * LANES, LANES), pl.ds(j * LANES, LANES)]
-        piece = packed.shape[0] // n
-        for k in range(n):
-            outs[k][...] = packed[pl.ds(pl.multiple_of((me ^ k) * piece, SUBS), piece), :]
-
-
-def gram(n, parts, before, last):
+            add(s, (pl.ds(i, tall), pl.ds(i, cols - i)), times(hi, his) + (times(hi, los) + times(lo, his)))
+
+
+def split(x):
+    top = x.astype(jnp.bfloat16)
+    return top, (x - top.astype(jnp.float32)).astype(jnp.bfloat16)
+
+
+def early_kernel(shape, cols, tile, raw, counts_ref, lon_ref, cols_ref, *refs):
+    n = shape[0]
+    ins, (acc, high, low, inner_ref, outer_ref) = refs[:n], refs[n:]
+    blocks = Blocks(shape, counts_ref)
+    me = lax.axis_index("ord")
+    each = cols // n
+    tops = range(0, each, SUBS)
+    lane = lax.broadcasted_iota(jnp.int32, (SUBS, LANES), 1)
+    begins = blocks.place(blocks.first(me) + lane)
+    for q, k in enumerate(raw):
+        harmonic, phase = wide_columns(cols_ref[pl.ds(pl.multiple_of((me ^ k) * each, each), each), :])
+        inner = inner_tables(shape, harmonic, tops)
+        outer = outer_tables(shape, lon_ref[0], begins, harmonic, phase, tops)
+        for t, top in enumerate(tops):
+            for half in range(2):
+                inner_ref[half, pl.ds(q * each + top, SUBS), :] = inner[t][half]
+                outer_ref[half, pl.ds(q * each + top, SUBS), :] = outer[t][half]
+    step = 2 * SUBS
+
+    def value(k, s, begin, part, high_ref, low_ref):
+        if k not in raw:
+            at = pl.ds(begin, each)
+            high_ref[at, :], low_ref[at, :] = split(part[:, pl.ds(s * tile, tile)])
+            return
+        for top in range(0, each, step):
+            there = pl.ds(raw.index(k) * each + top, step)
+            inside = [inner_ref[half, there, :] for half in range(2)]
+            outside = [outer_ref[half, there, :] for half in range(2)]
+            for i in range(tile // LANES):
+                b = s * (tile // LANES) + i
+                c, d = (jnp.broadcast_to(x[:, b : b + 1], (step, LANES)) for x in outside)
+                x = part[pl.ds(top, step), pl.ds(b * LANES, LANES)] * (c * inside[0] - d * inside[1])
+                here = (pl.ds(pl.multiple_of(begin + top, step), step), pl.ds(i * LANES, LANES))
+                high_ref[here], low_ref[here] = split(x)
+
+    def add(s, at, block):
+        acc[at] = acc[at] + block if s else block
+
+    gram_terms(n, cols, tile, ins, high, low, value, add)
+
+
+def late_kernel(n, cols, tile, *refs):
+    ins, (before, keep, give, high, low, acc, packed) = refs[:n], refs[n:]
+    me = lax.axis_index("ord")
+    each = cols // n
+
+    def value(k, s, begin, part, high_ref, low_ref):
+        at = pl.ds(begin, each)
+        high_ref[at, :], low_ref[at, :] = split(part[:, pl.ds(s * tile, tile)])
+
+    def add(s, at, block):
+        acc[at] = (acc[at] if s else before[at]) + block
+
+    gram_terms(n, cols, tile, ins, high, low, value, add)
+    for t, (i, j) in enumerate(upper_blocks(cols)):
+        packed[pl.ds(t * LANES, LANES), :] = acc[pl.ds(i * LANES, LANES), pl.ds(j * LANES, LANES)]
+    piece = packed.shape[0] // n
+    for k in range(n):
+        there = packed[pl.ds(pl.multiple_of((me ^ k) * piece, SUBS), piece), :]
+        (give if k % 2 else keep)[pl.ds(k // 2 * piece, piece), :] = there
+
+
+def tile_of(rows):
+    return max(t for t in range(LANES, 641, LANES) if rows % t == 0)
+
+
+def early_gram(shape, raw, counts, lon_center, columns, parts):
+    n = shape[0]
     each, rows = parts[0].shape
-    cols = each * n
-    tile = 640 if rows % 640 == 0 else LANES
+    cols, tile = each * n, tile_of(rows)
+    vmem = pl.BlockSpec(memory_space=VMEM)
+    return pl.pallas_call(
+        functools.partial(early_kernel, shape, cols, tile, raw),
+        out_shape=jax.ShapeDtypeStruct((cols, cols), jnp.float32),
+        in_specs=[pl.BlockSpec(memory_space=SMEM)] * 2 + [vmem] * (n + 1),
+        out_specs=vmem,
+        scratch_shapes=[pltpu.VMEM((2, cols, tile), jnp.bfloat16)] * 2
+        + [pltpu.VMEM((2, len(raw) * each, LANES), jnp.float32)] * 2,
+        compiler_params=pltpu.CompilerParams(vmem_limit_bytes=32 << 20),
+        cost_estimate=pl.CostEstimate(flops=0, bytes_accessed=0, transcendentals=0),
+        name="gram",
+    )(counts, lon_center, columns, *parts)
+
+
+def late_gram(n, parts, before):
+    each, rows = parts[0].shape
+    cols, tile = each * n, tile_of(rows)
     height = len(upper_blocks(cols)) * LANES
-    scratch = [pltpu.VMEM((2, cols, tile), jnp.bfloat16)] * 2
-    if last:
-        out_shape = [jax.ShapeDtypeStruct((height // n, LANES), jnp.float32)] * n
-        scratch += [pltpu.VMEM((cols, cols), jnp.float32), pltpu.VMEM((height, LANES), jnp.float32)]
-    else:
-        out_shape = [jax.ShapeDtypeStruct((cols, cols), jnp.float32)]
+    vmem = pl.BlockSpec(memory_space=VMEM)
     return pl.pallas_call(
-        functools.partial(gram_kernel, n, cols, tile, not before, last),
-        out_shape=out_shape,
-        in_specs=[pl.BlockSpec(memory_space=VMEM)] * (n + len(before)),
-        out_specs=[pl.BlockSpec(memory_space=VMEM)] * len(out_shape),
-        scratch_shapes=scratch,
+        functools.partial(late_kernel, n, cols, tile),
+        out_shape=[jax.ShapeDtypeStruct((height // 2, LANES), jnp.float32)] * 2,
+        in_specs=[vmem] * (n + 1),
+        out_specs=[vmem] * 2,
+        scratch_shapes=[pltpu.VMEM((2, cols, tile), jnp.bfloat16)] * 2
+        + [pltpu.VMEM((cols, cols), jnp.float32), pltpu.VMEM((height, LANES), jnp.float32)],
         compiler_params=pltpu.CompilerParams(vmem_limit_bytes=32 << 20),
         cost_estimate=pl.CostEstimate(
             flops=6 * cols * cols * rows, bytes_accessed=4 * cols * rows, transcendentals=0
         ),
-        name="gram",
-    )(*parts, *before)
+        name="gram_late",
+    )(*parts, before)
 
 
 def row_wide(ref, row, column):
@@ -345,22 +508,33 @@
     cols = cols_dev * n
     rows_dev = rows_grp // n
     valid_rows = 3 * rows_grp // 4
-    per = -(-((valid_rows + (LANES - 1) * n) // LANES) // n)
-    late = max(1, per // 5)
-    shape = (n, (per - late, late), rows_dev, rows_grp, 1.0 / math.sqrt(rows_grp * groups))
-    order = sorted(range(1, n), key=lambda k: (-bin(k >> 1).count("1"), k)) + [0]
-    early_parts, late_parts = [None] * n, [None] * n
-    for k in order:
-        early_parts[k], late_parts[k] = design(shape, k, counts, lon_center, column_index, legendre)
-        early_parts[k] = swap(early_parts[k], "ord", k)
-    gate = order[1]
-    early_parts[gate], late_parts = lax.optimization_barrier((early_parts[gate], late_parts))
+    per = valid_rows // LANES // n
+    late = max(1, per // 6)
+    early = per - late
+    shape = (n, per, rows_dev, rows_grp, 1.0 / math.sqrt(rows_grp * groups))
+    columns = column_index[1:3].astype(jnp.float32).T
+    own = lax.dynamic_slice_in_dim(columns, lax.axis_index("ord") * cols_dev, cols_dev, 0)
+    far = sorted(range(2, n), key=lambda k: (-bin(k >> 1).count("1"), k & 1, k))
+    raw = (far[0], far[1], 1, far[2], far[3])
+    early_parts = [None] * n
+    for k in raw:
+        early_parts[k] = swap(pick(shape, k, early, counts, legendre), "ord", k)
+    early_parts[1], now = lax.optimization_barrier((early_parts[1], counts))
+    for k in far[4:5] + [0] + far[5:]:
+        part = design(shape, (k,), 0, early, now, lon_center, own, legendre)[0]
+        part, now = lax.optimization_barrier((part, now))
+        early_parts[k] = swap(part, "ord", k)
+    late_parts = design(shape, tuple(range(n)), early, late, now, lon_center, own, legendre)
     late_parts = [swap(late_parts[k], "ord", k) for k in range(n)]
-    before = gram(n, early_parts, [], False)
-    pieces = gram(n, late_parts, before, True)
-    share = tree_sum([swap(pieces[k], "ord", k) for k in range(n)])
-    share = tree_sum([swap(share, "grp", k) for k in range(groups)])
-    gathered = [swap(share, "ord", k) for k in range(n)]
+    before = early_gram(shape, raw, counts, lon_center, columns, early_parts)
+    keep, give = late_gram(n, late_parts, before)
+    half = (keep + swap(give, "ord", 1)).reshape(n // 2, -1, LANES)
+    share = tree_sum([swap(half[c], "ord", 2 * c) for c in reversed(range(n // 2))])
+    share = tree_sum([swap(share, "grp", k) for k in reversed(range(groups))])
+    gathered = []
+    for c in range(n // 2):
+        there = swap(share, "ord", 2 * c)
+        gathered += [there, swap(there, "ord", 1)]
     degree = column_index[0:1].astype(jnp.float32)
     kaula_weight = kaula_gain * (degree / NMAX) ** 2
     return factor(n, cols, kaula_weight * kaula_weight, gathered)

time: 136 us -> 132 us (0.971)
  starting transfers between devices: 34.1 us -> 29.6 us
  waiting for transfers between devices: 39.9 us -> 37.6 us
  local copies, waits for them, and re-layouts: 1.13 us -> 3.18 us
    ppermute x31 -> x28, starting transfers between devices: 34.1 us -> 29.6 us  [swap(): return lax.ppermute(x, axis, pairs(lax.axis_size(axis), k)) if k else x]
    ppermute x31 -> x28, waiting for transfers between devices: 39.9 us -> 37.6 us  [swap(): return lax.ppermute(x, axis, pairs(lax.axis_size(axis), k)) if k else x]
    transpose x0 -> x1, other arithmetic: none -> 1.69 us  [body(): columns = column_index[1:3].astype(jnp.float32).T]
    dynamic_slice x0 -> x1, local copies, waits for them, and re-layouts: none -> 1.38 us  [body(): lax.dynamic_slice_in_dim(columns, lax.axis_index('ord') * cols_dev, cols_...]
    pallas_call x10 -> x11, Pallas kernels: 44.5 us -> 43.5 us  [the longest x4 21.5 us: design(): pl.pallas_call(functools.partial(design_kernel, shape, ks, first, size),...]
  transfers between devices with their start and end apart: 31 -> 28, of which waited for: 9 -> 12; matrix products, arithmetic and copies ran while one was open for 1% -> 3% of each run, Pallas kernels for 28% -> 30%
where the time goes in v3:
time: 132 us; the launch traced here: 130 us
  Pallas kernels  57.3 us (43%)
  waiting for transfers between devices  37.6 us (28%)
  starting transfers between devices  29.6 us (22%)
  local copies, waits for them, and re-layouts  3.18 us (2%)
  other arithmetic  1.77 us (1%)
    ppermute x28, waiting for transfers between devices, swap(): return lax.ppermute(x, axis, pairs(lax.axis_size(axis), k)) if k else x  37.6 us
    ppermute x28, starting transfers between devices, swap(): return lax.ppermute(x, axis, pairs(lax.axis_size(axis), k)) if k else x  29.6 us
    pallas_call x4, Pallas kernels, design(): pl.pallas_call(functools.partial(design_kernel, shape, ks, first, size),...  21.5 us
    pallas_call x5, Pallas kernels, pick(): pl.pallas_call(functools.partial(pick_kernel, shape, k, size), out_shape=...  14.2 us
    pallas_call x1, Pallas kernels, factor(): pl.pallas_call(functools.partial(factor_kernel, n, cols), out_shape=jax.S...  13.8 us
    pallas_call x1, Pallas kernels, early_gram(): pl.pallas_call(functools.partial(early_kernel, shape, cols, tile, raw), o...  6.76 us
  transfers between devices with their start and end apart: 28, of which 12 were waited for; matrix products, arithmetic and copies ran while one was open for 3% of the time, Pallas kernels for 30%

profile of v3, /device:TPU:0, one launch (start us, length us, event | category | flops | bytes accessed | tf_op | source)
XLA Modules:
  0.0 130.3 jit_solution(13600229736825444587)
XLA Ops:
  0.0 2.8 %pick.5 = f32[64,2560]{1,0:T(8,128)} custom-call(s32[1,8]{1,0:T(1,128)} %counts_ref.15, f32[64,32768]{1,0:T(8,128)} %leg_ref.17), custom_call_target="tpu_custom_call" | custom-call | flops 1310720 | bytes 1310720 | tf_op jit(solution)/shard_map/jit(pick)/pick/pallas_call | solution.py:98
  3.3 2.8 %pick.7 = f32[64,2560]{1,0:T(8,128)} custom-call(s32[1,8]{1,0:T(1,128)} %counts_ref.15, f32[64,32768]{1,0:T(8,128)} %leg_ref.17), custom_call_target="tpu_custom_call" | custom-call | flops 1310720 | bytes 1310720 | tf_op jit(solution)/shard_map/jit(pick)/pick/pallas_call | solution.py:98
  6.2 2.6 %collective-permute-start.10 = (f32[64,2560]{1,0:T(8,128)}, f32[64,2560]{1,0:T(8,128)S(1)}, u32[]{:S(2)}, u32[]{:S(2)}) collective-permute-start(f32[64,2560]{1,0:T(8,128)} %pick.7), channel_id=1, source_target_pairs={{0,4},{1,5},{2,6},{3,7},{4,0},{5,1},{6,2},{7,3},{8,12},{9,13},{10,... | collective-permute-start | bytes 1966088 | tf_op jit(solution)/shard_map/ppermute | solution.py:496
  8.8 2.9 %pick.8 = f32[64,2560]{1,0:T(8,128)} custom-call(s32[1,8]{1,0:T(1,128)} %counts_ref.15, f32[64,32768]{1,0:T(8,128)} %leg_ref.17), custom_call_target="tpu_custom_call" | custom-call | flops 1310720 | bytes 1310720 | tf_op jit(solution)/shard_map/jit(pick)/pick/pallas_call | solution.py:98
  13.2 2.8 %pick.9 = f32[64,2560]{1,0:T(8,128)} custom-call(s32[1,8]{1,0:T(1,128)} %counts_ref.15, f32[64,32768]{1,0:T(8,128)} %leg_ref.17), custom_call_target="tpu_custom_call" | custom-call | flops 1310720 | bytes 1310720 | tf_op jit(solution)/shard_map/jit(pick)/pick/pallas_call | solution.py:98
  17.1 2.8 %pick.6 = f32[64,2560]{1,0:T(8,128)} custom-call(s32[1,8]{1,0:T(1,128)} %counts_ref.15, f32[64,32768]{1,0:T(8,128)} %leg_ref.17), custom_call_target="tpu_custom_call" | custom-call | flops 1310720 | bytes 1310720 | tf_op jit(solution)/shard_map/jit(pick)/pick/pallas_call | solution.py:98
  22.4 1.7 %convert_bitcast_fusion = (f32[512,2]{1,0:T(8,128)S(1)}, f32[2,512]{0,1:T(8,128)}) fusion(s32[2,512]{0,1:T(8,128)} %copy.5), kind=kLoop, calls=%fused_computation.5 | loop fusion | flops 1024 | bytes 12288 | tf_op jit(solution)/shard_map/transpose | solution.py:515
  26.1 4.4 %design.4 = f32[64,2560]{1,0:T(8,128)} custom-call(s32[1,8]{1,0:T(1,128)} %counts_ref.15, f32[1]{0:T(128)S(6)} %copy.6.lon_ref, f32[64,2]{1,0:T(8,128)} %dynamic-slice_bitcast_fusion.cols_ref, f32[64,32768]{1,0:T(8,128)} %leg_ref.17), custom_call_target="tpu_custom_call" | custom-call | flops 1310720 | bytes 1310720 | tf_op jit(solution)/shard_map/jit(design)/design/pallas_call | solution.py:207
  30.5 4.5 %design.5.refs_0_ = f32[64,2560]{1,0:T(8,128)} custom-call(s32[1,8]{1,0:T(1,128)} %counts_ref.15, f32[1]{0:T(128)S(6)} %copy.6.lon_ref, f32[64,2]{1,0:T(8,128)} %dynamic-slice_bitcast_fusion.cols_ref, f32[64,32768]{1,0:T(8,128)} %leg_ref.17), custom_call_target="tpu_custom_call" | custom-call | flops 1310720 | bytes 1310720 | tf_op jit(solution)/shard_map/jit(design)/design/pallas_call | solution.py:207
  35.0 4.5 %design.6 = f32[64,2560]{1,0:T(8,128)} custom-call(s32[1,8]{1,0:T(1,128)} %counts_ref.15, f32[1]{0:T(128)S(6)} %copy.6.lon_ref, f32[64,2]{1,0:T(8,128)} %dynamic-slice_bitcast_fusion.cols_ref, f32[64,32768]{1,0:T(8,128)} %leg_ref.17), custom_call_target="tpu_custom_call" | custom-call | flops 1310720 | bytes 1310720 | tf_op jit(solution)/shard_map/jit(design)/design/pallas_call | solution.py:207
  40.0 12.7 %collective-permute-done.10.refs_4_ = f32[64,2560]{1,0:T(8,128)S(1)} collective-permute-done((f32[64,2560]{1,0:T(8,128)}, f32[64,2560]{1,0:T(8,128)S(1)}, u32[]{:S(2)}, u32[]{:S(2)}) %collective-permute-start.10) | collective-permute-done | bytes 655392 | tf_op jit(solution)/shard_map/ppermute | solution.py:496
  53.5 8.2 %design.7 = (f32[64,512]{1,0:T(8,128)}, f32[64,512]{1,0:T(8,128)}, f32[64,512]{1,0:T(8,128)}, f32[64,512]{1,0:T(8,128)}, f32[64,512]{1,0:T(8,128)}, /*index=5*/f...) custom-call(s32[1,8]{1,0:T(1,128)} %counts_ref.15, f32[1]{0:T(128)S(6)} %copy.6.lon_ref, ...), custom_call_target="tpu_custom_call" | custom-call | flops 2097152 | bytes 2097152 | tf_op jit(solution)/shard_map/jit(design)/design/pallas_call | solution.py:207
  65.9 8.0 %collective-permute-done.2.refs_2_ = f32[64,512]{1,0:T(8,128)S(1)} collective-permute-done((f32[64,512]{1,0:T(8,128)}, f32[64,512]{1,0:T(8,128)S(1)}, u32[]{:S(2)}, u32[]{:S(2)}) %collective-permute-start.2) | collective-permute-done | bytes 131104 | tf_op jit(solution)/shard_map/ppermute | solution.py:496
  74.2 2.6 %collective-permute-start.6 = (f32[64,512]{1,0:T(8,128)}, f32[64,512]{1,0:T(8,128)S(1)}, u32[]{:S(2)}, u32[]{:S(2)}) collective-permute-start(f32[64,512]{1,0:T(8,128)} %get-tuple-element.33), channel_id=1, source_target_pairs={{0,6},{1,7},{2,4},{3,5},{4,2},{5,3},{6,0},{7,1},{8,14},{9,15},{10,... | collective-permute-start | bytes 393224 | tf_op jit(solution)/shard_map/ppermute | solution.py:496
  78.3 6.8 %gram.1.refs_8_ = f32[512,512]{1,0:T(8,128)S(1)} custom-call(s32[1,8]{1,0:T(1,128)S(1)} %copy-done.1, f32[1]{0:T(128)S(6)} %copy.6.lon_ref, f32[512,2]{1,0:T(8,128)S(1)} %get-tuple-element.44.cols_ref, f32[64,2560]{1,0:T(8,128)S(1)} %copy-done, f32[64,2560]{1,0:T(8,128)S(1)} %collective-permute-done.refs_1_, f32[64,2560]{1,0:T(8,128)S(1)} %collective-permute-done.8.refs_2_, ...), custom_call_target="tpu_custom_call" | custom-call | tf_op jit(solution)/shard_map/gram/pallas_call | solution.py:333
  88.9 2.5 %collective-permute-start.15 = (f32[160,128]{1,0:T(8,128)S(1)}, f32[160,128]{1,0:T(8,128)S(1)}, u32[]{:S(2)}, u32[]{:S(2)}) collective-permute-start(f32[160,128]{1,0:T(8,128)S(1)} %get-tuple-element.43), channel_id=1, source_target_pairs={{0,6},{1,7},{2,4},{3,5},{4,2},{5,3},{6,0},{7,1},{8,14},{9,15},{10,... | collective-permute-start | bytes 245768 | tf_op jit(solution)/shard_map/ppermute | solution.py:496
  92.7 1.7 %collective-permute-done.15 = f32[160,128]{1,0:T(8,128)S(1)} collective-permute-done((f32[160,128]{1,0:T(8,128)S(1)}, f32[160,128]{1,0:T(8,128)S(1)}, u32[]{:S(2)}, u32[]{:S(2)}) %collective-permute-start.15) | collective-permute-done | bytes 81952 | tf_op jit(solution)/shard_map/ppermute | solution.py:496
  94.5 1.7 %collective-permute-done.16 = f32[160,128]{1,0:T(8,128)S(1)} collective-permute-done((f32[160,128]{1,0:T(8,128)S(1)}, f32[160,128]{1,0:T(8,128)S(1)}, u32[]{:S(2)}, u32[]{:S(2)}) %collective-permute-start.16) | collective-permute-done | bytes 81952 | tf_op jit(solution)/shard_map/ppermute | solution.py:496
  97.2 3.7 %collective-permute-start.18 = (f32[160,128]{1,0:T(8,128)S(1)}, f32[160,128]{1,0:T(8,128)S(1)}, u32[]{:S(2)}, u32[]{:S(2)}) collective-permute-start(f32[160,128]{1,0:T(8,128)S(1)} %fusion), channel_id=1, source_target_pairs={{0,24},{8,16},{16,8},{24,0},{1,25},{9,17},{17,9},{25,1},{2,26},{10... | collective-permute-start | bytes 245768 | tf_op jit(solution)/shard_map/ppermute | solution.py:496
  101.6 2.6 %collective-permute-done.18 = f32[160,128]{1,0:T(8,128)S(1)} collective-permute-done((f32[160,128]{1,0:T(8,128)S(1)}, f32[160,128]{1,0:T(8,128)S(1)}, u32[]{:S(2)}, u32[]{:S(2)}) %collective-permute-start.18) | collective-permute-done | bytes 81952 | tf_op jit(solution)/shard_map/ppermute | solution.py:496
  104.2 3.4 %collective-permute-done.19 = f32[160,128]{1,0:T(8,128)S(1)} collective-permute-done((f32[160,128]{1,0:T(8,128)S(1)}, f32[160,128]{1,0:T(8,128)S(1)}, u32[]{:S(2)}, u32[]{:S(2)}) %collective-permute-start.19) | collective-permute-done | bytes 81952 | tf_op jit(solution)/shard_map/ppermute | solution.py:496
  107.9 2.0 %collective-permute-start.24 = (f32[160,128]{1,0:T(8,128)S(1)}, f32[160,128]{1,0:T(8,128)S(1)}, u32[]{:S(2)}, u32[]{:S(2)}) collective-permute-start(f32[160,128]{1,0:T(8,128)S(1)} %add_add_fusion.refs_0_), channel_id=1, source_target_pairs={{0,4},{1,5},{2,6},{3,7},{4,0},{5,1},{6,2},{7,3},{8,12},{9,13},{10,... | collective-permute-start | bytes 245768 | tf_op jit(solution)/shard_map/ppermute | solution.py:496
  113.4 1.8 %collective-permute-done.26.refs_6_ = f32[160,128]{1,0:T(8,128)S(1)} collective-permute-done((f32[160,128]{1,0:T(8,128)S(1)}, f32[160,128]{1,0:T(8,128)S(1)}, u32[]{:S(2)}, u32[]{:S(2)}) %collective-permute-start.26) | collective-permute-done | bytes 81952 | tf_op jit(solution)/shard_map/ppermute | solution.py:496
  116.5 13.8 %factor.1 = f32[512,512]{1,0:T(8,128)} custom-call(f32[1,512]{1,0:T(1,128)S(1)} %multiply_multiply_fusion.kaula_ref, f32[160,128]{1,0:T(8,128)S(1)} %add_add_fusion.refs_0_, f32[160,128]{1,0:T(8,128)S(1)} %collective-permute-done.21.refs_1_, f32[160,128]{1,0:T(8,128)S(1)} %collective-permute-done.22.refs_2_, f32[160,128]{1,0:T(8,128)S(1)} %collective-permute-done.23.refs_3_, ...), custom_call_target="tpu_custom_call" | custom-call | tf_op jit(solution)/shard_map/factor/pallas_call | solution.py:475
  (63 shorter events, 26.1 us)
Async XLA Ops:
  2.8 23.2 %collective-permute-start = (f32[64,2560]{1,0:T(8,128)}, f32[64,2560]{1,0:T(8,128)S(1)}, u32[]{:S(2)}, u32[]{:S(2)}) collective-permute-start(f32[64,2560]{1,0:T(8,128)} %pick.5), channel_id=1, source_target_pairs={{0,1},{1,0},{2,3},{3,2},{4,5},{5,4},{6,7},{7,6},{8,9},{9,8},{10,11... | collective-permute-start | bytes 1966088 | tf_op jit(solution)/shard_map/ppermute | solution.py:496
  6.2 46.5 %collective-permute-start.10 = (f32[64,2560]{1,0:T(8,128)}, f32[64,2560]{1,0:T(8,128)S(1)}, u32[]{:S(2)}, u32[]{:S(2)}) collective-permute-start(f32[64,2560]{1,0:T(8,128)} %pick.7), channel_id=1, source_target_pairs={{0,4},{1,5},{2,6},{3,7},{4,0},{5,1},{6,2},{7,3},{8,12},{9,13},{10,... | collective-permute-start | bytes 1966088 | tf_op jit(solution)/shard_map/ppermute | solution.py:496
  11.7 50.0 %collective-permute-start.12 = (f32[64,2560]{1,0:T(8,128)}, f32[64,2560]{1,0:T(8,128)S(1)}, u32[]{:S(2)}, u32[]{:S(2)}) collective-permute-start(f32[64,2560]{1,0:T(8,128)} %pick.8), channel_id=1, source_target_pairs={{0,6},{1,7},{2,4},{3,5},{4,2},{5,3},{6,0},{7,1},{8,14},{9,15},{10,... | collective-permute-start | bytes 1966088 | tf_op jit(solution)/shard_map/ppermute | solution.py:496
  16.0 47.0 %collective-permute-start.13 = (f32[64,2560]{1,0:T(8,128)}, f32[64,2560]{1,0:T(8,128)S(1)}, u32[]{:S(2)}, u32[]{:S(2)}) collective-permute-start(f32[64,2560]{1,0:T(8,128)} %pick.9), channel_id=1, source_target_pairs={{0,7},{1,6},{2,5},{3,4},{4,3},{5,2},{6,1},{7,0},{8,15},{9,14},{10,... | collective-permute-start | bytes 1966088 | tf_op jit(solution)/shard_map/ppermute | solution.py:496
  19.9 43.2 %collective-permute-start.8 = (f32[64,2560]{1,0:T(8,128)}, f32[64,2560]{1,0:T(8,128)S(1)}, u32[]{:S(2)}, u32[]{:S(2)}) collective-permute-start(f32[64,2560]{1,0:T(8,128)} %pick.6), channel_id=1, source_target_pairs={{0,2},{1,3},{2,0},{3,1},{4,6},{5,7},{6,4},{7,5},{8,10},{9,11},{10,... | collective-permute-start | bytes 1966088 | tf_op jit(solution)/shard_map/ppermute | solution.py:496
  39.5 34.7 %collective-permute-start.11 = (f32[64,2560]{1,0:T(8,128)}, f32[64,2560]{1,0:T(8,128)S(1)}, u32[]{:S(2)}, u32[]{:S(2)}) collective-permute-start(f32[64,2560]{1,0:T(8,128)} %design.6), channel_id=1, source_target_pairs={{0,5},{1,4},{2,7},{3,6},{4,1},{5,0},{6,3},{7,2},{8,13},{9,12},{10,... | collective-permute-start | bytes 1966088 | tf_op jit(solution)/shard_map/ppermute | solution.py:496
  52.7 24.2 %collective-permute-start.9 = (f32[64,2560]{1,0:T(8,128)S(1)}, f32[64,2560]{1,0:T(8,128)S(1)}, u32[]{:S(2)}, u32[]{:S(2)}) collective-permute-start(f32[64,2560]{1,0:T(8,128)S(1)} %copy-done.3), channel_id=1, source_target_pairs={{0,3},{1,2},{2,1},{3,0},{4,7},{5,6},{6,5},{7,4},{8,11},{9,10},{10,... | collective-permute-start | bytes 1966088 | tf_op jit(solution)/shard_map/ppermute | solution.py:496
  61.7 2.7 %collective-permute-start.1 = (f32[64,512]{1,0:T(8,128)}, f32[64,512]{1,0:T(8,128)S(1)}, u32[]{:S(2)}, u32[]{:S(2)}) collective-permute-start(f32[64,512]{1,0:T(8,128)} %get-tuple-element.28), channel_id=1, source_target_pairs={{0,1},{1,0},{2,3},{3,2},{4,5},{5,4},{6,7},{7,6},{8,9},{9,8},{10,11... | collective-permute-start | bytes 393224 | tf_op jit(solution)/shard_map/ppermute | solution.py:496
  63.0 11.0 %collective-permute-start.2 = (f32[64,512]{1,0:T(8,128)}, f32[64,512]{1,0:T(8,128)S(1)}, u32[]{:S(2)}, u32[]{:S(2)}) collective-permute-start(f32[64,512]{1,0:T(8,128)} %get-tuple-element.29), channel_id=1, source_target_pairs={{0,2},{1,3},{2,0},{3,1},{4,6},{5,7},{6,4},{7,5},{8,10},{9,11},{10,... | collective-permute-start | bytes 393224 | tf_op jit(solution)/shard_map/ppermute | solution.py:496
  63.1 22.0 %collective-permute-start.3 = (f32[64,512]{1,0:T(8,128)}, f32[64,512]{1,0:T(8,128)S(1)}, u32[]{:S(2)}, u32[]{:S(2)}) collective-permute-start(f32[64,512]{1,0:T(8,128)} %get-tuple-element.30), channel_id=1, source_target_pairs={{0,3},{1,2},{2,1},{3,0},{4,7},{5,6},{6,5},{7,4},{8,11},{9,10},{10,... | collective-permute-start | bytes 393224 | tf_op jit(solution)/shard_map/ppermute | solution.py:496
  64.4 20.7 %collective-permute-start.4 = (f32[64,512]{1,0:T(8,128)}, f32[64,512]{1,0:T(8,128)S(1)}, u32[]{:S(2)}, u32[]{:S(2)}) collective-permute-start(f32[64,512]{1,0:T(8,128)} %get-tuple-element.31), channel_id=1, source_target_pairs={{0,4},{1,5},{2,6},{3,7},{4,0},{5,1},{6,2},{7,3},{8,12},{9,13},{10,... | collective-permute-start | bytes 393224 | tf_op jit(solution)/shard_map/ppermute | solution.py:496
  73.9 11.2 %collective-permute-start.5 = (f32[64,512]{1,0:T(8,128)}, f32[64,512]{1,0:T(8,128)S(1)}, u32[]{:S(2)}, u32[]{:S(2)}) collective-permute-start(f32[64,512]{1,0:T(8,128)} %get-tuple-element.32), channel_id=1, source_target_pairs={{0,5},{1,4},{2,7},{3,6},{4,1},{5,0},{6,3},{7,2},{8,13},{9,12},{10,... | collective-permute-start | bytes 393224 | tf_op jit(solution)/shard_map/ppermute | solution.py:496
  74.2 10.9 %collective-permute-start.6 = (f32[64,512]{1,0:T(8,128)}, f32[64,512]{1,0:T(8,128)S(1)}, u32[]{:S(2)}, u32[]{:S(2)}) collective-permute-start(f32[64,512]{1,0:T(8,128)} %get-tuple-element.33), channel_id=1, source_target_pairs={{0,6},{1,7},{2,4},{3,5},{4,2},{5,3},{6,0},{7,1},{8,14},{9,15},{10,... | collective-permute-start | bytes 393224 | tf_op jit(solution)/shard_map/ppermute | solution.py:496
  76.9 8.2 %collective-permute-start.7 = (f32[64,512]{1,0:T(8,128)}, f32[64,512]{1,0:T(8,128)S(1)}, u32[]{:S(2)}, u32[]{:S(2)}) collective-permute-start(f32[64,512]{1,0:T(8,128)} %get-tuple-element.34), channel_id=1, source_target_pairs={{0,7},{1,6},{2,5},{3,4},{4,3},{5,2},{6,1},{7,0},{8,15},{9,14},{10,... | collective-permute-start | bytes 393224 | tf_op jit(solution)/shard_map/ppermute | solution.py:496
  88.9 5.6 %collective-permute-start.15 = (f32[160,128]{1,0:T(8,128)S(1)}, f32[160,128]{1,0:T(8,128)S(1)}, u32[]{:S(2)}, u32[]{:S(2)}) collective-permute-start(f32[160,128]{1,0:T(8,128)S(1)} %get-tuple-element.43), channel_id=1, source_target_pairs={{0,6},{1,7},{2,4},{3,5},{4,2},{5,3},{6,0},{7,1},{8,14},{9,15},{10,... | collective-permute-start | bytes 245768 | tf_op jit(solution)/shard_map/ppermute | solution.py:496
  91.3 4.8 %collective-permute-start.16 = (f32[160,128]{1,0:T(8,128)S(1)}, f32[160,128]{1,0:T(8,128)S(1)}, u32[]{:S(2)}, u32[]{:S(2)}) collective-permute-start(f32[160,128]{1,0:T(8,128)S(1)} %get-tuple-element.41), channel_id=1, source_target_pairs={{0,4},{1,5},{2,6},{3,7},{4,0},{5,1},{6,2},{7,3},{8,12},{9,13},{10,... | collective-permute-start | bytes 245768 | tf_op jit(solution)/shard_map/ppermute | solution.py:496
  92.7 4.4 %collective-permute-start.17 = (f32[160,128]{1,0:T(8,128)S(1)}, f32[160,128]{1,0:T(8,128)S(1)}, u32[]{:S(2)}, u32[]{:S(2)}) collective-permute-start(f32[160,128]{1,0:T(8,128)S(1)} %get-tuple-element.42), channel_id=1, source_target_pairs={{0,2},{1,3},{2,0},{3,1},{4,6},{5,7},{6,4},{7,5},{8,10},{9,11},{10,... | collective-permute-start | bytes 245768 | tf_op jit(solution)/shard_map/ppermute | solution.py:496
  97.2 7.0 %collective-permute-start.18 = (f32[160,128]{1,0:T(8,128)S(1)}, f32[160,128]{1,0:T(8,128)S(1)}, u32[]{:S(2)}, u32[]{:S(2)}) collective-permute-start(f32[160,128]{1,0:T(8,128)S(1)} %fusion), channel_id=1, source_target_pairs={{0,24},{8,16},{16,8},{24,0},{1,25},{9,17},{17,9},{25,1},{2,26},{10... | collective-permute-start | bytes 245768 | tf_op jit(solution)/shard_map/ppermute | solution.py:496
  100.8 6.8 %collective-permute-start.19 = (f32[160,128]{1,0:T(8,128)S(1)}, f32[160,128]{1,0:T(8,128)S(1)}, u32[]{:S(2)}, u32[]{:S(2)}) collective-permute-start(f32[160,128]{1,0:T(8,128)S(1)} %fusion), channel_id=1, source_target_pairs={{0,16},{8,24},{16,0},{24,8},{1,17},{9,25},{17,1},{25,9},{2,18},{10... | collective-permute-start | bytes 245768 | tf_op jit(solution)/shard_map/ppermute | solution.py:496
  100.8 6.8 %collective-permute-start.20 = (f32[160,128]{1,0:T(8,128)S(1)}, f32[160,128]{1,0:T(8,128)S(1)}, u32[]{:S(2)}, u32[]{:S(2)}) collective-permute-start(f32[160,128]{1,0:T(8,128)S(1)} %fusion), channel_id=1, source_target_pairs={{0,8},{8,0},{16,24},{24,16},{1,9},{9,1},{17,25},{25,17},{2,10},{10... | collective-permute-start | bytes 245768 | tf_op jit(solution)/shard_map/ppermute | solution.py:496
  107.7 5.2 %collective-permute-start.22 = (f32[160,128]{1,0:T(8,128)S(1)}, f32[160,128]{1,0:T(8,128)S(1)}, u32[]{:S(2)}, u32[]{:S(2)}) collective-permute-start(f32[160,128]{1,0:T(8,128)S(1)} %add_add_fusion.refs_0_), channel_id=1, source_target_pairs={{0,2},{1,3},{2,0},{3,1},{4,6},{5,7},{6,4},{7,5},{8,10},{9,11},{10,... | collective-permute-start | bytes 245768 | tf_op jit(solution)/shard_map/ppermute | solution.py:496
  107.9 5.3 %collective-permute-start.24 = (f32[160,128]{1,0:T(8,128)S(1)}, f32[160,128]{1,0:T(8,128)S(1)}, u32[]{:S(2)}, u32[]{:S(2)}) collective-permute-start(f32[160,128]{1,0:T(8,128)S(1)} %add_add_fusion.refs_0_), channel_id=1, source_target_pairs={{0,4},{1,5},{2,6},{3,7},{4,0},{5,1},{6,2},{7,3},{8,12},{9,13},{10,... | collective-permute-start | bytes 245768 | tf_op jit(solution)/shard_map/ppermute | solution.py:496
  109.9 5.3 %collective-permute-start.26 = (f32[160,128]{1,0:T(8,128)S(1)}, f32[160,128]{1,0:T(8,128)S(1)}, u32[]{:S(2)}, u32[]{:S(2)}) collective-permute-start(f32[160,128]{1,0:T(8,128)S(1)} %add_add_fusion.refs_0_), channel_id=1, source_target_pairs={{0,6},{1,7},{2,4},{3,5},{4,2},{5,3},{6,0},{7,1},{8,14},{9,15},{10,... | collective-permute-start | bytes 245768 | tf_op jit(solution)/shard_map/ppermute | solution.py:496
  111.2 4.0 %collective-permute-start.21 = (f32[160,128]{1,0:T(8,128)S(1)}, f32[160,128]{1,0:T(8,128)S(1)}, u32[]{:S(2)}, u32[]{:S(2)}) collective-permute-start(f32[160,128]{1,0:T(8,128)S(1)} %add_add_fusion.refs_0_), channel_id=1, source_target_pairs={{0,1},{1,0},{2,3},{3,2},{4,5},{5,4},{6,7},{7,6},{8,9},{9,8},{10,11... | collective-permute-start | bytes 245768 | tf_op jit(solution)/shard_map/ppermute | solution.py:496
  (9 other events, 127.0 us)

commit v4 on v3

--- a/solution.py
+++ b/solution.py
@@ -122,16 +122,16 @@
     return lane_wide(outer[0], i) * inner[0] - lane_wide(outer[1], i) * inner[1]
 
 
-def wide_columns(columns):
-    rows = columns.shape[0]
-    harmonic = jnp.broadcast_to(columns[:, 0:1], (rows, LANES))
-    return harmonic, jnp.broadcast_to(columns[:, 1:2] * quarter_turn, (rows, LANES))
-
-
-def design_kernel(shape, ks, first, size, counts_ref, lon_ref, cols_ref, leg_ref, *refs):
+def wide_columns(cols_ref):
+    rows = cols_ref.shape[0]
+    harmonic = jnp.broadcast_to(cols_ref[:, 0:1], (rows, LANES))
+    return harmonic, jnp.broadcast_to(cols_ref[:, 1:2] * quarter_turn, (rows, LANES))
+
+
+def design_kernel(shape, first, size, counts_ref, lon_ref, cols_ref, leg_ref, *refs):
     blocks = Blocks(shape, counts_ref)
-    n, last = blocks.n, first + size == blocks.per
-    outs, (held, left, table, sems, left_sems) = refs[: len(ks)], refs[len(ks) :]
+    n = blocks.n
+    outs, (held, left, table, sems, left_sems) = refs[:n], refs[n:]
     me = lax.axis_index("ord")
 
     def origin(k):
@@ -146,43 +146,41 @@
         return pltpu.make_async_copy(leg_ref.at[:, pl.ds(start, LANES)], left.at[:, here], left_sems.at[r])
 
     def send(i):
-        for q, k in enumerate(ks):
-            copy(q * size + i, pl.multiple_of(blocks.place(origin(k) + i), LANES)).start()
+        for k in range(n):
+            copy(k * size + i, pl.multiple_of(blocks.place(origin(k) + i), LANES)).start()
 
     over(size, n, send)
-    for r in range(n if last else 0):
+    for r in range(n):
         copy_rest(r, pl.multiple_of(blocks.rest_places[r], LANES)).start()
         table[0, r] = blocks.rest[r]
         table[1, r] = blocks.rest_starts[r]
     rows = held.shape[0]
     tops = range(0, rows, SUBS)
     lane = lax.broadcasted_iota(jnp.int32, (SUBS, LANES), 1)
-    harmonic, phase = wide_columns(cols_ref[...])
+    harmonic, phase = wide_columns(cols_ref)
     inner = inner_tables(shape, harmonic, tops)
     begin = jnp.zeros_like(lane)
     for r in range(n):
         begin = jnp.where(lane == r, blocks.rest_places[r], begin)
-    outer = outer_tables(shape, lon_ref[0], begin, harmonic, phase, tops) if last else None
-    for r in range(n if last else 0):
+    outer = outer_tables(shape, lon_ref[0], begin, harmonic, phase, tops)
+    for r in range(n):
         copy_rest(r, 0).wait()
         for t, top in enumerate(tops):
             at = (pl.ds(top, SUBS), pl.ds(r * LANES, LANES))
             left[at] = jnp.where(lane < blocks.rest[r], left[at] * wave(outer[t], inner[t], r), 0.0)
     whole_lane = lax.broadcasted_iota(jnp.int32, (rows, LANES), 1)
-    for q, k in enumerate(ks):
+    for k in range(n):
         outer = outer_tables(shape, lon_ref[0], blocks.place(origin(k) + lane), harmonic, phase, tops)
         for i in range(size):
-            copy(q * size + i, 0).wait()
+            copy(k * size + i, 0).wait()
             for t, top in enumerate(tops):
-                tile = held[pl.ds(top, SUBS), pl.ds((q * size + i) * LANES, LANES)]
-                outs[q][pl.ds(top, SUBS), pl.ds(i * LANES, LANES)] = tile * wave(outer[t], inner[t], i)
-        if not last:
-            continue
+                tile = held[pl.ds(top, SUBS), pl.ds((k * size + i) * LANES, LANES)]
+                outs[k][pl.ds(top, SUBS), pl.ds(i * LANES, LANES)] = tile * wave(outer[t], inner[t], i)
 
         @pl.when((me ^ k) < blocks.packed)
-        def _(q=q, k=k):
+        def _(k=k):
             here = pl.ds((size - 1) * LANES, LANES)
-            outs[q][:, here] = jnp.zeros((rows, LANES), jnp.float32)
+            outs[k][:, here] = jnp.zeros((rows, LANES), jnp.float32)
 
             def add(r, _):
                 many = table[0, r]
@@ -193,32 +191,32 @@
                     spot = whole_lane - shift
                     tile = left[:, pl.ds(pl.multiple_of(r * LANES, LANES), LANES)]
                     rolled = pltpu.roll(tile, lax.rem(shift + LANES, LANES), 1)
-                    outs[q][:, here] += jnp.where((spot >= 0) & (spot < many), rolled, 0.0)
+                    outs[k][:, here] += jnp.where((spot >= 0) & (spot < many), rolled, 0.0)
 
                 return 0
 
             lax.fori_loop(0, n, add, 0)
 
 
-@functools.partial(jax.jit, static_argnums=(0, 1, 2, 3))
-def design(shape, ks, first, size, counts, lon_center, own, legendre):
-    n, rows, many = shape[0], legendre.shape[0], len(ks) * size
-    elements = rows * many * LANES
+@functools.partial(jax.jit, static_argnums=(0, 1, 2))
+def design(shape, first, size, counts, lon_center, own, legendre):
+    n, rows = shape[0], legendre.shape[0]
+    elements = rows * n * size * LANES
     return pl.pallas_call(
-        functools.partial(design_kernel, shape, ks, first, size),
-        out_shape=[jax.ShapeDtypeStruct((rows, size * LANES), jnp.float32)] * len(ks),
+        functools.partial(design_kernel, shape, first, size),
+        out_shape=[jax.ShapeDtypeStruct((rows, size * LANES), jnp.float32)] * n,
         in_specs=[
             pl.BlockSpec(memory_space=SMEM),
             pl.BlockSpec(memory_space=SMEM),
             pl.BlockSpec(memory_space=VMEM),
             pl.BlockSpec(memory_space=pltpu.HBM),
         ],
-        out_specs=[pl.BlockSpec(memory_space=VMEM)] * len(ks),
+        out_specs=[pl.BlockSpec(memory_space=VMEM)] * n,
         scratch_shapes=[
-            pltpu.VMEM((rows, many * LANES), jnp.float32),
+            pltpu.VMEM((rows, n * size * LANES), jnp.float32),
             pltpu.VMEM((rows, n * LANES), jnp.float32),
             pltpu.SMEM((2, n), jnp.int32),
-            pltpu.SemaphoreType.DMA((many,)),
+            pltpu.SemaphoreType.DMA((n * size,)),
             pltpu.SemaphoreType.DMA((n,)),
         ],
         compiler_params=pltpu.CompilerParams(vmem_limit_bytes=56 << 20),
@@ -247,7 +245,7 @@
     for s in range(rows // tile):
         for k in range(n):
             begin = pl.multiple_of((me ^ k) * each, each)
-            value(k, s, begin, ins[k], high.at[s % 2], low.at[s % 2])
+            value(s, begin, ins[k], high.at[s % 2], low.at[s % 2])
         for i in range(0, cols, tall):
             hi, lo = high[s % 2, pl.ds(i, tall), :], low[s % 2, pl.ds(i, tall), :]
             his, los = high[s % 2, pl.ds(i, cols - i), :], low[s % 2, pl.ds(i, cols - i), :]
@@ -259,39 +257,34 @@
     return top, (x - top.astype(jnp.float32)).astype(jnp.bfloat16)
 
 
-def early_kernel(shape, cols, tile, raw, counts_ref, lon_ref, cols_ref, *refs):
+def early_kernel(shape, cols, tile, counts_ref, lon_ref, cols_ref, *refs):
     n = shape[0]
     ins, (acc, high, low, inner_ref, outer_ref) = refs[:n], refs[n:]
     blocks = Blocks(shape, counts_ref)
     me = lax.axis_index("ord")
-    each = cols // n
-    tops = range(0, each, SUBS)
     lane = lax.broadcasted_iota(jnp.int32, (SUBS, LANES), 1)
     begins = blocks.place(blocks.first(me) + lane)
-    for q, k in enumerate(raw):
-        harmonic, phase = wide_columns(cols_ref[pl.ds(pl.multiple_of((me ^ k) * each, each), each), :])
-        inner = inner_tables(shape, harmonic, tops)
-        outer = outer_tables(shape, lon_ref[0], begins, harmonic, phase, tops)
-        for t, top in enumerate(tops):
-            for half in range(2):
-                inner_ref[half, pl.ds(q * each + top, SUBS), :] = inner[t][half]
-                outer_ref[half, pl.ds(q * each + top, SUBS), :] = outer[t][half]
+    harmonic, phase = wide_columns(cols_ref)
+    tops = range(0, cols, SUBS)
+    inner = inner_tables(shape, harmonic, tops)
+    outer = outer_tables(shape, lon_ref[0], begins, harmonic, phase, tops)
+    for t, top in enumerate(tops):
+        for half in range(2):
+            inner_ref[half, pl.ds(top, SUBS), :] = inner[t][half]
+            outer_ref[half, pl.ds(top, SUBS), :] = outer[t][half]
+    each = cols // n
     step = 2 * SUBS
 
-    def value(k, s, begin, part, high_ref, low_ref):
-        if k not in raw:
-            at = pl.ds(begin, each)
-            high_ref[at, :], low_ref[at, :] = split(part[:, pl.ds(s * tile, tile)])
-            return
+    def value(s, begin, leg, high_ref, low_ref):
         for top in range(0, each, step):
-            there = pl.ds(raw.index(k) * each + top, step)
-            inside = [inner_ref[half, there, :] for half in range(2)]
-            outside = [outer_ref[half, there, :] for half in range(2)]
+            at = pl.ds(pl.multiple_of(begin + top, step), step)
+            inside = [inner_ref[half, at, :] for half in range(2)]
+            outside = [outer_ref[half, at, :] for half in range(2)]
             for i in range(tile // LANES):
                 b = s * (tile // LANES) + i
                 c, d = (jnp.broadcast_to(x[:, b : b + 1], (step, LANES)) for x in outside)
-                x = part[pl.ds(top, step), pl.ds(b * LANES, LANES)] * (c * inside[0] - d * inside[1])
-                here = (pl.ds(pl.multiple_of(begin + top, step), step), pl.ds(i * LANES, LANES))
+                x = leg[pl.ds(top, step), pl.ds(b * LANES, LANES)] * (c * inside[0] - d * inside[1])
+                here = (at, pl.ds(i * LANES, LANES))
                 high_ref[here], low_ref[here] = split(x)
 
     def add(s, at, block):
@@ -305,7 +298,7 @@
     me = lax.axis_index("ord")
     each = cols // n
 
-    def value(k, s, begin, part, high_ref, low_ref):
+    def value(s, begin, part, high_ref, low_ref):
         at = pl.ds(begin, each)
         high_ref[at, :], low_ref[at, :] = split(part[:, pl.ds(s * tile, tile)])
 
@@ -325,18 +318,18 @@
     return max(t for t in range(LANES, 641, LANES) if rows % t == 0)
 
 
-def early_gram(shape, raw, counts, lon_center, columns, parts):
+def early_gram(shape, counts, lon_center, columns, parts):
     n = shape[0]
     each, rows = parts[0].shape
     cols, tile = each * n, tile_of(rows)
     vmem = pl.BlockSpec(memory_space=VMEM)
     return pl.pallas_call(
-        functools.partial(early_kernel, shape, cols, tile, raw),
+        functools.partial(early_kernel, shape, cols, tile),
         out_shape=jax.ShapeDtypeStruct((cols, cols), jnp.float32),
         in_specs=[pl.BlockSpec(memory_space=SMEM)] * 2 + [vmem] * (n + 1),
         out_specs=vmem,
         scratch_shapes=[pltpu.VMEM((2, cols, tile), jnp.bfloat16)] * 2
-        + [pltpu.VMEM((2, len(raw) * each, LANES), jnp.float32)] * 2,
+        + [pltpu.VMEM((2, cols, LANES), jnp.float32)] * 2,
         compiler_params=pltpu.CompilerParams(vmem_limit_bytes=32 << 20),
         cost_estimate=pl.CostEstimate(flops=0, bytes_accessed=0, transcendentals=0),
         name="gram",
@@ -514,23 +507,20 @@
     shape = (n, per, rows_dev, rows_grp, 1.0 / math.sqrt(rows_grp * groups))
     columns = column_index[1:3].astype(jnp.float32).T
     own = lax.dynamic_slice_in_dim(columns, lax.axis_index("ord") * cols_dev, cols_dev, 0)
-    far = sorted(range(2, n), key=lambda k: (-bin(k >> 1).count("1"), k & 1, k))
-    raw = (far[0], far[1], 1, far[2], far[3])
+    far = sorted(range(1, n), key=lambda k: (-bin(k >> 1).count("1"), k))
     early_parts = [None] * n
-    for k in raw:
+    for k in far:
         early_parts[k] = swap(pick(shape, k, early, counts, legendre), "ord", k)
-    early_parts[1], now = lax.optimization_barrier((early_parts[1], counts))
-    for k in far[4:5] + [0] + far[5:]:
-        part = design(shape, (k,), 0, early, now, lon_center, own, legendre)[0]
-        part, now = lax.optimization_barrier((part, now))
-        early_parts[k] = swap(part, "ord", k)
-    late_parts = design(shape, tuple(range(n)), early, late, now, lon_center, own, legendre)
+    gate = far[1]
+    early_parts[gate], now = lax.optimization_barrier((early_parts[gate], counts))
+    early_parts[0], now = lax.optimization_barrier((pick(shape, 0, early, now, legendre), now))
+    late_parts = design(shape, early, late, now, lon_center, own, legendre)
     late_parts = [swap(late_parts[k], "ord", k) for k in range(n)]
-    before = early_gram(shape, raw, counts, lon_center, columns, early_parts)
+    before = early_gram(shape, counts, lon_center, columns, early_parts)
     keep, give = late_gram(n, late_parts, before)
     half = (keep + swap(give, "ord", 1)).reshape(n // 2, -1, LANES)
-    share = tree_sum([swap(half[c], "ord", 2 * c) for c in reversed(range(n // 2))])
-    share = tree_sum([swap(share, "grp", k) for k in reversed(range(groups))])
+    share = tree_sum([swap(half[c], "ord", 2 * c) for c in range(n // 2)])
+    share = tree_sum([swap(share, "grp", k) for k in range(groups)])
     gathered = []
     for c in range(n // 2):
         there = swap(share, "ord", 2 * c)

time: 132 us -> 129 us (0.977)
  waiting for transfers between devices: 37.6 us -> 43.4 us
  Pallas kernels: 57.3 us -> 54.4 us
  starting transfers between devices: 29.6 us -> 27.6 us
  other arithmetic: 1.77 us -> 0.13 us
  local copies, waits for them, and re-layouts: 3.18 us -> 1.7 us
    pallas_call x5 -> x2, Pallas kernels: 28.3 us -> 16.8 us  [the longest x1 8.47 us: design(): pl.pallas_call(functools.partial(design_kernel, shape, first, size), out_...]
    pallas_call x5 -> x8, Pallas kernels: 14.2 us -> 22.8 us  [pick(): pl.pallas_call(functools.partial(pick_kernel, shape, k, size), out_shape=...]
    ppermute x28, waiting for transfers between devices: 37.6 us -> 43.4 us  [swap(): return lax.ppermute(x, axis, pairs(lax.axis_size(axis), k)) if k else x]
    ppermute x28, starting transfers between devices: 29.6 us -> 27.6 us  [swap(): return lax.ppermute(x, axis, pairs(lax.axis_size(axis), k)) if k else x]
    transpose x1, other arithmetic: 1.69 us -> 0.04 us  [body(): columns = column_index[1:3].astype(jnp.float32).T]
  transfers between devices with their start and end apart: 28 -> 28, of which waited for: 12 -> 15; matrix products, arithmetic and copies ran while one was open for 3% -> 1% of each run, Pallas kernels for 30% -> 29%
where the time goes in v4:
time: 129 us; the launch traced here: 128 us
  Pallas kernels  54.4 us (42%)
  waiting for transfers between devices  43.4 us (34%)
  starting transfers between devices  27.6 us (21%)
  local copies, waits for them, and re-layouts  1.7 us (1%)
    ppermute x28, waiting for transfers between devices, swap(): return lax.ppermute(x, axis, pairs(lax.axis_size(axis), k)) if k else x  43.4 us
    ppermute x28, starting transfers between devices, swap(): return lax.ppermute(x, axis, pairs(lax.axis_size(axis), k)) if k else x  27.6 us
    pallas_call x8, Pallas kernels, pick(): pl.pallas_call(functools.partial(pick_kernel, shape, k, size), out_shape=...  22.8 us
    pallas_call x1, Pallas kernels, factor(): pl.pallas_call(functools.partial(factor_kernel, n, cols), out_shape=jax.S...  13.8 us
    pallas_call x1, Pallas kernels, design(): pl.pallas_call(functools.partial(design_kernel, shape, first, size), out_...  8.47 us
    pallas_call x1, Pallas kernels, early_gram(): pl.pallas_call(functools.partial(early_kernel, shape, cols, tile), out_sh...  8.34 us
  transfers between devices with their start and end apart: 28, of which 15 were waited for; matrix products, arithmetic and copies ran while one was open for 1% of the time, Pallas kernels for 29%

profile of v4, /device:TPU:0, one launch (start us, length us, event | category | flops | bytes accessed | tf_op | source)
XLA Modules:
  0.0 128.1 jit_solution(8850361587834958547)
XLA Ops:
  0.0 2.8 %pick.14 = f32[64,2560]{1,0:T(8,128)} custom-call(s32[1,8]{1,0:T(1,128)} %counts_ref.17, f32[64,32768]{1,0:T(8,128)} %leg_ref.17), custom_call_target="tpu_custom_call" | custom-call | flops 1310720 | bytes 1310720 | tf_op jit(solution)/shard_map/jit(pick)/pick/pallas_call | solution.py:98
  2.8 2.5 %collective-permute-start.12 = (f32[64,2560]{1,0:T(8,128)}, f32[64,2560]{1,0:T(8,128)S(1)}, u32[]{:S(2)}, u32[]{:S(2)}) collective-permute-start(f32[64,2560]{1,0:T(8,128)} %pick.14), channel_id=1, source_target_pairs={{0,5},{1,4},{2,7},{3,6},{4,1},{5,0},{6,3},{7,2},{8,13},{9,12},{10,... | collective-permute-start | bytes 1966088 | tf_op jit(solution)/shard_map/ppermute | solution.py:489
  5.3 2.9 %pick.8 = f32[64,2560]{1,0:T(8,128)} custom-call(s32[1,8]{1,0:T(1,128)} %counts_ref.17, f32[64,32768]{1,0:T(8,128)} %leg_ref.17), custom_call_target="tpu_custom_call" | custom-call | flops 1310720 | bytes 1310720 | tf_op jit(solution)/shard_map/jit(pick)/pick/pallas_call | solution.py:98
  8.2 1.8 %collective-permute-start = (f32[64,2560]{1,0:T(8,128)}, f32[64,2560]{1,0:T(8,128)S(1)}, u32[]{:S(2)}, u32[]{:S(2)}) collective-permute-start(f32[64,2560]{1,0:T(8,128)} %pick.8), channel_id=1, source_target_pairs={{0,7},{1,6},{2,5},{3,4},{4,3},{5,2},{6,1},{7,0},{8,15},{9,14},{10,... | collective-permute-start | bytes 1966088 | tf_op jit(solution)/shard_map/ppermute | solution.py:489
  9.9 2.8 %pick.15 = f32[64,2560]{1,0:T(8,128)} custom-call(s32[1,8]{1,0:T(1,128)} %counts_ref.17, f32[64,32768]{1,0:T(8,128)} %leg_ref.17), custom_call_target="tpu_custom_call" | custom-call | flops 1310720 | bytes 1310720 | tf_op jit(solution)/shard_map/jit(pick)/pick/pallas_call | solution.py:98
  14.3 2.8 %pick.10 = f32[64,2560]{1,0:T(8,128)} custom-call(s32[1,8]{1,0:T(1,128)} %counts_ref.17, f32[64,32768]{1,0:T(8,128)} %leg_ref.17), custom_call_target="tpu_custom_call" | custom-call | flops 1310720 | bytes 1310720 | tf_op jit(solution)/shard_map/jit(pick)/pick/pallas_call | solution.py:98
  17.2 2.8 %pick.11 = f32[64,2560]{1,0:T(8,128)} custom-call(s32[1,8]{1,0:T(1,128)} %counts_ref.17, f32[64,32768]{1,0:T(8,128)} %leg_ref.17), custom_call_target="tpu_custom_call" | custom-call | flops 1310720 | bytes 1310720 | tf_op jit(solution)/shard_map/jit(pick)/pick/pallas_call | solution.py:98
  21.6 2.8 %pick.12 = f32[64,2560]{1,0:T(8,128)} custom-call(s32[1,8]{1,0:T(1,128)} %counts_ref.17, f32[64,32768]{1,0:T(8,128)} %leg_ref.17), custom_call_target="tpu_custom_call" | custom-call | flops 1310720 | bytes 1310720 | tf_op jit(solution)/shard_map/jit(pick)/pick/pallas_call | solution.py:98
  24.5 24.3 %collective-permute-done.12.refs_5_ = f32[64,2560]{1,0:T(8,128)S(1)} collective-permute-done((f32[64,2560]{1,0:T(8,128)}, f32[64,2560]{1,0:T(8,128)S(1)}, u32[]{:S(2)}, u32[]{:S(2)}) %collective-permute-start.12) | collective-permute-done | bytes 655392 | tf_op jit(solution)/shard_map/ppermute | solution.py:489
  48.8 2.1 %collective-permute-start.10 = (f32[64,2560]{1,0:T(8,128)}, f32[64,2560]{1,0:T(8,128)}, u32[]{:S(2)}, u32[]{:S(2)}) collective-permute-start(f32[64,2560]{1,0:T(8,128)} %pick.12), channel_id=1, source_target_pairs={{0,3},{1,2},{2,1},{3,0},{4,7},{5,6},{6,5},{7,4},{8,11},{9,10},{10,... | collective-permute-start | bytes 1966088 | tf_op jit(solution)/shard_map/ppermute | solution.py:489
  50.9 2.8 %pick.13 = f32[64,2560]{1,0:T(8,128)} custom-call(s32[1,8]{1,0:T(1,128)} %counts_ref.17, f32[64,32768]{1,0:T(8,128)} %leg_ref.17), custom_call_target="tpu_custom_call" | custom-call | flops 1310720 | bytes 1310720 | tf_op jit(solution)/shard_map/jit(pick)/pick/pallas_call | solution.py:98
  56.8 3.0 %pick.9.refs_0_ = f32[64,2560]{1,0:T(8,128)} custom-call(s32[1,8]{1,0:T(1,128)} %counts_ref.17, f32[64,32768]{1,0:T(8,128)} %leg_ref.17), custom_call_target="tpu_custom_call" | custom-call | flops 1310720 | bytes 1310720 | tf_op jit(solution)/shard_map/jit(pick)/pick/pallas_call | solution.py:98
  59.8 8.5 %design.1 = (f32[64,512]{1,0:T(8,128)}, f32[64,512]{1,0:T(8,128)}, f32[64,512]{1,0:T(8,128)}, f32[64,512]{1,0:T(8,128)}, f32[64,512]{1,0:T(8,128)}, /*index=5*/f...) custom-call(s32[1,8]{1,0:T(1,128)} %counts_ref.17, f32[1]{0:T(128)S(6)} %copy.6.lon_ref, ...), custom_call_target="tpu_custom_call" | custom-call | flops 2097152 | bytes 2097152 | tf_op jit(solution)/shard_map/jit(design)/design/pallas_call | solution.py:205
  72.6 2.3 %collective-permute-done.2.refs_2_ = f32[64,512]{1,0:T(8,128)S(1)} collective-permute-done((f32[64,512]{1,0:T(8,128)}, f32[64,512]{1,0:T(8,128)S(1)}, u32[]{:S(2)}, u32[]{:S(2)}) %collective-permute-start.2) | collective-permute-done | bytes 131104 | tf_op jit(solution)/shard_map/ppermute | solution.py:489
  75.0 8.3 %gram.1.refs_8_ = f32[512,512]{1,0:T(8,128)S(1)} custom-call(s32[1,8]{1,0:T(1,128)S(1)} %copy-done.1, f32[1]{0:T(128)S(6)} %copy.6.lon_ref, f32[512,2]{1,0:T(8,128)S(1)} %get-tuple-element.36.cols_ref, f32[64,2560]{1,0:T(8,128)S(1)} %copy-done, f32[64,2560]{1,0:T(8,128)S(1)} %collective-permute-done.8.refs_1_, ...), custom_call_target="tpu_custom_call" | custom-call | tf_op jit(solution)/shard_map/gram/pallas_call | solution.py:326
  87.8 2.0 %collective-permute-start.17 = (f32[160,128]{1,0:T(8,128)S(1)}, f32[160,128]{1,0:T(8,128)S(1)}, u32[]{:S(2)}, u32[]{:S(2)}) collective-permute-start(f32[160,128]{1,0:T(8,128)S(1)} %get-tuple-element.33), channel_id=1, source_target_pairs={{0,6},{1,7},{2,4},{3,5},{4,2},{5,3},{6,0},{7,1},{8,14},{9,15},{10,... | collective-permute-start | bytes 245768 | tf_op jit(solution)/shard_map/ppermute | solution.py:489
  91.4 2.2 %collective-permute-done.17 = f32[160,128]{1,0:T(8,128)S(1)} collective-permute-done((f32[160,128]{1,0:T(8,128)S(1)}, f32[160,128]{1,0:T(8,128)S(1)}, u32[]{:S(2)}, u32[]{:S(2)}) %collective-permute-start.17) | collective-permute-done | bytes 81952 | tf_op jit(solution)/shard_map/ppermute | solution.py:489
  93.6 1.7 %collective-permute-done.16 = f32[160,128]{1,0:T(8,128)S(1)} collective-permute-done((f32[160,128]{1,0:T(8,128)S(1)}, f32[160,128]{1,0:T(8,128)S(1)}, u32[]{:S(2)}, u32[]{:S(2)}) %collective-permute-start.16) | collective-permute-done | bytes 81952 | tf_op jit(solution)/shard_map/ppermute | solution.py:489
  95.3 3.6 %collective-permute-start.20 = (f32[160,128]{1,0:T(8,128)S(1)}, f32[160,128]{1,0:T(8,128)S(1)}, u32[]{:S(2)}, u32[]{:S(2)}) collective-permute-start(f32[160,128]{1,0:T(8,128)S(1)} %fusion), channel_id=1, source_target_pairs={{0,24},{8,16},{16,8},{24,0},{1,25},{9,17},{17,9},{25,1},{2,26},{10... | collective-permute-start | bytes 245768 | tf_op jit(solution)/shard_map/ppermute | solution.py:489
  99.7 2.3 %collective-permute-done.20 = f32[160,128]{1,0:T(8,128)S(1)} collective-permute-done((f32[160,128]{1,0:T(8,128)S(1)}, f32[160,128]{1,0:T(8,128)S(1)}, u32[]{:S(2)}, u32[]{:S(2)}) %collective-permute-start.20) | collective-permute-done | bytes 81952 | tf_op jit(solution)/shard_map/ppermute | solution.py:489
  102.0 4.0 %collective-permute-done.19 = f32[160,128]{1,0:T(8,128)S(1)} collective-permute-done((f32[160,128]{1,0:T(8,128)S(1)}, f32[160,128]{1,0:T(8,128)S(1)}, u32[]{:S(2)}, u32[]{:S(2)}) %collective-permute-start.19) | collective-permute-done | bytes 81952 | tf_op jit(solution)/shard_map/ppermute | solution.py:489
  106.1 1.6 %collective-permute-start.26 = (f32[160,128]{1,0:T(8,128)S(1)}, f32[160,128]{1,0:T(8,128)S(1)}, u32[]{:S(2)}, u32[]{:S(2)}) collective-permute-start(f32[160,128]{1,0:T(8,128)S(1)} %add_add_fusion.refs_0_), channel_id=1, source_target_pairs={{0,6},{1,7},{2,4},{3,5},{4,2},{5,3},{6,0},{7,1},{8,14},{9,15},{10,... | collective-permute-start | bytes 245768 | tf_op jit(solution)/shard_map/ppermute | solution.py:489
  109.6 2.8 %collective-permute-done.26.refs_6_ = f32[160,128]{1,0:T(8,128)S(1)} collective-permute-done((f32[160,128]{1,0:T(8,128)S(1)}, f32[160,128]{1,0:T(8,128)S(1)}, u32[]{:S(2)}, u32[]{:S(2)}) %collective-permute-start.26) | collective-permute-done | bytes 81952 | tf_op jit(solution)/shard_map/ppermute | solution.py:489
  114.3 13.8 %factor.1 = f32[512,512]{1,0:T(8,128)} custom-call(f32[1,512]{1,0:T(1,128)S(1)} %multiply_multiply_fusion.kaula_ref, f32[160,128]{1,0:T(8,128)S(1)} %add_add_fusion.refs_0_, f32[160,128]{1,0:T(8,128)S(1)} %collective-permute-done.21.refs_1_, f32[160,128]{1,0:T(8,128)S(1)} %collective-permute-done.22.refs_2_, f32[160,128]{1,0:T(8,128)S(1)} %collective-permute-done.23.refs_3_, ...), custom_call_target="tpu_custom_call" | custom-call | tf_op jit(solution)/shard_map/factor/pallas_call | solution.py:468
  (61 shorter events, 20.6 us)
Async XLA Ops:
  2.8 46.0 %collective-permute-start.12 = (f32[64,2560]{1,0:T(8,128)}, f32[64,2560]{1,0:T(8,128)S(1)}, u32[]{:S(2)}, u32[]{:S(2)}) collective-permute-start(f32[64,2560]{1,0:T(8,128)} %pick.14), channel_id=1, source_target_pairs={{0,5},{1,4},{2,7},{3,6},{4,1},{5,0},{6,3},{7,2},{8,13},{9,12},{10,... | collective-permute-start | bytes 1966088 | tf_op jit(solution)/shard_map/ppermute | solution.py:489
  8.2 45.6 %collective-permute-start = (f32[64,2560]{1,0:T(8,128)}, f32[64,2560]{1,0:T(8,128)S(1)}, u32[]{:S(2)}, u32[]{:S(2)}) collective-permute-start(f32[64,2560]{1,0:T(8,128)} %pick.8), channel_id=1, source_target_pairs={{0,7},{1,6},{2,5},{3,4},{4,3},{5,2},{6,1},{7,0},{8,15},{9,14},{10,... | collective-permute-start | bytes 1966088 | tf_op jit(solution)/shard_map/ppermute | solution.py:489
  12.8 55.5 %collective-permute-start.13 = (f32[64,2560]{1,0:T(8,128)}, f32[64,2560]{1,0:T(8,128)S(1)}, u32[]{:S(2)}, u32[]{:S(2)}) collective-permute-start(f32[64,2560]{1,0:T(8,128)} %pick.15), channel_id=1, source_target_pairs={{0,6},{1,7},{2,4},{3,5},{4,2},{5,3},{6,0},{7,1},{8,14},{9,15},{10,... | collective-permute-start | bytes 1966088 | tf_op jit(solution)/shard_map/ppermute | solution.py:489
  17.1 51.3 %collective-permute-start.8 = (f32[64,2560]{1,0:T(8,128)}, f32[64,2560]{1,0:T(8,128)S(1)}, u32[]{:S(2)}, u32[]{:S(2)}) collective-permute-start(f32[64,2560]{1,0:T(8,128)} %pick.10), channel_id=1, source_target_pairs={{0,1},{1,0},{2,3},{3,2},{4,5},{5,4},{6,7},{7,6},{8,9},{9,8},{10,11... | collective-permute-start | bytes 1966088 | tf_op jit(solution)/shard_map/ppermute | solution.py:489
  20.1 48.9 %collective-permute-start.9 = (f32[64,2560]{1,0:T(8,128)}, f32[64,2560]{1,0:T(8,128)S(1)}, u32[]{:S(2)}, u32[]{:S(2)}) collective-permute-start(f32[64,2560]{1,0:T(8,128)} %pick.11), channel_id=1, source_target_pairs={{0,2},{1,3},{2,0},{3,1},{4,6},{5,7},{6,4},{7,5},{8,10},{9,11},{10,... | collective-permute-start | bytes 1966088 | tf_op jit(solution)/shard_map/ppermute | solution.py:489
  48.8 21.4 %collective-permute-start.10 = (f32[64,2560]{1,0:T(8,128)}, f32[64,2560]{1,0:T(8,128)}, u32[]{:S(2)}, u32[]{:S(2)}) collective-permute-start(f32[64,2560]{1,0:T(8,128)} %pick.12), channel_id=1, source_target_pairs={{0,3},{1,2},{2,1},{3,0},{4,7},{5,6},{6,5},{7,4},{8,11},{9,10},{10,... | collective-permute-start | bytes 1966088 | tf_op jit(solution)/shard_map/ppermute | solution.py:489
  53.7 17.3 %collective-permute-start.11 = (f32[64,2560]{1,0:T(8,128)}, f32[64,2560]{1,0:T(8,128)}, u32[]{:S(2)}, u32[]{:S(2)}) collective-permute-start(f32[64,2560]{1,0:T(8,128)} %pick.13), channel_id=1, source_target_pairs={{0,4},{1,5},{2,6},{3,7},{4,0},{5,1},{6,2},{7,3},{8,12},{9,13},{10,... | collective-permute-start | bytes 1966088 | tf_op jit(solution)/shard_map/ppermute | solution.py:489
  68.3 3.7 %collective-permute-start.1 = (f32[64,512]{1,0:T(8,128)}, f32[64,512]{1,0:T(8,128)S(1)}, u32[]{:S(2)}, u32[]{:S(2)}) collective-permute-start(f32[64,512]{1,0:T(8,128)} %get-tuple-element.22), channel_id=1, source_target_pairs={{0,1},{1,0},{2,3},{3,2},{4,5},{5,4},{6,7},{7,6},{8,9},{9,8},{10,11... | collective-permute-start | bytes 393224 | tf_op jit(solution)/shard_map/ppermute | solution.py:489
  68.4 6.5 %collective-permute-start.2 = (f32[64,512]{1,0:T(8,128)}, f32[64,512]{1,0:T(8,128)S(1)}, u32[]{:S(2)}, u32[]{:S(2)}) collective-permute-start(f32[64,512]{1,0:T(8,128)} %get-tuple-element.23), channel_id=1, source_target_pairs={{0,2},{1,3},{2,0},{3,1},{4,6},{5,7},{6,4},{7,5},{8,10},{9,11},{10,... | collective-permute-start | bytes 393224 | tf_op jit(solution)/shard_map/ppermute | solution.py:489
  69.0 14.4 %collective-permute-start.3 = (f32[64,512]{1,0:T(8,128)}, f32[64,512]{1,0:T(8,128)S(1)}, u32[]{:S(2)}, u32[]{:S(2)}) collective-permute-start(f32[64,512]{1,0:T(8,128)} %get-tuple-element.24), channel_id=1, source_target_pairs={{0,3},{1,2},{2,1},{3,0},{4,7},{5,6},{6,5},{7,4},{8,11},{9,10},{10,... | collective-permute-start | bytes 393224 | tf_op jit(solution)/shard_map/ppermute | solution.py:489
  70.2 13.1 %collective-permute-start.4 = (f32[64,512]{1,0:T(8,128)}, f32[64,512]{1,0:T(8,128)S(1)}, u32[]{:S(2)}, u32[]{:S(2)}) collective-permute-start(f32[64,512]{1,0:T(8,128)} %get-tuple-element.25), channel_id=1, source_target_pairs={{0,4},{1,5},{2,6},{3,7},{4,0},{5,1},{6,2},{7,3},{8,12},{9,13},{10,... | collective-permute-start | bytes 393224 | tf_op jit(solution)/shard_map/ppermute | solution.py:489
  71.1 13.0 %collective-permute-start.5 = (f32[64,512]{1,0:T(8,128)}, f32[64,512]{1,0:T(8,128)S(1)}, u32[]{:S(2)}, u32[]{:S(2)}) collective-permute-start(f32[64,512]{1,0:T(8,128)} %get-tuple-element.26), channel_id=1, source_target_pairs={{0,5},{1,4},{2,7},{3,6},{4,1},{5,0},{6,3},{7,2},{8,13},{9,12},{10,... | collective-permute-start | bytes 393224 | tf_op jit(solution)/shard_map/ppermute | solution.py:489
  71.9 12.1 %collective-permute-start.6 = (f32[64,512]{1,0:T(8,128)}, f32[64,512]{1,0:T(8,128)S(1)}, u32[]{:S(2)}, u32[]{:S(2)}) collective-permute-start(f32[64,512]{1,0:T(8,128)} %get-tuple-element.27), channel_id=1, source_target_pairs={{0,6},{1,7},{2,4},{3,5},{4,2},{5,3},{6,0},{7,1},{8,14},{9,15},{10,... | collective-permute-start | bytes 393224 | tf_op jit(solution)/shard_map/ppermute | solution.py:489
  75.0 9.1 %collective-permute-start.7 = (f32[64,512]{1,0:T(8,128)}, f32[64,512]{1,0:T(8,128)S(1)}, u32[]{:S(2)}, u32[]{:S(2)}) collective-permute-start(f32[64,512]{1,0:T(8,128)} %get-tuple-element.28), channel_id=1, source_target_pairs={{0,7},{1,6},{2,5},{3,4},{4,3},{5,2},{6,1},{7,0},{8,15},{9,14},{10,... | collective-permute-start | bytes 393224 | tf_op jit(solution)/shard_map/ppermute | solution.py:489
  87.8 5.8 %collective-permute-start.17 = (f32[160,128]{1,0:T(8,128)S(1)}, f32[160,128]{1,0:T(8,128)S(1)}, u32[]{:S(2)}, u32[]{:S(2)}) collective-permute-start(f32[160,128]{1,0:T(8,128)S(1)} %get-tuple-element.33), channel_id=1, source_target_pairs={{0,6},{1,7},{2,4},{3,5},{4,2},{5,3},{6,0},{7,1},{8,14},{9,15},{10,... | collective-permute-start | bytes 245768 | tf_op jit(solution)/shard_map/ppermute | solution.py:489
  89.8 5.4 %collective-permute-start.16 = (f32[160,128]{1,0:T(8,128)S(1)}, f32[160,128]{1,0:T(8,128)S(1)}, u32[]{:S(2)}, u32[]{:S(2)}) collective-permute-start(f32[160,128]{1,0:T(8,128)S(1)} %get-tuple-element.34), channel_id=1, source_target_pairs={{0,4},{1,5},{2,6},{3,7},{4,0},{5,1},{6,2},{7,3},{8,12},{9,13},{10,... | collective-permute-start | bytes 245768 | tf_op jit(solution)/shard_map/ppermute | solution.py:489
  90.3 4.9 %collective-permute-start.15 = (f32[160,128]{1,0:T(8,128)S(1)}, f32[160,128]{1,0:T(8,128)S(1)}, u32[]{:S(2)}, u32[]{:S(2)}) collective-permute-start(f32[160,128]{1,0:T(8,128)S(1)} %get-tuple-element.35), channel_id=1, source_target_pairs={{0,2},{1,3},{2,0},{3,1},{4,6},{5,7},{6,4},{7,5},{8,10},{9,11},{10,... | collective-permute-start | bytes 245768 | tf_op jit(solution)/shard_map/ppermute | solution.py:489
  95.3 6.8 %collective-permute-start.20 = (f32[160,128]{1,0:T(8,128)S(1)}, f32[160,128]{1,0:T(8,128)S(1)}, u32[]{:S(2)}, u32[]{:S(2)}) collective-permute-start(f32[160,128]{1,0:T(8,128)S(1)} %fusion), channel_id=1, source_target_pairs={{0,24},{8,16},{16,8},{24,0},{1,25},{9,17},{17,9},{25,1},{2,26},{10... | collective-permute-start | bytes 245768 | tf_op jit(solution)/shard_map/ppermute | solution.py:489
  98.9 7.2 %collective-permute-start.19 = (f32[160,128]{1,0:T(8,128)S(1)}, f32[160,128]{1,0:T(8,128)S(1)}, u32[]{:S(2)}, u32[]{:S(2)}) collective-permute-start(f32[160,128]{1,0:T(8,128)S(1)} %fusion), channel_id=1, source_target_pairs={{0,16},{8,24},{16,0},{24,8},{1,17},{9,25},{17,1},{25,9},{2,18},{10... | collective-permute-start | bytes 245768 | tf_op jit(solution)/shard_map/ppermute | solution.py:489
  98.9 7.2 %collective-permute-start.18 = (f32[160,128]{1,0:T(8,128)S(1)}, f32[160,128]{1,0:T(8,128)S(1)}, u32[]{:S(2)}, u32[]{:S(2)}) collective-permute-start(f32[160,128]{1,0:T(8,128)S(1)} %fusion), channel_id=1, source_target_pairs={{0,8},{8,0},{16,24},{24,16},{1,9},{9,1},{17,25},{25,17},{2,10},{10... | collective-permute-start | bytes 245768 | tf_op jit(solution)/shard_map/ppermute | solution.py:489
  106.1 6.4 %collective-permute-start.26 = (f32[160,128]{1,0:T(8,128)S(1)}, f32[160,128]{1,0:T(8,128)S(1)}, u32[]{:S(2)}, u32[]{:S(2)}) collective-permute-start(f32[160,128]{1,0:T(8,128)S(1)} %add_add_fusion.refs_0_), channel_id=1, source_target_pairs={{0,6},{1,7},{2,4},{3,5},{4,2},{5,3},{6,0},{7,1},{8,14},{9,15},{10,... | collective-permute-start | bytes 245768 | tf_op jit(solution)/shard_map/ppermute | solution.py:489
  107.7 5.0 %collective-permute-start.24 = (f32[160,128]{1,0:T(8,128)S(1)}, f32[160,128]{1,0:T(8,128)S(1)}, u32[]{:S(2)}, u32[]{:S(2)}) collective-permute-start(f32[160,128]{1,0:T(8,128)S(1)} %add_add_fusion.refs_0_), channel_id=1, source_target_pairs={{0,4},{1,5},{2,6},{3,7},{4,0},{5,1},{6,2},{7,3},{8,12},{9,13},{10,... | collective-permute-start | bytes 245768 | tf_op jit(solution)/shard_map/ppermute | solution.py:489
  108.6 4.4 %collective-permute-start.22 = (f32[160,128]{1,0:T(8,128)S(1)}, f32[160,128]{1,0:T(8,128)S(1)}, u32[]{:S(2)}, u32[]{:S(2)}) collective-permute-start(f32[160,128]{1,0:T(8,128)S(1)} %add_add_fusion.refs_0_), channel_id=1, source_target_pairs={{0,2},{1,3},{2,0},{3,1},{4,6},{5,7},{6,4},{7,5},{8,10},{9,11},{10,... | collective-permute-start | bytes 245768 | tf_op jit(solution)/shard_map/ppermute | solution.py:489
  109.6 3.6 %collective-permute-start.21 = (f32[160,128]{1,0:T(8,128)S(1)}, f32[160,128]{1,0:T(8,128)S(1)}, u32[]{:S(2)}, u32[]{:S(2)}) collective-permute-start(f32[160,128]{1,0:T(8,128)S(1)} %add_add_fusion.refs_0_), channel_id=1, source_target_pairs={{0,1},{1,0},{2,3},{3,2},{4,5},{5,4},{6,7},{7,6},{8,9},{9,8},{10,11... | collective-permute-start | bytes 245768 | tf_op jit(solution)/shard_map/ppermute | solution.py:489
  (8 other events, 75.8 us)
